TPU v7x, 32 devices: a whole 2x2x4 slice. The times are simulated.
32 devices in a mesh: sub: 8 (over z, y), crs: 4 (over x, core).
Axes of the slice: x: 2, y: 2, z: 4, core: 2. Of those that a mesh axis runs over, the one named last changes fastest.
Arguments:
- jump_data: float32 [8, 4, 6, 384], P('sub', 'crs'), may hold values from -6 to 6
- lumped_scale: float32 [8, 4, 384], P('sub', 'crs'), may hold values from 0.3 to 3
- schur_inverse: float32 [8, 4, 768, 768], P('sub', 'crs'), as said below
- coarse_coupling: float32 [8, 4, 24, 768], P('sub', 'crs'), may hold values from -0.4375 to 0.4375
- corner_inverse: float32 [1024, 1024], P(None, 'crs'), as said below
- own_dof: int32 [8, 4, 384], P('sub', 'crs'), may hold values from 0 to 767, as said below
- nbr_dof: int32 [8, 4, 384], P('sub', 'crs'), may hold values from 0 to 767, as said below
- live_count: int32 [8, 4], P('sub', 'crs'), may hold values from 1 to 384, as said below
- corner_index: int32 [8, 4, 24], P('sub', 'crs'), may hold values from 0 to 1023
Outputs:
- multipliers: float32 [8, 4, 6, 384], P('sub', 'crs')
- residual: float32 [8, 4, 6, 384], P('sub', 'crs')
Inputs may be any that keep to these rules, and one draw needn't show every extreme that they name: `own_dof`: the 384 entries of one subdomain are distinct. `nbr_dof`: the 384 entries of one subdomain are distinct. `live_count`: some subdomain has all 384 slots live. `schur_inverse`: symmetric positive definite. `corner_inverse`: symmetric positive definite.
All inputs are finite; a program needn't handle non-finite values.
Results may differ from a plain program's by a relative error of at most 0.00021.
Values sent between devices are 32-bit elements; how exact they have to be, the bound alone decides.
No kernel may reach another device: no remote copies, remote signals or barrier semaphores. Data moves between devices by JAX's collectives and lax.ppermute only.
A program may use at most 64 MiB of HBM per device.

v0:
```python
import jax
import jax.numpy as jnp
from jax import lax
from jax.sharding import PartitionSpec as P

ITERS = 2


def passed_along(value, axis, steps):
    count = lax.axis_size(axis)
    pairs = [(source, (source + steps) % count) for source in range(count)]
    return lax.ppermute(value, axis, pairs)


def product(left, right):
    return jnp.dot(left, right, precision=lax.Precision.HIGHEST, preferred_element_type=jnp.float32)


def paired_inner(residual, precon, image):
    return lax.psum(
        (jnp.sum(residual * precon, axis=1), jnp.sum(precon * image, axis=1)), ("sub", "crs")
    )


def per_device(
    jump_data,
    lumped_scale,
    schur_inverse,
    coarse_coupling,
    corner_inverse,
    own_dof,
    nbr_dof,
    live_count,
    corner_index,
):
    given = jump_data[0, 0]
    scale = lumped_scale[0, 0][None, :]
    schur = schur_inverse[0, 0]
    coupling = coarse_coupling[0, 0]
    records = given.shape[1]
    iface = schur.shape[0]
    corners = corner_inverse.shape[0]
    live = (jnp.arange(records, dtype=jnp.int32) < live_count[0, 0]).astype(jnp.float32)
    columns = jnp.arange(iface, dtype=jnp.int32)[None, :]
    own_map = (own_dof[0, 0][:, None] == columns).astype(jnp.float32) * live[:, None]
    next_map = (nbr_dof[0, 0][:, None] == columns).astype(jnp.float32) * live[:, None]
    corner_map = (
        corner_index[0, 0][:, None] == jnp.arange(corners, dtype=jnp.int32)[None, :]
    ).astype(jnp.float32)

    def operate(field):
        own_load = product(field, own_map)
        next_load = product(field, next_map)
        from_left = passed_along(next_load, "sub", 1)
        load = own_load - from_left
        local_part = product(load, schur)
        corner_force = product(load, coupling.T)
        spread = product(corner_force, corner_map)
        chain_rows = lax.psum_scatter(spread, "crs", scatter_dimension=1, tiled=True)
        corner_total = lax.psum(chain_rows, "sub")
        partial_solution = product(corner_total, corner_inverse.T)
        corner_solution = lax.psum(partial_solution, "crs")
        picked = product(corner_solution, corner_map.T)
        displacement = local_part + product(picked, coupling)
        from_right = passed_along(displacement, "sub", -1)
        return product(displacement, own_map.T) - product(from_right, next_map.T)

    residual = given * live[None, :]
    multipliers = jnp.zeros_like(residual)
    precon = scale * residual
    image = operate(precon)
    norm_now, curvature = paired_inner(residual, precon, image)
    alpha = norm_now / curvature
    direction, along = (precon, image)
    for step in range(ITERS):
        multipliers = multipliers + alpha[:, None] * direction
        residual = residual - alpha[:, None] * along
        if step + 1 < ITERS:
            precon = scale * residual
            image = operate(precon)
            norm_next, curvature = paired_inner(residual, precon, image)
            ratio = norm_next / norm_now
            alpha = norm_next / (curvature - ratio * norm_next / alpha)
            direction = precon + ratio[:, None] * direction
            along = image + ratio[:, None] * along
            norm_now = norm_next
    return (multipliers[None, None], residual[None, None])


def solution(mesh):
    return jax.shard_map(
        per_device,
        mesh=mesh,
        in_specs=(
            P("sub", "crs", None, None),
            P("sub", "crs", None),
            P("sub", "crs", None, None),
            P("sub", "crs", None, None),
            P(None, "crs"),
            P("sub", "crs", None),
            P("sub", "crs", None),
            P("sub", "crs"),
            P("sub", "crs", None),
        ),
        out_specs=(P("sub", "crs", None, None), P("sub", "crs", None, None)),
        check_vma=False,
    )
```

profile of v0, /device:TPU:0, one launch (start us, length us, event | category | flops | bytes accessed | tf_op | source)
XLA Modules:
  0.0 232.9 jit_solution(4371522302135669060)
XLA Ops:
  7.2 0.0 copy-start
  7.2 0.0 reduce-scatter.3.cloned.1.call-start
  8.1 0.8 reduce
  8.8 0.7 reduce.2
  9.5 1.5 fusion.10
  11.1 3.0 %collective-permute-start = (f32[6,768]{1,0:T(8,128)S(1)}, f32[6,768]{1,0:T(8,128)S(1)}, u32[]{:S(2)}, u32[]{:S(2)}) collective-permute-start(f32[6,768]{1,0:T(8,128)S(1)} %fusion.10), channel_id=1, source_target_pairs={{0,4},{4,8},{8,12},{12,16},{16,20},{20,24},{24,28},{28,0},{1,5},{5... | collective-permute-start | bytes 55304 | tf_op jit(solution)/shard_map/ppermute | solution.py:12
  14.1 0.7 reduce.1
  14.8 4.1 %collective-permute-done = f32[6,768]{1,0:T(8,128)S(1)} collective-permute-done((f32[6,768]{1,0:T(8,128)S(1)}, f32[6,768]{1,0:T(8,128)S(1)}, u32[]{:S(2)}, u32[]{:S(2)}) %collective-permute-start) | collective-permute-done | bytes 18464 | tf_op jit(solution)/shard_map/ppermute | solution.py:12
  18.9 1.5 fusion.20
  20.4 0.2 fusion.72
  20.6 0.8 fusion.65
  21.4 0.0 reduce-scatter.3.cloned.1.call-update
  21.5 0.0 reduce-scatter.5.cloned.1.call-start
  21.5 18.2 %reduce-scatter.3.cloned.1.call-done = f32[6,256]{1,0:T(8,128)} async-done(((f32[6,1024]{1,0:T(8,128)}), f32[6,256]{1,0:T(8,128)}) %reduce-scatter.3.cloned.1.call-update) | async-done | bytes 6160 | tf_op jit(solution)/shard_map/reduce_scatter | solution.py:59
  39.7 21.7 %psum.57 = f32[6,256]{1,0:T(8,128)S(1)} all-reduce(f32[6,256]{1,0:T(8,128)} %reduce-scatter.3.cloned.1.call-done), channel_id=1, replica_groups=mesh['sub'=8,'crs'=4] {'sub'}, use_global_device_ids=true, to_apply=%region_3.0 | all-reduce | flops 1536 | bytes 12288 | tf_op jit(solution)/shard_map/psum | solution.py:60
  61.4 1.0 fusion.105
  62.4 11.0 %psum.58 = f32[6,1024]{1,0:T(8,128)} all-reduce(f32[6,1024]{1,0:T(8,128)S(1)} %fusion.105), channel_id=1, replica_groups=mesh['sub'=8,'crs'=4] {'crs'}, use_global_device_ids=true, to_apply=%region_4.0 | all-reduce | flops 6144 | bytes 49152 | tf_op jit(solution)/shard_map/psum | solution.py:62
  73.4 1.0 fusion.64
  74.3 0.2 fusion.70
  74.6 1.2 fusion.26
  75.8 0.0 collective-permute-start.1
  75.8 1.2 fusion.16
  77.0 2.6 %collective-permute-done.1 = f32[6,768]{1,0:T(8,128)S(1)} collective-permute-done((f32[6,768]{1,0:T(8,128)S(1)}, f32[6,768]{1,0:T(8,128)S(1)}, u32[]{:S(2)}, u32[]{:S(2)}) %collective-permute-start.1) | collective-permute-done | bytes 18464 | tf_op jit(solution)/shard_map/ppermute | solution.py:12
  79.6 1.3 fusion.83
  80.9 37.1 %all-reduce.1 = (f32[6]{0:T(128)S(1)}, f32[6]{0:T(128)S(1)}) all-reduce(f32[6]{0:T(128)S(1)} %get-tuple-element.7, f32[6]{0:T(128)S(1)} %get-tuple-element.6), channel_id=1, replica_groups=mesh['sub'=8,'crs'=4] {'sub','crs'}, use_global_device_ids=true, to_apply=%region_1.0 | all-reduce | flops 12 | bytes 96 | tf_op jit(solution)/shard_map/psum | solution.py:20
  118.1 0.1 fusion.89
  118.1 0.8 fusion.6
  119.0 2.3 collective-permute-start.2
  121.3 4.2 %collective-permute-done.2 = f32[6,768]{1,0:T(8,128)S(1)} collective-permute-done((f32[6,768]{1,0:T(8,128)S(1)}, f32[6,768]{1,0:T(8,128)S(1)}, u32[]{:S(2)}, u32[]{:S(2)}) %collective-permute-start.2) | collective-permute-done | bytes 18464 | tf_op jit(solution)/shard_map/ppermute | solution.py:12
  125.5 0.8 fusion.23
  126.3 0.2 fusion.68
  126.5 0.8 fusion.63
  127.4 0.0 reduce-scatter.5.cloned.1.call-update
  127.4 18.2 %reduce-scatter.5.cloned.1.call-done = f32[6,256]{1,0:T(8,128)} async-done(((f32[6,1024]{1,0:T(8,128)}), f32[6,256]{1,0:T(8,128)}) %reduce-scatter.5.cloned.1.call-update) | async-done | bytes 6160 | tf_op jit(solution)/shard_map/reduce_scatter | solution.py:59
  145.6 22.3 %psum.61 = f32[6,256]{1,0:T(8,128)} all-reduce(f32[6,256]{1,0:T(8,128)} %reduce-scatter.5.cloned.1.call-done), channel_id=1, replica_groups=mesh['sub'=8,'crs'=4] {'sub'}, use_global_device_ids=true, to_apply=%region_10.0 | all-reduce | flops 1536 | bytes 12288 | tf_op jit(solution)/shard_map/psum | solution.py:60
  167.8 1.7 fusion.106
  169.5 10.4 %psum.62 = f32[6,1024]{1,0:T(8,128)S(1)} all-reduce(f32[6,1024]{1,0:T(8,128)S(1)} %fusion.106), channel_id=1, replica_groups=mesh['sub'=8,'crs'=4] {'crs'}, use_global_device_ids=true, to_apply=%region_11.0 | all-reduce | flops 6144 | bytes 49152 | tf_op jit(solution)/shard_map/psum | solution.py:62
  179.9 0.8 fusion.62
  180.8 0.2 fusion.66
  181.0 1.2 fusion.29
  182.3 0.2 collective-permute-start.3
  182.5 1.2 fusion.12
  183.7 2.6 %collective-permute-done.3 = f32[6,768]{1,0:T(8,128)S(1)} collective-permute-done((f32[6,768]{1,0:T(8,128)S(1)}, f32[6,768]{1,0:T(8,128)S(1)}, u32[]{:S(2)}, u32[]{:S(2)}) %collective-permute-start.3) | collective-permute-done | bytes 18464 | tf_op jit(solution)/shard_map/ppermute | solution.py:12
  186.3 1.3 fusion.87
  187.6 37.1 %all-reduce = (f32[6]{0:T(128)S(1)}, f32[6]{0:T(128)S(1)}) all-reduce(f32[6]{0:T(128)S(1)} %get-tuple-element.5, f32[6]{0:T(128)S(1)} %get-tuple-element.4), channel_id=1, replica_groups=mesh['sub'=8,'crs'=4] {'sub','crs'}, use_global_device_ids=true, to_apply=%region_8.0 | all-reduce | flops 12 | bytes 96 | tf_op jit(solution)/shard_map/psum | solution.py:20
  224.8 0.1 subtract_bitcast_fusion
  224.8 0.6 copy.11
  225.5 0.6 copy.12
  (52 shorter events, 0.1 us)
Async XLA Ops:
  7.2 67.4 %copy-start = (f32[1,1,768,768]{3,2,1,0:T(8,128)S(1)}, f32[1,1,768,768]{3,2,1,0:T(8,128)}, u32[]{:S(2)}) copy-start(f32[1,1,768,768]{3,2,1,0:T(8,128)} %param.11) | copy-start | bytes 7077892
  7.2 13.2 %copy-start.2 = (f32[1,1,24,768]{3,2,1,0:T(8,128)S(1)}, f32[1,1,24,768]{3,2,1,0:T(8,128)}, u32[]{:S(2)}) copy-start(f32[1,1,24,768]{3,2,1,0:T(8,128)} %param.12) | copy-start | bytes 221188
  7.2 13.4 %copy-start.23 = (s32[1,1,24]{2,1,0:T(1,128)S(1)}, s32[1,1,24]{2,1,0:T(1,128)}, u32[]{:S(2)}) copy-start(s32[1,1,24]{2,1,0:T(1,128)} %param.17) | copy-start | bytes 292
  7.2 54.2 %copy-start.1 = (f32[1024,256]{1,0:T(8,128)S(1)}, f32[1024,256]{1,0:T(8,128)}, u32[]{:S(2)}) copy-start(f32[1024,256]{1,0:T(8,128)} %param.13) | copy-start | bytes 3145732
  7.2 32.5 %reduce-scatter.3.cloned.1.call-start = ((), (), s32[]{:S(2)}) async-start(), calls=%async_computation.2 | async-start | bytes 40960 | tf_op jit(solution)/shard_map/reduce_scatter | solution.py:59
  8.8 12.7 %copy-start.8 = (f32[384]{0:T(512)}, f32[384]{0:T(512)S(1)}, u32[]{:S(2)}) copy-start(f32[384]{0:T(512)S(1)} %reduce) | copy-start | bytes 4612
  9.5 9.4 %copy-start.13 = (s32[384]{0:T(512)}, s32[384]{0:T(512)S(1)}, u32[]{:S(2)}) copy-start(s32[384]{0:T(512)S(1)} %reduce.2) | copy-start | bytes 4612
  11.1 7.8 %collective-permute-start = (f32[6,768]{1,0:T(8,128)S(1)}, f32[6,768]{1,0:T(8,128)S(1)}, u32[]{:S(2)}, u32[]{:S(2)}) collective-permute-start(f32[6,768]{1,0:T(8,128)S(1)} %fusion.10), channel_id=1, source_target_pairs={{0,4},{4,8},{8,12},{12,16},{16,20},{20,24},{24,28},{28,0},{1,5},{5... | collective-permute-start | bytes 55304 | tf_op jit(solution)/shard_map/ppermute | solution.py:12
  14.8 61.1 %copy-start.16 = (s32[384]{0:T(512)}, s32[384]{0:T(512)S(1)}, u32[]{:S(2)}) copy-start(s32[384]{0:T(512)S(1)} %reduce.1) | copy-start | bytes 4612
  21.5 124.1 %reduce-scatter.5.cloned.1.call-start = ((), (), s32[]{:S(2)}) async-start(), calls=%async_computation.3 | async-start | bytes 40960 | tf_op jit(solution)/shard_map/reduce_scatter | solution.py:59
  74.5 5.1 %copy-start.5 = (f32[1,1,6,384]{3,1,2,0:T(1,128)S(1)}, f32[1,1,6,384]{3,1,2,0:T(1,128)}, u32[]{:S(2)}) copy-start(f32[1,1,6,384]{3,1,2,0:T(1,128)} %param.9) | copy-start | bytes 27652
  74.6 5.1 %copy-start.9 = (f32[384]{0:T(512)S(1)}, f32[384]{0:T(512)}, u32[]{:S(2)}) copy-start(f32[384]{0:T(512)} %copy-done.8) | copy-start | bytes 4612
  74.6 5.1 %copy-start.14 = (s32[384]{0:T(512)S(1)}, s32[384]{0:T(512)}, u32[]{:S(2)}) copy-start(s32[384]{0:T(512)} %copy-done.13) | copy-start | bytes 4612
  75.8 42.3 %copy-start.6 = (f32[1,1,6,384]{3,1,2,0:T(1,128)S(1)}, f32[1,1,6,384]{3,1,2,0:T(1,128)}, u32[]{:S(2)}) copy-start(f32[1,1,6,384]{3,1,2,0:T(1,128)} %param.9) | copy-start | bytes 27652
  75.8 3.8 %collective-permute-start.1 = (f32[6,768]{1,0:T(8,128)S(1)}, f32[6,768]{1,0:T(8,128)S(1)}, u32[]{:S(2)}, u32[]{:S(2)}) collective-permute-start(f32[6,768]{1,0:T(8,128)S(1)} %fusion.26), channel_id=1, source_target_pairs={{0,28},{4,0},{8,4},{12,8},{16,12},{20,16},{24,20},{28,24},{1,29},{... | collective-permute-start | bytes 55304 | tf_op jit(solution)/shard_map/ppermute | solution.py:12
  77.0 48.5 %copy-start.17 = (s32[384]{0:T(512)S(1)}, s32[384]{0:T(512)}, u32[]{:S(2)}) copy-start(s32[384]{0:T(512)} %copy-done.16) | copy-start | bytes 4612
  80.9 45.6 %copy-start.24 = (s32[1,1,24]{2,1,0:T(1,128)S(1)}, s32[1,1,24]{2,1,0:T(1,128)}, u32[]{:S(2)}) copy-start(s32[1,1,24]{2,1,0:T(1,128)} %param.17) | copy-start | bytes 292
  118.0 3.2 %copy-start.19 = (f32[6]{0:T(128)}, f32[6]{0:T(128)S(1)}, u32[]{:S(2)}) copy-start(f32[6]{0:T(128)S(1)} %get-tuple-element.10) | copy-start | bytes 76
  118.0 3.2 %copy-start.21 = (f32[6]{0:T(128)}, f32[6]{0:T(128)S(1)}, u32[]{:S(2)}) copy-start(f32[6]{0:T(128)S(1)} %get-tuple-element.11) | copy-start | bytes 76
  118.0 3.2 %copy-start.11 = (f32[6]{0:T(128)}, f32[6]{0:T(128)S(1)}, u32[]{:S(2)}) copy-start(f32[6]{0:T(128)S(1)} %div.12) | copy-start | bytes 76
  118.1 27.4 %copy-start.3 = (f32[6,384]{1,0:T(8,128)}, f32[6,384]{1,0:T(8,128)S(1)}, u32[]{:S(2)}) copy-start(f32[6,384]{1,0:T(8,128)S(1)} %fusion.89) | copy-start | bytes 27652
  119.0 6.5 %collective-permute-start.2 = (f32[6,768]{1,0:T(8,128)S(1)}, f32[6,768]{1,0:T(8,128)S(1)}, u32[]{:S(2)}, u32[]{:S(2)}) collective-permute-start(f32[6,768]{1,0:T(8,128)S(1)} %fusion.6), channel_id=1, source_target_pairs={{0,4},{4,8},{8,12},{12,16},{16,20},{20,24},{24,28},{28,0},{1,5},{5... | collective-permute-start | bytes 55304 | tf_op jit(solution)/shard_map/ppermute | solution.py:12
  181.0 1.5 copy-start.18
  181.0 5.3 %copy-start.4 = (f32[6,384]{1,0:T(8,128)S(1)}, f32[6,384]{1,0:T(8,128)}, u32[]{:S(2)}) copy-start(f32[6,384]{1,0:T(8,128)} %copy-done.3) | copy-start | bytes 27652
  181.0 5.3 %copy-start.10 = (f32[384]{0:T(512)S(1)}, f32[384]{0:T(512)}, u32[]{:S(2)}) copy-start(f32[384]{0:T(512)} %copy-done.8) | copy-start | bytes 4612
  181.0 5.3 %copy-start.15 = (s32[384]{0:T(512)S(1)}, s32[384]{0:T(512)}, u32[]{:S(2)}) copy-start(s32[384]{0:T(512)} %copy-done.13) | copy-start | bytes 4612
  182.2 42.5 %copy-start.20 = (f32[6]{0:T(128)S(1)}, f32[6]{0:T(128)}, u32[]{:S(2)}) copy-start(f32[6]{0:T(128)} %copy-done.19) | copy-start | bytes 76
  182.2 42.5 %copy-start.22 = (f32[6]{0:T(128)S(1)}, f32[6]{0:T(128)}, u32[]{:S(2)}) copy-start(f32[6]{0:T(128)} %copy-done.21) | copy-start | bytes 76
  182.2 42.5 %copy-start.7 = (f32[1,1,6,384]{3,1,2,0:T(1,128)S(1)}, f32[1,1,6,384]{3,1,2,0:T(1,128)}, u32[]{:S(2)}) copy-start(f32[1,1,6,384]{3,1,2,0:T(1,128)} %param.9) | copy-start | bytes 27652
  182.3 42.5 %copy-start.12 = (f32[6]{0:T(128)S(1)}, f32[6]{0:T(128)}, u32[]{:S(2)}) copy-start(f32[6]{0:T(128)} %copy-done.11) | copy-start | bytes 76
  182.3 4.1 %collective-permute-start.3 = (f32[6,768]{1,0:T(8,128)S(1)}, f32[6,768]{1,0:T(8,128)S(1)}, u32[]{:S(2)}, u32[]{:S(2)}) collective-permute-start(f32[6,768]{1,0:T(8,128)S(1)} %fusion.29), channel_id=1, source_target_pairs={{0,28},{4,0},{8,4},{12,8},{16,12},{20,16},{24,20},{28,24},{1,29},{... | collective-permute-start | bytes 55304 | tf_op jit(solution)/shard_map/ppermute | solution.py:12
Sparse Core Ops, SparseCore 0:
  21.6 18.0 reduce-scatter.2
  127.5 18.0 reduce-scatter.4
where the time goes:
time: 234 us; the launch traced here: 233 us
  blocking collectives  140 us (60%)
  waiting for transfers between devices  50.1 us (21%)
  matrix products  18.9 us (8%)
  between operations  15.1 us (6%)
  starting transfers between devices  5.6 us (2%)
  other arithmetic  2.34 us (1%)
    psum x2, blocking collectives, paired_inner(): lax.psum((jnp.sum(residual * precon, axis=1), jnp.sum(precon * image, axi...  74.2 us
    psum x2, blocking collectives, operate(): corner_total = lax.psum(chain_rows, 'sub')  44 us
    reduce_scatter x2, waiting for transfers between devices, operate(): lax.psum_scatter(spread, 'crs', scatter_dimension=1, tiled=True)  36.3 us
    psum x2, blocking collectives, operate(): corner_solution = lax.psum(partial_solution, 'crs')  21.4 us
    dot_general x20, matrix products, product(): jnp.dot(left, right, precision=lax.Precision.HIGHEST, preferred_element_t...  18.9 us
    ppermute x4, waiting for transfers between devices, passed_along(): return lax.ppermute(value, axis, pairs)  13.7 us
    ppermute x4, starting transfers between devices, passed_along(): return lax.ppermute(value, axis, pairs)  5.53 us
  transfers between devices with their start and end apart: 6, of which 6 were waited for; matrix products, arithmetic and copies ran while one was open for 1% of the time, Pallas kernels for 0%

commit v1 on v0

v1 whole, which is shorter than its diff:
```python
import functools

import jax
import jax.numpy as jnp
from jax import lax
from jax.experimental import pallas as pl
from jax.experimental.pallas import tpu as pltpu
from jax.sharding import PartitionSpec as P

F32 = jnp.float32
BF16 = jnp.bfloat16
ROWS = 8
LANES = 128
SLOT = 32
GROUP = LANES // SLOT
VMEM_LIMIT = 40 << 20


def parts(x, count):
    out = []
    for _ in range(count):
        out.append(x.astype(BF16))
        x = x - out[-1].astype(F32)
    return out


def dot(a, b, transposed=False):
    dims = (((1,), (1 if transposed else 0,)), ((), ()))
    return lax.dot_general(a, b, dims, preferred_element_type=F32)


def moved(a, chosen, transposed=False):
    rows = a.shape[0]
    all_parts = dot(jnp.concatenate(parts(a, 3), axis=0), chosen, transposed)
    return all_parts[:rows] + all_parts[rows : 2 * rows] + all_parts[2 * rows :]


def product(a, high, low, transposed=False):
    rows = a.shape[0]
    top, rest = parts(a, 2)
    both = dot(jnp.concatenate([top, rest], axis=0), high, transposed)
    return both[:rows] + both[rows:] + dot(top, low, transposed)


def chosen_columns(index, count):
    shape = (count, index.shape[1])
    rows = lax.broadcasted_iota(jnp.int32, shape, 0)
    return jnp.where(rows == index, 1.0, 0.0).astype(BF16)


def row_sum(x):
    return jnp.sum(x, axis=1, keepdims=True)


def padded(x, rows):
    return jnp.concatenate([x, jnp.zeros((rows - x.shape[0], x.shape[1]), x.dtype)], axis=0)


def pack_kernel(live_ref, jump_ref, scale_ref, nbr_ref, out_ref):
    cases, records = jump_ref.shape[2:]
    live = lax.broadcasted_iota(jnp.int32, (1, records), 1) < live_ref[0, 0]
    live = live.astype(F32)
    out_ref[:cases] = jump_ref[0, 0] * live
    out_ref[cases : cases + 1] = scale_ref[0] * live
    out_ref[cases + 1 : cases + 2] = nbr_ref[0].astype(F32)


def unpacked(pack, cases):
    rows = lax.broadcasted_iota(jnp.int32, pack.shape, 0)
    residual = jnp.where(rows < cases, pack, 0.0)
    return residual, pack[cases : cases + 1], pack[cases + 1 : cases + 2].astype(jnp.int32)


def prepare_kernel(
    cases, pack_ref, schur_ref, coupling_ref, inverse_ref, own_ref,
    s_high, s_low, inv_high, inv_low, c_high, c_low, own_map, own_coupling, load_ref,
):
    s_high[...], s_low[...] = parts(schur_ref[0, 0], 2)
    inv_high[...], inv_low[...] = parts(inverse_ref[...], 2)
    coupling = coupling_ref[0, 0]
    block = padded(coupling, SLOT)
    c_high[...], c_low[...] = parts(jnp.concatenate([block] * GROUP, axis=0), 2)
    chosen = chosen_columns(own_ref[0], coupling.shape[1])
    own_map[...] = chosen
    own_coupling[...] = moved(coupling, chosen)
    residual, scale, _ = unpacked(pack_ref[...], cases)
    load_ref[...] = moved(residual * scale, chosen, True)


def forces(load, through, first, c_high, c_low, index_ref, cases, send_ref):
    force = product(load, c_high[...], c_low[...], True)
    lane = lax.broadcasted_iota(jnp.int32, force.shape, 1) % SLOT
    row = lax.broadcasted_iota(jnp.int32, force.shape, 0)
    force = jnp.where(lane == SLOT - 2, first, force)
    force = jnp.where(lane == SLOT - 1, row_sum(load * through), force)
    force = jnp.where(row == cases, index_ref[...], force)
    send_ref[...] = jnp.broadcast_to(force[None], send_ref.shape)


def first_kernel(
    cases, left_ref, pack_ref, load_ref, coupling_ref, own_coupling, index_ref,
    s_high, s_low, c_high, c_low, own_map,
    send_ref, right_ref, back_ref, left_map,
):
    left_residual, left_scale, left_index = unpacked(left_ref[...], cases)
    chosen = chosen_columns(left_index, coupling_ref.shape[3])
    left_map[...] = chosen
    load = load_ref[...] - moved(left_residual * left_scale, chosen, True)
    through = product(load, s_high[...], s_low[...])
    residual, scale, _ = unpacked(pack_ref[...], cases)
    norm = row_sum(residual * residual * scale)
    forces(load, through, norm, c_high, c_low, index_ref, cases, send_ref)
    right_ref[:ROWS] = moved(through, own_map[...])
    right_ref[ROWS:] = own_coupling[...]
    back_ref[:ROWS] = moved(through, chosen)
    back_ref[ROWS:] = moved(coupling_ref[0, 0], chosen)


def coarse_kernel(cases, place_ref, all_ref, inv_high, inv_low, x_ref, total_ref, sums_ref, index_ref):
    devices = all_ref.shape[0]
    corners = total_ref.shape[1]
    chunk = min(devices, LANES // GROUP)
    lane = lax.broadcasted_iota(jnp.int32, (ROWS, LANES), 1) // SLOT
    row = lax.broadcasted_iota(jnp.int32, (ROWS, 1), 0)
    step = min(corners, 1024)

    def add(at):
        pieces = []
        sums = jnp.zeros((ROWS, LANES), F32)
        for group in range(chunk // GROUP):
            piece = all_ref[at + group * GROUP]
            sums = sums + piece
            for e in range(1, GROUP):
                other = all_ref[at + group * GROUP + e]
                sums = sums + other
                piece = jnp.where(lane == e, other, piece)
            pieces.append(piece)
        flat = jnp.concatenate(pieces, axis=1)
        index = flat[cases : cases + 1].astype(jnp.int32)
        force = jnp.where(row < cases, flat, 0.0)
        total = [
            moved(force, chosen_columns(index - start, step), True)
            for start in range(0, corners, step)
        ]
        return sums, jnp.concatenate(total, axis=1)

    sums, total = add(0)
    sums_ref[...] = sums
    total_ref[...] = total
    if devices > chunk:

        @pl.loop(1, devices // chunk)
        def _(i):
            sums, total = add(i * chunk)
            sums_ref[...] += sums
            total_ref[...] += total

    x_ref[...] = product(total_ref[...], inv_high[...], inv_low[...])
    index = all_ref[place_ref[0], cases : cases + 1]
    for e in (1, 2):
        index = jnp.where(lane[:1] == e, all_ref[place_ref[e], cases : cases + 1], index)
    index_ref[...] = jnp.broadcast_to(index, index_ref.shape)


def picked_corners(place_ref, pieces, whole, index_ref):
    width = pieces[0].shape[1]
    for m, piece in enumerate(pieces):
        base = lax.rem(place_ref[3] + m, len(pieces)) * width
        whole[:, pl.ds(pl.multiple_of(base, width), width)] = piece[...]
    solution = whole[...]
    index = index_ref[:1].astype(jnp.int32)
    return solution, moved(solution, chosen_columns(index, solution.shape[1]))


def column(x, lane):
    return x[:, lane : lane + 1]


def second_kernel(
    cases, count, place_ref, *refs,
):
    pieces = refs[:count]
    (
        total_ref, sums_ref, index_ref, pack_ref, left_ref, right_ref, back_ref, from_left, from_right,
        own_map, left_map, s_high, s_low, c_high, c_low, corner_ref,
        send_ref, out_ref, keep_ref, spread_ref, scalar_ref, whole,
    ) = refs[count:]
    solution, picked = picked_corners(place_ref, pieces, whole, index_ref)
    blank = jnp.zeros((SLOT - (right_ref.shape[0] - ROWS), right_ref.shape[1]), F32)
    none = jnp.zeros((SLOT, right_ref.shape[1]), F32)
    own = jnp.concatenate([none, right_ref[ROWS:], blank, -from_right[ROWS:], blank, none], axis=0)
    other = jnp.concatenate([from_left[ROWS:], blank, -back_ref[ROWS:], blank, none, none], axis=0)
    spread_ref[...] = own
    both = product(picked, *parts(jnp.concatenate([own, other], axis=1), 2))
    records = right_ref.shape[1]
    residual, scale, _ = unpacked(pack_ref[...], cases)
    left_residual, left_scale, _ = unpacked(left_ref[...], cases)
    live = (scale > 0.0).astype(F32)
    left_live = (left_scale > 0.0).astype(F32)
    image = (right_ref[:ROWS] - from_right[:ROWS] + both[:, :records]) * live
    left_image = (from_left[:ROWS] - back_ref[:ROWS] + both[:, records:]) * left_live
    norm = column(sums_ref[...], SLOT - 2)
    curvature = column(sums_ref[...], SLOT - 1) + row_sum(total_ref[...] * solution)
    row = lax.broadcasted_iota(jnp.int32, (ROWS, 1), 0)
    alpha = jnp.where(row < cases, norm / curvature, 0.0)
    residual = residual - alpha * image
    left_residual = left_residual - alpha * left_image
    precon = scale * residual
    left_precon = left_scale * left_residual
    load = moved(precon, own_map[...], True) - moved(left_precon, left_map[...], True)
    through = product(load, s_high[...], s_low[...])
    forces(load, through, row_sum(residual * precon), c_high, c_low, corner_ref, cases, send_ref)
    out_ref[...] = moved(through, left_map[...])
    keep_ref[:ROWS] = moved(through, own_map[...])
    keep_ref[ROWS:] = image
    lane = lax.broadcasted_iota(jnp.int32, scalar_ref.shape, 1)
    scalar_ref[...] = jnp.where(lane == 0, norm, alpha)


def last_kernel(cases, count, place_ref, *refs):
    pieces = refs[:count]
    (
        total_ref, sums_ref, index_ref, pack_ref, from_right, keep_ref, spread_ref, scalar_ref,
        multipliers_ref, residual_ref, whole,
    ) = refs[count:]
    solution, picked = picked_corners(place_ref, pieces, whole, index_ref)
    residual, scale, _ = unpacked(pack_ref[...], cases)
    live = (scale > 0.0).astype(F32)
    coarse = product(picked, *parts(spread_ref[...], 2))
    image = (keep_ref[:ROWS] - from_right[...] + coarse) * live
    along = keep_ref[ROWS:]
    first_norm = column(scalar_ref[...], 0)
    first_alpha = column(scalar_ref[...], 1)
    norm = column(sums_ref[...], SLOT - 2)
    curvature = column(sums_ref[...], SLOT - 1) + row_sum(total_ref[...] * solution)
    ratio = norm / first_norm
    alpha = norm / (curvature - ratio * norm / first_alpha)
    direction = scale * residual
    multipliers = first_alpha * direction
    residual = residual - first_alpha * along
    direction = scale * residual + ratio * direction
    along = image + ratio * along
    multipliers = multipliers + alpha * direction
    residual = residual - alpha * along
    multipliers_ref[0, 0] = multipliers[:cases]
    residual_ref[0, 0] = residual[:cases]


VM = pl.BlockSpec(memory_space=pltpu.VMEM)
SM = pl.BlockSpec(memory_space=pltpu.SMEM)


def call(kernel, outs, given, scalars=0, scratch=()):
    return pl.pallas_call(
        kernel,
        out_shape=[jax.ShapeDtypeStruct(shape, kind) for shape, kind in outs],
        in_specs=[SM] * scalars + [VM] * (len(given) - scalars),
        out_specs=[VM] * len(outs),
        scratch_shapes=list(scratch),
        compiler_params=pltpu.CompilerParams(vmem_limit_bytes=VMEM_LIMIT),
    )(*given)


def passed_along(value, axis, steps):
    count = lax.axis_size(axis)
    pairs = [(source, (source + steps) % count) for source in range(count)]
    return lax.ppermute(value, axis, pairs)


def per_device(
    jump_data,
    lumped_scale,
    schur_inverse,
    coarse_coupling,
    corner_inverse,
    own_dof,
    nbr_dof,
    live_count,
    corner_index,
):
    cases, records = jump_data.shape[2:]
    held, iface = coarse_coupling.shape[2:]
    corners, width = corner_inverse.shape
    chain, slabs = lax.axis_size("sub"), lax.axis_size("crs")
    devices = chain * slabs
    here, slab = lax.axis_index("sub"), lax.axis_index("crs")
    place = jnp.stack(
        [
            (here + chain - 1) % chain * slabs + slab,
            here * slabs + slab,
            (here + 1) % chain * slabs + slab,
            slab,
        ]
    ).astype(jnp.int32)
    index = jnp.pad(corner_index[0, 0].astype(F32), (0, SLOT - held), constant_values=-1.0)
    index = jnp.tile(index, GROUP)[None]

    (pack,) = call(
        pack_kernel, [((ROWS, records), F32)], (live_count, jump_data, lumped_scale, nbr_dof), 1
    )
    left = passed_along(pack, "sub", 1)
    s_high, s_low, inv_high, inv_low, c_high, c_low, own_map, own_coupling, load = call(
        functools.partial(prepare_kernel, cases),
        [
            ((iface, iface), BF16),
            ((iface, iface), BF16),
            ((corners, width), BF16),
            ((corners, width), BF16),
            ((LANES, iface), BF16),
            ((LANES, iface), BF16),
            ((iface, records), BF16),
            ((held, records), F32),
            ((ROWS, iface), F32),
        ],
        (pack, schur_inverse, coarse_coupling, corner_inverse, own_dof),
    )
    send, right, back, left_map = call(
        functools.partial(first_kernel, cases),
        [
            ((devices, ROWS, LANES), F32),
            ((ROWS + held, records), F32),
            ((ROWS + held, records), F32),
            ((iface, records), BF16),
        ],
        (
            left, pack, load, coarse_coupling, own_coupling, index,
            s_high, s_low, c_high, c_low, own_map,
        ),
    )

    def coarse(send):
        gathered = lax.all_to_all(send, ("sub", "crs"), 0, 0)
        x, total, sums, near = call(
            functools.partial(coarse_kernel, cases),
            [
                ((ROWS, width), F32),
                ((ROWS, corners), F32),
                ((ROWS, LANES), F32),
                ((ROWS, LANES), F32),
            ],
            (place, gathered, inv_high, inv_low),
            1,
        )
        pieces = [x] + [passed_along(x, "crs", -m) for m in range(1, slabs)]
        return pieces, total, sums, near

    from_left = passed_along(right, "sub", 1)
    from_right = passed_along(back, "sub", -1)
    pieces, total, sums, near = coarse(send)
    whole = [pltpu.VMEM((ROWS, corners), F32)]
    send, out, keep, spread, scalars = call(
        functools.partial(second_kernel, cases, slabs),
        [
            ((devices, ROWS, LANES), F32),
            ((ROWS, records), F32),
            ((2 * ROWS, records), F32),
            ((LANES, records), F32),
            ((ROWS, LANES), F32),
        ],
        (
            place, *pieces, total, sums, near, pack, left, right, back, from_left, from_right,
            own_map, left_map, s_high, s_low, c_high, c_low, index,
        ),
        1,
        whole,
    )
    from_right = passed_along(out, "sub", -1)
    pieces, total, sums, near = coarse(send)
    shape = jump_data.shape
    return tuple(
        call(
            functools.partial(last_kernel, cases, slabs),
            [(shape, F32), (shape, F32)],
            (
                place, *pieces, total, sums, near, pack, from_right, keep, spread, scalars,
            ),
            1,
            whole,
        )
    )


def solution(mesh):
    return jax.shard_map(
        per_device,
        mesh=mesh,
        in_specs=(
            P("sub", "crs", None, None),
            P("sub", "crs", None),
            P("sub", "crs", None, None),
            P("sub", "crs", None, None),
            P(None, "crs"),
            P("sub", "crs", None),
            P("sub", "crs", None),
            P("sub", "crs"),
            P("sub", "crs", None),
        ),
        out_specs=(P("sub", "crs", None, None), P("sub", "crs", None, None)),
        check_vma=False,
    )
```

time: 234 us -> 62.9 us (0.27)
  blocking collectives: 140 us -> 0 us
  waiting for transfers between devices: 50.1 us -> 11.2 us
  matrix products: 18.9 us -> 0 us
  starting transfers between devices: 5.6 us -> 24.1 us
  local copies, waits for them, and re-layouts: 1.33 us -> 15.2 us
  between operations: 15.1 us -> 1.48 us
  Pallas kernels: 0 us -> 8.99 us
    psum x6 -> x0, blocking collectives: 140 us -> none  [the longest x2 74.2 us: paired_inner(): lax.psum((jnp.sum(residual * precon, axis=1), jnp.sum(precon * image, axi...]
    reduce_scatter x2 -> x0, waiting for transfers between devices: 36.3 us -> none  [operate(): lax.psum_scatter(spread, 'crs', scatter_dimension=1, tiled=True)]
    dot_general x20 -> x0, matrix products: 18.9 us -> none  [product(): jnp.dot(left, right, precision=lax.Precision.HIGHEST, preferred_element_t...]
    unnamed x52 -> x53, local copies, waits for them, and re-layouts: 1.33 us -> 13.9 us
    ppermute x4 -> x10, starting transfers between devices: 5.53 us -> 16.4 us  [passed_along(): return lax.ppermute(value, axis, pairs)]
    ppermute x4 -> x10, waiting for transfers between devices: 13.7 us -> 4.18 us  [passed_along(): return lax.ppermute(value, axis, pairs)]
    pallas_call x0 -> x7, Pallas kernels: none -> 8.99 us  [call(): pl.pallas_call(kernel, out_shape=[jax.ShapeDtypeStruct(shape, kind) for s...]
    all_to_all x0 -> x2, starting transfers between devices: none -> 7.72 us  [coarse(): gathered = lax.all_to_all(send, ('sub', 'crs'), 0, 0)]
  transfers between devices with their start and end apart: 6 -> 12, of which waited for: 6 -> 6; matrix products, arithmetic and copies ran while one was open for 1% -> 1% of each run, Pallas kernels for 0% -> 8%
where the time goes in v1:
time: 62.9 us; the launch traced here: 61.7 us
  starting transfers between devices  24.1 us (38%)
  local copies, waits for them, and re-layouts  15.2 us (24%)
  waiting for transfers between devices  11.2 us (18%)
  Pallas kernels  8.99 us (14%)
  between operations  1.48 us (2%)
  other arithmetic  0.73 us (1%)
    ppermute x10, starting transfers between devices, passed_along(): return lax.ppermute(value, axis, pairs)  16.4 us
    unnamed x53, local copies, waits for them, and re-layouts  13.9 us
    pallas_call x7, Pallas kernels, call(): pl.pallas_call(kernel, out_shape=[jax.ShapeDtypeStruct(shape, kind) for s...  8.99 us
    all_to_all x2, starting transfers between devices, coarse(): gathered = lax.all_to_all(send, ('sub', 'crs'), 0, 0)  7.72 us
    all_to_all x2, waiting for transfers between devices, coarse(): gathered = lax.all_to_all(send, ('sub', 'crs'), 0, 0)  7 us
    ppermute x10, waiting for transfers between devices, passed_along(): return lax.ppermute(value, axis, pairs)  4.18 us
  transfers between devices with their start and end apart: 12, of which 6 were waited for; matrix products, arithmetic and copies ran while one was open for 1% of the time, Pallas kernels for 8%

profile of v1, /device:TPU:0, one launch (start us, length us, event | category | flops | bytes accessed | tf_op | source)
XLA Modules:
  0.0 61.7 jit_solution(10007352423650453109)
XLA Ops:
  1.3 0.7 %copy.11.jump_ref = f32[1,1,6,384]{3,2,1,0:T(8,128)S(1)} copy(f32[1,1,6,384]{3,1,2,0:T(1,128)} %param.9) | data formatting | bytes 18432 | tf_op args[0]
  2.0 0.7 %copy-done.23 = f32[1,1,384]{2,1,0:T(1,128)S(1)} copy-done((f32[1,1,384]{2,1,0:T(1,128)S(1)}, f32[1,1,384]{2,1,0:T(1,128)}, u32[]{:S(2)}) %copy-start.23) | copy-done | bytes 1560
  2.7 0.7 %copy-done.24 = s32[1,1,384]{2,1,0:T(1,128)S(1)} copy-done((s32[1,1,384]{2,1,0:T(1,128)S(1)}, s32[1,1,384]{2,1,0:T(1,128)}, u32[]{:S(2)}) %copy-start.24) | copy-done | bytes 1560
  3.4 3.0 %collective-permute-start = (f32[8,384]{1,0:T(8,128)S(1)}, f32[8,384]{1,0:T(8,128)S(1)}, u32[]{:S(2)}, u32[]{:S(2)}) collective-permute-start(f32[8,384]{1,0:T(8,128)S(1)} %shard_map.104.pack_ref.refs_7_), channel_id=1, source_target_pairs={{0,4},{4,8},{8,12},{12,16},{16,20},{20,24},{24,28},{28,0},{1,5},{5... | collective-permute-start | bytes 36872 | tf_op jit(solution)/shard_map/ppermute | solution.py:267
  6.4 0.7 %convert_bitcast_fusion = f32[24]{0:T(128)S(1)} fusion(s32[1,1,24]{2,1,0:T(1,128)} %param.17), kind=kLoop, calls=%fused_computation.1 | loop fusion | flops 24 | bytes 192 | tf_op jit(solution)/shard_map/convert_element_type | solution.py:295
  7.0 0.1 broadcast_in_dim_tile.3.index_ref.refs_19_
  7.1 1.7 %copy-done = f32[1,1,768,768]{3,2,1,0:T(8,128)S(1)} copy-done((f32[1,1,768,768]{3,2,1,0:T(8,128)S(1)}, f32[1,1,768,768]{3,2,1,0:T(8,128)}, u32[]{:S(2)}) %copy-start) | copy-done | bytes 2359320
  8.8 1.2 %copy-done.4 = f32[1024,256]{1,0:T(8,128)S(1)} copy-done((f32[1024,256]{1,0:T(8,128)S(1)}, f32[1024,256]{1,0:T(8,128)}, u32[]{:S(2)}) %copy-start.4) | copy-done | bytes 1048600
  10.0 0.9 %copy-done.11 = f32[1,1,24,768]{3,2,1,0:T(8,128)S(1)} copy-done((f32[1,1,24,768]{3,2,1,0:T(8,128)S(1)}, f32[1,1,24,768]{3,2,1,0:T(8,128)}, u32[]{:S(2)}) %copy-start.11) | copy-done | bytes 73752
  10.9 0.7 %copy-done.22 = s32[1,1,384]{2,1,0:T(1,128)S(1)} copy-done((s32[1,1,384]{2,1,0:T(1,128)S(1)}, s32[1,1,384]{2,1,0:T(1,128)}, u32[]{:S(2)}) %copy-start.22) | copy-done | bytes 1560
  11.6 1.4 %shard_map.105 = (bf16[768,768]{1,0:T(8,128)(2,1)S(1)}, bf16[768,768]{1,0:T(8,128)(2,1)S(1)}, bf16[1024,256]{1,0:T(8,128)(2,1)S(1)}, bf16[1024,256]{1,0:T(8,128)...) custom-call(f32[8,384]{1,0:T(8,128)S(1)} %shard_map.104.pack_ref.ref, ...), custom_call_target="tpu_custom_call" | custom-call | tf_op jit(solution)/shard_map/pallas_call | solution.py:254
  13.1 0.0 collective-permute-done.left_ref.refs_8_
  13.1 1.2 %shard_map.106 = (f32[32,8,128]{2,1,0:T(8,128)S(1)}, f32[32,384]{1,0:T(8,128)S(1)}, f32[32,384]{1,0:T(8,128)S(1)}, bf16[768,384]{1,0:T(8,128)(2,1)S(1)}) custom-call(f32[8,384]{1,0:T(8,128)S(1)} %collective-permute-done.left_ref.refs_8_, f32[8,384]{1,0:T(8,128)S(1)} %shard_map.104.pack_ref.refs_7_, f32[8,768]{1,0:T(8,128)S(1)} %get-tuple-element.28.load_ref, ...), custom_call_target="tpu_custom_call" | custom-call | tf_op jit(solution)/shard_map/pallas_call | solution.py:254
  14.3 0.8 %copy-done.9 = bf16[768,384]{1,0:T(8,128)(2,1)} copy-done((bf16[768,384]{1,0:T(8,128)(2,1)}, bf16[768,384]{1,0:T(8,128)(2,1)S(1)}, u32[]{:S(2)}) %copy-start.9) | copy-done | bytes 589848
  15.1 0.7 %copy-done.14 = f32[32,8,128]{2,1,0:T(8,128)} copy-done((f32[32,8,128]{2,1,0:T(8,128)}, f32[32,8,128]{2,1,0:T(8,128)S(1)}, u32[]{:S(2)}) %copy-start.14) | copy-done | bytes 131096
  15.8 0.6 %copy-done.16 = f32[32,384]{1,0:T(8,128)} copy-done((f32[32,384]{1,0:T(8,128)}, f32[32,384]{1,0:T(8,128)S(1)}, u32[]{:S(2)}) %copy-start.16) | copy-done | bytes 49176
  16.4 5.0 %all-to-all-start = ((f32[32,8,128]{2,1,0:T(8,128)}), f32[32,8,128]{2,1,0:T(8,128)}, u32[]{:S(2)}, u32[]{:S(2)}) async-start(f32[32,8,128]{2,1,0:T(8,128)} %copy-done.14), calls=%async_computation | async-start | bytes 262144 | tf_op jit(solution)/shard_map/all_to_all | solution.py:332
  21.4 1.7 %collective-permute-start.4 = (f32[32,384]{1,0:T(8,128)S(1)}, f32[32,384]{1,0:T(8,128)}, u32[]{:S(2)}, u32[]{:S(2)}) collective-permute-start(f32[32,384]{1,0:T(8,128)S(1)} %get-tuple-element.42.refs_9_), channel_id=1, source_target_pairs={{0,4},{4,8},{8,12},{12,16},{16,20},{20,24},{24,28},{28,0},{1,5},{5... | collective-permute-start | bytes 147464 | tf_op jit(solution)/shard_map/ppermute | solution.py:267
  23.2 3.0 %collective-permute-start.5 = (f32[32,384]{1,0:T(8,128)}, f32[32,384]{1,0:T(8,128)}, u32[]{:S(2)}, u32[]{:S(2)}) collective-permute-start(f32[32,384]{1,0:T(8,128)} %copy-done.16), channel_id=1, source_target_pairs={{0,28},{4,0},{8,4},{12,8},{16,12},{20,16},{24,20},{28,24},{1,29},{... | collective-permute-start | bytes 147464 | tf_op jit(solution)/shard_map/ppermute | solution.py:267
  26.2 0.1 pad_add_fusion.place_ref
  26.3 3.4 %all-to-all-done.all_ref = f32[32,8,128]{2,1,0:T(8,128)} async-done(((f32[32,8,128]{2,1,0:T(8,128)}), f32[32,8,128]{2,1,0:T(8,128)}, u32[]{:S(2)}, u32[]{:S(2)}) %all-to-all-start) | async-done | bytes 131104 | tf_op jit(solution)/shard_map/all_to_all | solution.py:332
  29.7 1.0 %copy-done.2 = bf16[1024,256]{1,0:T(8,128)(2,1)S(1)} copy-done((bf16[1024,256]{1,0:T(8,128)(2,1)S(1)}, bf16[1024,256]{1,0:T(8,128)(2,1)}, u32[]{:S(2)}) %copy-start.2) | copy-done | bytes 524312
  30.7 1.9 %shard_map.107 = (f32[8,256]{1,0:T(8,128)S(1)}, f32[8,1024]{1,0:T(8,128)S(1)}, f32[8,128]{1,0:T(8,128)S(1)}, f32[8,128]{1,0:T(8,128)S(1)}) custom-call(s32[4]{0:T(128)S(1)} %pad_add_fusion.place_ref, f32[32,8,128]{2,1,0:T(8,128)} %all-to-all-done.all_ref, bf16[1024,256]{1,0:T(8,128)(2,1)S(1)} %get-tuple-element.36.inv_high, bf16[1024,256]{1,0:T(8,128)(2,1)S(1)} %copy-done.2), custom_call_target="tpu_custom_call" | custom-call | tf_op jit(solution)/shard_map/pallas_call | solution.py:254
  32.6 0.6 %collective-permute-start.3 = (f32[8,256]{1,0:T(8,128)S(1)}, f32[8,256]{1,0:T(8,128)S(1)}, u32[]{:S(2)}, u32[]{:S(2)}) collective-permute-start(f32[8,256]{1,0:T(8,128)S(1)} %get-tuple-element.38.refs_0_), channel_id=1, source_target_pairs={{0,1},{1,2},{2,3},{3,0},{4,5},{5,6},{6,7},{7,4},{8,9},{9,10},{10,1... | collective-permute-start | bytes 24584 | tf_op jit(solution)/shard_map/ppermute | solution.py:267
  33.2 0.1 collective-permute-start.2
  33.4 1.3 %collective-permute-start.1 = (f32[8,256]{1,0:T(8,128)S(1)}, f32[8,256]{1,0:T(8,128)S(1)}, u32[]{:S(2)}, u32[]{:S(2)}) collective-permute-start(f32[8,256]{1,0:T(8,128)S(1)} %get-tuple-element.38.refs_0_), channel_id=1, source_target_pairs={{0,3},{1,0},{2,1},{3,2},{4,7},{5,4},{6,5},{7,6},{8,11},{9,8},{10,9... | collective-permute-start | bytes 24584 | tf_op jit(solution)/shard_map/ppermute | solution.py:267
  34.7 0.0 collective-permute-done.4.refs_11_
  34.7 1.0 %collective-permute-done.3.refs_3_ = f32[8,256]{1,0:T(8,128)S(1)} collective-permute-done((f32[8,256]{1,0:T(8,128)S(1)}, f32[8,256]{1,0:T(8,128)S(1)}, u32[]{:S(2)}, u32[]{:S(2)}) %collective-permute-start.3) | collective-permute-done | bytes 8224 | tf_op jit(solution)/shard_map/ppermute | solution.py:267
  35.7 1.2 %collective-permute-done.2.refs_2_ = f32[8,256]{1,0:T(8,128)S(1)} collective-permute-done((f32[8,256]{1,0:T(8,128)S(1)}, f32[8,256]{1,0:T(8,128)S(1)}, u32[]{:S(2)}, u32[]{:S(2)}) %collective-permute-start.2) | collective-permute-done | bytes 8224 | tf_op jit(solution)/shard_map/ppermute | solution.py:267
  36.9 2.2 %shard_map.108 = (f32[32,8,128]{2,1,0:T(8,128)S(1)}, f32[8,384]{1,0:T(8,128)S(1)}, f32[16,384]{1,0:T(8,128)S(1)}, f32[128,384]{1,0:T(8,128)S(1)}, f32[8,128]{1,0:T(8,128)S(1)}) custom-call(s32[4]{0:T(128)S(1)} %pad_add_fusion.place_ref, f32[8,256]{1,0:T(8,128)S(1)} %get-tuple-element.38.refs_0_, f32[8,256]{1,0:T(8,128)S(1)} %collective-permute-done.1.refs_1_, ...), custom_call_target="tpu_custom_call" | custom-call | tf_op jit(solution)/shard_map/pallas_call | solution.py:254
  39.1 0.7 %copy-done.12 = f32[128,384]{1,0:T(8,128)} copy-done((f32[128,384]{1,0:T(8,128)}, f32[128,384]{1,0:T(8,128)S(1)}, u32[]{:S(2)}) %copy-start.12) | copy-done | bytes 196632
  39.8 0.6 %copy-done.15 = f32[32,8,128]{2,1,0:T(8,128)} copy-done((f32[32,8,128]{2,1,0:T(8,128)}, f32[32,8,128]{2,1,0:T(8,128)S(1)}, u32[]{:S(2)}) %copy-start.15) | copy-done | bytes 131096
  40.5 0.6 copy-done.18
  41.1 0.6 copy-done.20
  41.7 0.6 copy-done.25
  42.3 2.7 %all-to-all-start.1 = ((f32[32,8,128]{2,1,0:T(8,128)}), f32[32,8,128]{2,1,0:T(8,128)S(1)}, u32[]{:S(2)}, u32[]{:S(2)}) async-start(f32[32,8,128]{2,1,0:T(8,128)} %copy-done.15), calls=%async_computation.1 | async-start | bytes 262144 | tf_op jit(solution)/shard_map/all_to_all | solution.py:332
  45.0 4.6 %collective-permute-start.9 = (f32[8,384]{1,0:T(8,128)}, f32[8,384]{1,0:T(8,128)S(1)}, u32[]{:S(2)}, u32[]{:S(2)}) collective-permute-start(f32[8,384]{1,0:T(8,128)} %copy-done.25), channel_id=1, source_target_pairs={{0,28},{4,0},{8,4},{12,8},{16,12},{20,16},{24,20},{28,24},{1,29},{... | collective-permute-start | bytes 36872 | tf_op jit(solution)/shard_map/ppermute | solution.py:267
  49.6 3.6 %all-to-all-done.1.all_ref = f32[32,8,128]{2,1,0:T(8,128)S(1)} async-done(((f32[32,8,128]{2,1,0:T(8,128)}), f32[32,8,128]{2,1,0:T(8,128)S(1)}, u32[]{:S(2)}, u32[]{:S(2)}) %all-to-all-start.1) | async-done | bytes 131104 | tf_op jit(solution)/shard_map/all_to_all | solution.py:332
  53.2 1.0 %copy-done.3 = bf16[1024,256]{1,0:T(8,128)(2,1)S(1)} copy-done((bf16[1024,256]{1,0:T(8,128)(2,1)S(1)}, bf16[1024,256]{1,0:T(8,128)(2,1)}, u32[]{:S(2)}) %copy-start.3) | copy-done | bytes 524312
  54.3 1.4 %shard_map.109 = (f32[8,256]{1,0:T(8,128)S(1)}, f32[8,1024]{1,0:T(8,128)S(1)}, f32[8,128]{1,0:T(8,128)S(1)}, f32[8,128]{1,0:T(8,128)S(1)}) custom-call(s32[4]{0:T(128)S(1)} %pad_add_fusion.place_ref, f32[32,8,128]{2,1,0:T(8,128)S(1)} %all-to-all-done.1.all_ref, bf16[1024,256]{1,0:T(8,128)(2,1)S(1)} %get-tuple-element.36.inv_high, bf16[1024,256]{1,0:T(8,128)(2,1)S(1)} %copy-done.3), custom_call_target="tpu_custom_call" | custom-call | tf_op jit(solution)/shard_map/pallas_call | solution.py:254
  55.7 0.2 collective-permute-start.8
  55.9 0.3 collective-permute-start.7
  56.3 1.4 %collective-permute-start.6 = (f32[8,256]{1,0:T(8,128)S(1)}, f32[8,256]{1,0:T(8,128)S(1)}, u32[]{:S(2)}, u32[]{:S(2)}) collective-permute-start(f32[8,256]{1,0:T(8,128)S(1)} %get-tuple-element.46.refs_0_), channel_id=1, source_target_pairs={{0,3},{1,0},{2,1},{3,2},{4,7},{5,4},{6,5},{7,6},{8,11},{9,8},{10,9... | collective-permute-start | bytes 24584 | tf_op jit(solution)/shard_map/ppermute | solution.py:267
  57.6 1.2 %collective-permute-done.8.refs_3_ = f32[8,256]{1,0:T(8,128)S(1)} collective-permute-done((f32[8,256]{1,0:T(8,128)S(1)}, f32[8,256]{1,0:T(8,128)S(1)}, u32[]{:S(2)}, u32[]{:S(2)}) %collective-permute-start.8) | collective-permute-done | bytes 8224 | tf_op jit(solution)/shard_map/ppermute | solution.py:267
  58.8 0.8 %collective-permute-done.7.refs_2_ = f32[8,256]{1,0:T(8,128)S(1)} collective-permute-done((f32[8,256]{1,0:T(8,128)S(1)}, f32[8,256]{1,0:T(8,128)S(1)}, u32[]{:S(2)}, u32[]{:S(2)}) %collective-permute-start.7) | collective-permute-done | bytes 8224 | tf_op jit(solution)/shard_map/ppermute | solution.py:267
  59.6 0.9 %shard_map.110 = (f32[1,1,6,384]{3,2,1,0:T(8,128)S(1)}, f32[1,1,6,384]{3,2,1,0:T(8,128)S(1)}) custom-call(s32[4]{0:T(128)S(1)} %pad_add_fusion.place_ref, f32[8,256]{1,0:T(8,128)S(1)} %get-tuple-element.46.refs_0_, f32[8,256]{1,0:T(8,128)S(1)} %collective-permute-done.6.refs_1_, f32[8,256]{1,0:T(8,128)S(1)} %collective-permute-done.7.refs_2_, ...), custom_call_target="tpu_custom_call" | custom-call | tf_op jit(solution)/shard_map/pallas_call | solution.py:254
  60.5 0.6 %copy.12 = f32[1,1,6,384]{3,1,2,0:T(1,128)} copy(f32[1,1,6,384]{3,2,1,0:T(8,128)S(1)} %get-tuple-element.54) | data formatting | bytes 18432 | tf_op jit(solution)/shard_map/pallas_call | solution.py:254
  61.1 0.6 copy.13
  (43 shorter events, 0.1 us)
Async XLA Ops:
  2.0 0.7 %copy-start.23 = (f32[1,1,384]{2,1,0:T(1,128)S(1)}, f32[1,1,384]{2,1,0:T(1,128)}, u32[]{:S(2)}) copy-start(f32[1,1,384]{2,1,0:T(1,128)} %scale_ref.1) | copy-start | bytes 4612
  2.7 0.7 %copy-start.24 = (s32[1,1,384]{2,1,0:T(1,128)S(1)}, s32[1,1,384]{2,1,0:T(1,128)}, u32[]{:S(2)}) copy-start(s32[1,1,384]{2,1,0:T(1,128)} %nbr_ref.1) | copy-start | bytes 4612
  3.4 9.7 %collective-permute-start = (f32[8,384]{1,0:T(8,128)S(1)}, f32[8,384]{1,0:T(8,128)S(1)}, u32[]{:S(2)}, u32[]{:S(2)}) collective-permute-start(f32[8,384]{1,0:T(8,128)S(1)} %shard_map.104.pack_ref.refs_7_), channel_id=1, source_target_pairs={{0,4},{4,8},{8,12},{12,16},{16,20},{20,24},{24,28},{28,0},{1,5},{5... | collective-permute-start | bytes 36872 | tf_op jit(solution)/shard_map/ppermute | solution.py:267
  7.1 1.7 %copy-start = (f32[1,1,768,768]{3,2,1,0:T(8,128)S(1)}, f32[1,1,768,768]{3,2,1,0:T(8,128)}, u32[]{:S(2)}) copy-start(f32[1,1,768,768]{3,2,1,0:T(8,128)} %schur_ref.1) | copy-start | bytes 7077892
  8.8 1.2 %copy-start.4 = (f32[1024,256]{1,0:T(8,128)S(1)}, f32[1024,256]{1,0:T(8,128)}, u32[]{:S(2)}) copy-start(f32[1024,256]{1,0:T(8,128)} %inverse_ref.1) | copy-start | bytes 3145732
  10.0 0.9 %copy-start.11 = (f32[1,1,24,768]{3,2,1,0:T(8,128)S(1)}, f32[1,1,24,768]{3,2,1,0:T(8,128)}, u32[]{:S(2)}) copy-start(f32[1,1,24,768]{3,2,1,0:T(8,128)} %coupling_ref.3) | copy-start | bytes 221188
  10.9 0.7 %copy-start.22 = (s32[1,1,384]{2,1,0:T(1,128)S(1)}, s32[1,1,384]{2,1,0:T(1,128)}, u32[]{:S(2)}) copy-start(s32[1,1,384]{2,1,0:T(1,128)} %own_ref.1) | copy-start | bytes 4612
  13.0 1.2 %copy-start.1 = (bf16[1024,256]{1,0:T(8,128)(2,1)}, bf16[1024,256]{1,0:T(8,128)(2,1)S(1)}, u32[]{:S(2)}) copy-start(bf16[1024,256]{1,0:T(8,128)(2,1)S(1)} %get-tuple-element.37.inv_low) | copy-start | bytes 1572868
  13.1 1.2 %copy-start.5 = (bf16[128,768]{1,0:T(8,128)(2,1)}, bf16[128,768]{1,0:T(8,128)(2,1)S(1)}, u32[]{:S(2)}) copy-start(bf16[128,768]{1,0:T(8,128)(2,1)S(1)} %get-tuple-element.32.c_high.refs_17_) | copy-start | bytes 589828
  13.1 1.2 %copy-start.7 = (bf16[128,768]{1,0:T(8,128)(2,1)}, bf16[128,768]{1,0:T(8,128)(2,1)S(1)}, u32[]{:S(2)}) copy-start(bf16[128,768]{1,0:T(8,128)(2,1)S(1)} %get-tuple-element.33.c_low.refs_18_) | copy-start | bytes 589828
  14.3 0.8 %copy-start.9 = (bf16[768,384]{1,0:T(8,128)(2,1)}, bf16[768,384]{1,0:T(8,128)(2,1)S(1)}, u32[]{:S(2)}) copy-start(bf16[768,384]{1,0:T(8,128)(2,1)S(1)} %get-tuple-element.44.refs_14_) | copy-start | bytes 1769476
  15.1 0.7 %copy-start.14 = (f32[32,8,128]{2,1,0:T(8,128)}, f32[32,8,128]{2,1,0:T(8,128)S(1)}, u32[]{:S(2)}) copy-start(f32[32,8,128]{2,1,0:T(8,128)S(1)} %get-tuple-element.35) | copy-start | bytes 393220
  15.8 0.6 %copy-start.16 = (f32[32,384]{1,0:T(8,128)}, f32[32,384]{1,0:T(8,128)S(1)}, u32[]{:S(2)}) copy-start(f32[32,384]{1,0:T(8,128)S(1)} %get-tuple-element.43.refs_10_) | copy-start | bytes 147460
  16.4 13.3 %all-to-all-start = ((f32[32,8,128]{2,1,0:T(8,128)}), f32[32,8,128]{2,1,0:T(8,128)}, u32[]{:S(2)}, u32[]{:S(2)}) async-start(f32[32,8,128]{2,1,0:T(8,128)} %copy-done.14), calls=%async_computation | async-start | bytes 262144 | tf_op jit(solution)/shard_map/all_to_all | solution.py:332
  21.4 13.2 %collective-permute-start.4 = (f32[32,384]{1,0:T(8,128)S(1)}, f32[32,384]{1,0:T(8,128)}, u32[]{:S(2)}, u32[]{:S(2)}) collective-permute-start(f32[32,384]{1,0:T(8,128)S(1)} %get-tuple-element.42.refs_9_), channel_id=1, source_target_pairs={{0,4},{4,8},{8,12},{12,16},{16,20},{20,24},{24,28},{28,0},{1,5},{5... | collective-permute-start | bytes 147464 | tf_op jit(solution)/shard_map/ppermute | solution.py:267
  23.2 11.5 %collective-permute-start.5 = (f32[32,384]{1,0:T(8,128)}, f32[32,384]{1,0:T(8,128)}, u32[]{:S(2)}, u32[]{:S(2)}) collective-permute-start(f32[32,384]{1,0:T(8,128)} %copy-done.16), channel_id=1, source_target_pairs={{0,28},{4,0},{8,4},{12,8},{16,12},{20,16},{24,20},{28,24},{1,29},{... | collective-permute-start | bytes 147464 | tf_op jit(solution)/shard_map/ppermute | solution.py:267
  29.7 1.0 %copy-start.2 = (bf16[1024,256]{1,0:T(8,128)(2,1)S(1)}, bf16[1024,256]{1,0:T(8,128)(2,1)}, u32[]{:S(2)}) copy-start(bf16[1024,256]{1,0:T(8,128)(2,1)} %copy-done.1) | copy-start | bytes 1572868
  30.7 6.2 %copy-start.6 = (bf16[128,768]{1,0:T(8,128)(2,1)S(1)}, bf16[128,768]{1,0:T(8,128)(2,1)}, u32[]{:S(2)}) copy-start(bf16[128,768]{1,0:T(8,128)(2,1)} %copy-done.5) | copy-start | bytes 589828
  30.7 6.2 %copy-start.8 = (bf16[128,768]{1,0:T(8,128)(2,1)S(1)}, bf16[128,768]{1,0:T(8,128)(2,1)}, u32[]{:S(2)}) copy-start(bf16[128,768]{1,0:T(8,128)(2,1)} %copy-done.7) | copy-start | bytes 589828
  30.7 6.2 %copy-start.10 = (bf16[768,384]{1,0:T(8,128)(2,1)S(1)}, bf16[768,384]{1,0:T(8,128)(2,1)}, u32[]{:S(2)}) copy-start(bf16[768,384]{1,0:T(8,128)(2,1)} %copy-done.9) | copy-start | bytes 1769476
  30.7 6.2 %copy-start.17 = (f32[32,384]{1,0:T(8,128)S(1)}, f32[32,384]{1,0:T(8,128)}, u32[]{:S(2)}) copy-start(f32[32,384]{1,0:T(8,128)} %copy-done.16) | copy-start | bytes 147460
  32.6 3.1 %collective-permute-start.3 = (f32[8,256]{1,0:T(8,128)S(1)}, f32[8,256]{1,0:T(8,128)S(1)}, u32[]{:S(2)}, u32[]{:S(2)}) collective-permute-start(f32[8,256]{1,0:T(8,128)S(1)} %get-tuple-element.38.refs_0_), channel_id=1, source_target_pairs={{0,1},{1,2},{2,3},{3,0},{4,5},{5,6},{6,7},{7,4},{8,9},{9,10},{10,1... | collective-permute-start | bytes 24584 | tf_op jit(solution)/shard_map/ppermute | solution.py:267
  33.2 3.7 %collective-permute-start.2 = (f32[8,256]{1,0:T(8,128)S(1)}, f32[8,256]{1,0:T(8,128)S(1)}, u32[]{:S(2)}, u32[]{:S(2)}) collective-permute-start(f32[8,256]{1,0:T(8,128)S(1)} %get-tuple-element.38.refs_0_), channel_id=1, source_target_pairs={{0,2},{1,3},{2,0},{3,1},{4,6},{5,7},{6,4},{7,5},{8,10},{9,11},{10,... | collective-permute-start | bytes 24584 | tf_op jit(solution)/shard_map/ppermute | solution.py:267
  33.4 3.5 %collective-permute-start.1 = (f32[8,256]{1,0:T(8,128)S(1)}, f32[8,256]{1,0:T(8,128)S(1)}, u32[]{:S(2)}, u32[]{:S(2)}) collective-permute-start(f32[8,256]{1,0:T(8,128)S(1)} %get-tuple-element.38.refs_0_), channel_id=1, source_target_pairs={{0,3},{1,0},{2,1},{3,2},{4,7},{5,4},{6,5},{7,6},{8,11},{9,8},{10,9... | collective-permute-start | bytes 24584 | tf_op jit(solution)/shard_map/ppermute | solution.py:267
  39.1 0.7 %copy-start.12 = (f32[128,384]{1,0:T(8,128)}, f32[128,384]{1,0:T(8,128)S(1)}, u32[]{:S(2)}) copy-start(f32[128,384]{1,0:T(8,128)S(1)} %get-tuple-element.52.refs_10_) | copy-start | bytes 589828
  39.8 0.7 %copy-start.15 = (f32[32,8,128]{2,1,0:T(8,128)}, f32[32,8,128]{2,1,0:T(8,128)S(1)}, u32[]{:S(2)}) copy-start(f32[32,8,128]{2,1,0:T(8,128)S(1)} %get-tuple-element.45) | copy-start | bytes 393220
  40.5 0.6 copy-start.18
  41.1 0.6 copy-start.20
  41.7 0.6 copy-start.25
  42.3 17.3 %copy-start.13 = (f32[128,384]{1,0:T(8,128)S(1)}, f32[128,384]{1,0:T(8,128)}, u32[]{:S(2)}) copy-start(f32[128,384]{1,0:T(8,128)} %copy-done.12) | copy-start | bytes 589828
  42.3 17.3 %copy-start.19 = (f32[16,384]{1,0:T(8,128)S(1)}, f32[16,384]{1,0:T(8,128)}, u32[]{:S(2)}) copy-start(f32[16,384]{1,0:T(8,128)} %copy-done.18) | copy-start | bytes 73732
  42.3 17.3 %copy-start.21 = (f32[8,128]{1,0:T(8,128)S(1)}, f32[8,128]{1,0:T(8,128)}, u32[]{:S(2)}) copy-start(f32[8,128]{1,0:T(8,128)} %copy-done.20) | copy-start | bytes 12292
  42.3 10.9 %all-to-all-start.1 = ((f32[32,8,128]{2,1,0:T(8,128)}), f32[32,8,128]{2,1,0:T(8,128)S(1)}, u32[]{:S(2)}, u32[]{:S(2)}) async-start(f32[32,8,128]{2,1,0:T(8,128)} %copy-done.15), calls=%async_computation.1 | async-start | bytes 262144 | tf_op jit(solution)/shard_map/all_to_all | solution.py:332
  45.0 12.6 %collective-permute-start.9 = (f32[8,384]{1,0:T(8,128)}, f32[8,384]{1,0:T(8,128)S(1)}, u32[]{:S(2)}, u32[]{:S(2)}) collective-permute-start(f32[8,384]{1,0:T(8,128)} %copy-done.25), channel_id=1, source_target_pairs={{0,28},{4,0},{8,4},{12,8},{16,12},{20,16},{24,20},{28,24},{1,29},{... | collective-permute-start | bytes 36872 | tf_op jit(solution)/shard_map/ppermute | solution.py:267
  53.2 1.0 %copy-start.3 = (bf16[1024,256]{1,0:T(8,128)(2,1)S(1)}, bf16[1024,256]{1,0:T(8,128)(2,1)}, u32[]{:S(2)}) copy-start(bf16[1024,256]{1,0:T(8,128)(2,1)} %copy-done.1) | copy-start | bytes 1572868
  55.7 3.1 %collective-permute-start.8 = (f32[8,256]{1,0:T(8,128)S(1)}, f32[8,256]{1,0:T(8,128)S(1)}, u32[]{:S(2)}, u32[]{:S(2)}) collective-permute-start(f32[8,256]{1,0:T(8,128)S(1)} %get-tuple-element.46.refs_0_), channel_id=1, source_target_pairs={{0,1},{1,2},{2,3},{3,0},{4,5},{5,6},{6,7},{7,4},{8,9},{9,10},{10,1... | collective-permute-start | bytes 24584 | tf_op jit(solution)/shard_map/ppermute | solution.py:267
  55.9 3.7 %collective-permute-start.7 = (f32[8,256]{1,0:T(8,128)S(1)}, f32[8,256]{1,0:T(8,128)S(1)}, u32[]{:S(2)}, u32[]{:S(2)}) collective-permute-start(f32[8,256]{1,0:T(8,128)S(1)} %get-tuple-element.46.refs_0_), channel_id=1, source_target_pairs={{0,2},{1,3},{2,0},{3,1},{4,6},{5,7},{6,4},{7,5},{8,10},{9,11},{10,... | collective-permute-start | bytes 24584 | tf_op jit(solution)/shard_map/ppermute | solution.py:267
  56.3 3.3 %collective-permute-start.6 = (f32[8,256]{1,0:T(8,128)S(1)}, f32[8,256]{1,0:T(8,128)S(1)}, u32[]{:S(2)}, u32[]{:S(2)}) collective-permute-start(f32[8,256]{1,0:T(8,128)S(1)} %get-tuple-element.46.refs_0_), channel_id=1, source_target_pairs={{0,3},{1,0},{2,1},{3,2},{4,7},{5,4},{6,5},{7,6},{8,11},{9,8},{10,9... | collective-permute-start | bytes 24584 | tf_op jit(solution)/shard_map/ppermute | solution.py:267

commit v2 on v1

v2 whole, which is shorter than its diff:
```python
import functools

import jax
import jax.numpy as jnp
from jax import lax
from jax.experimental import pallas as pl
from jax.experimental.pallas import tpu as pltpu
from jax.sharding import PartitionSpec as P

F32 = jnp.float32
BF16 = jnp.bfloat16
ROWS = 8
LANES = 128
SLOT = 32
GROUP = LANES // SLOT
VMEM_LIMIT = 24 << 20


def parts(x, count):
    out = []
    for _ in range(count):
        out.append(x.astype(BF16))
        x = x - out[-1].astype(F32)
    return out


def dot(a, b, transposed=False):
    dims = (((1,), (1 if transposed else 0,)), ((), ()))
    return lax.dot_general(a, b, dims, preferred_element_type=F32)


def moved(a, chosen, transposed=False):
    rows = a.shape[0]
    all_parts = dot(jnp.concatenate(parts(a, 3), axis=0), chosen, transposed)
    return all_parts[:rows] + all_parts[rows : 2 * rows] + all_parts[2 * rows :]


def moved_parts(high, low, chosen):
    both = dot(jnp.concatenate([high, low], axis=0), chosen)
    return both[: high.shape[0]] + both[high.shape[0] :]


def product(a, high, low, transposed=False):
    rows = a.shape[0]
    top, rest = parts(a, 2)
    both = dot(jnp.concatenate([top, rest], axis=0), high, transposed)
    return both[:rows] + both[rows:] + dot(top, low, transposed)


def chosen_columns(index, count):
    shape = (count, index.shape[1])
    rows = lax.broadcasted_iota(jnp.int32, shape, 0)
    return jnp.where(rows == index, 1.0, 0.0).astype(BF16)


def row_sum(x):
    return jnp.sum(x, axis=1, keepdims=True)


def padded(x, rows):
    return jnp.concatenate([x, jnp.zeros((rows - x.shape[0], x.shape[1]), x.dtype)], axis=0)


def fetched(pairs, sems):
    copies = [
        pltpu.make_async_copy(source, target, sems.at[i]) for i, (source, target) in enumerate(pairs)
    ]
    for copy in copies:
        copy.start()
    return copies


def pack_kernel(
    live_ref, place_ref, jump_hbm, scale_hbm, nbr_hbm, inverse_hbm, out_ref, half_ref, jump, scale, nbr, sems,
):
    cases, _, records = jump.shape
    copies = fetched(
        [
            (jump_hbm, jump),
            (scale_hbm, scale),
            (nbr_hbm, nbr),
            (half_of(place_ref[3], inverse_hbm), half_ref),
        ],
        sems,
    )
    for copy in copies:
        copy.wait()
    live = lax.broadcasted_iota(jnp.int32, (1, records), 1) < live_ref[0, 0]
    live = live.astype(F32)
    for case in range(cases):
        out_ref[case : case + 1] = jump[case] * live
    out_ref[cases : cases + 1] = scale[0] * live
    out_ref[cases + 1 : cases + 2] = nbr[0].astype(F32)


def unpacked(pack, cases):
    rows = lax.broadcasted_iota(jnp.int32, pack.shape, 0)
    residual = jnp.where(rows < cases, pack, 0.0)
    return residual, pack[cases : cases + 1], pack[cases + 1 : cases + 2].astype(jnp.int32)


def half_of(slab, inverse_hbm):
    rows = 2 * inverse_hbm.shape[1]
    first = jnp.minimum(slab // 2 * rows, inverse_hbm.shape[0] - rows)
    return inverse_hbm.at[pl.ds(pl.multiple_of(first, 8), rows)]


def prepare_kernel(
    cases, pack_ref, schur_hbm, coupling_hbm, own_hbm, corner_hbm,
    s_high, s_low, c_high, c_low, own_coupling, load_ref, index_ref, own_ref,
    schur, coupling, own, corner, sems,
):
    copies = fetched(
        [
            (own_hbm, own),
            (coupling_hbm, coupling),
            (corner_hbm, corner),
            (schur_hbm, schur),
        ],
        sems,
    )
    for copy in copies[:3]:
        copy.wait()
    held, iface = coupling.shape[2:]
    block = padded(coupling[0, 0], SLOT)
    c_high[...], c_low[...] = parts(block, 2)
    chosen = chosen_columns(own[0], iface)
    own_ref[...] = own[0]
    own_coupling[...] = moved_parts(c_high[...], c_low[...], chosen)[:held]
    residual, scale, _ = unpacked(pack_ref[...], cases)
    load_ref[...] = moved(residual * scale, chosen, True)
    lane = lax.broadcasted_iota(jnp.int32, (held, LANES), 1) % SLOT
    tiles = jnp.where(lane == lax.broadcasted_iota(jnp.int32, (held, LANES), 0), 1.0, 0.0)
    index = jnp.broadcast_to(corner[0].astype(F32), (ROWS, held))
    index_ref[...] = jnp.where(lane[:1] < held, moved(index, tiles.astype(BF16))[:1], -1.0)
    copies[3].wait()
    s_high[...], s_low[...] = parts(schur[0, 0], 2)


def forces(load, through, first, c_high, c_low, index_ref, cases, send_ref):
    high, low = [jnp.concatenate([c[...]] * GROUP, axis=0) for c in (c_high, c_low)]
    force = product(load, high, low, True)
    lane = lax.broadcasted_iota(jnp.int32, force.shape, 1) % SLOT
    row = lax.broadcasted_iota(jnp.int32, force.shape, 0)
    force = jnp.where(lane == SLOT - 2, first, force)
    force = jnp.where(lane == SLOT - 1, row_sum(load * through), force)
    force = jnp.where(row == cases, index_ref[...], force)
    send_ref[...] = jnp.broadcast_to(force[None], send_ref.shape)


def first_kernel(
    cases, left_ref, pack_ref, load_ref, own_coupling, index_ref,
    s_high, s_low, c_high, c_low, own_ref,
    send_ref, right_ref, back_ref,
):
    left_residual, left_scale, left_index = unpacked(left_ref[...], cases)
    chosen = chosen_columns(left_index, load_ref.shape[1])
    load = load_ref[...] - moved(left_residual * left_scale, chosen, True)
    through = product(load, s_high[...], s_low[...])
    residual, scale, _ = unpacked(pack_ref[...], cases)
    norm = row_sum(residual * residual * scale)
    forces(load, through, norm, c_high, c_low, index_ref, cases, send_ref)
    right_ref[:ROWS] = moved(through, chosen_columns(own_ref[...], load_ref.shape[1]))
    right_ref[ROWS:] = own_coupling[...]
    back_ref[:ROWS] = moved(through, chosen)
    held = own_coupling.shape[0]
    back_ref[ROWS:] = moved_parts(c_high[...], c_low[...], chosen)[:held]


def gathered_forces(cases, all_ref, corners, flip, sums_ref, total_ref):
    devices = all_ref.shape[0]
    chunk = min(devices, LANES // GROUP)
    lane = lax.broadcasted_iota(jnp.int32, (ROWS, LANES), 1) // SLOT
    row = lax.broadcasted_iota(jnp.int32, (ROWS, 1), 0)
    step = min(corners, 1024)

    def add(at):
        pieces = []
        sums = jnp.zeros((ROWS, LANES), F32)
        for group in range(chunk // GROUP):
            piece = all_ref[at + group * GROUP]
            sums = sums + piece
            for e in range(1, GROUP):
                other = all_ref[at + group * GROUP + e]
                sums = sums + other
                piece = jnp.where(lane == e, other, piece)
            pieces.append(piece)
        flat = jnp.concatenate(pieces, axis=1)
        index = flat[cases : cases + 1].astype(jnp.int32) ^ flip
        force = jnp.where(row < cases, flat, 0.0)
        total = [
            moved(force, chosen_columns(index - start, step), True)
            for start in range(0, corners, step)
        ]
        return sums, jnp.concatenate(total, axis=1)

    sums_ref[...], total_ref[...] = add(0)
    if devices > chunk:

        @pl.loop(1, devices // chunk)
        def _(i):
            sums, total = add(i * chunk)
            sums_ref[...] += sums
            total_ref[...] += total


def near_index(cases, place_ref, all_ref):
    lane = lax.broadcasted_iota(jnp.int32, (1, LANES), 1) // SLOT
    index = all_ref[place_ref[0], cases : cases + 1]
    for e in (1, 2):
        index = jnp.where(lane == e, all_ref[place_ref[e], cases : cases + 1], index)
    return index.astype(jnp.int32)


def coarse_kernel(cases, place_ref, all_ref, inverse_hbm, x_ref, total_ref, sums_ref, index_ref, inverse, sems):
    (copy,) = fetched([(inverse_hbm, inverse)], sems)
    gathered_forces(cases, all_ref, total_ref.shape[1], 0, sums_ref, total_ref)
    index_ref[...] = jnp.broadcast_to(near_index(cases, place_ref, all_ref), index_ref.shape)
    copy.wait()
    x_ref[...] = product(total_ref[...], *parts(inverse[...], 2))


def shared_coarse(cases, width, refs):
    place_ref, *pieces, total_ref, sums_ref, index_ref, whole = refs
    for m, piece in enumerate(pieces):
        base = lax.rem(place_ref[3] + m, len(pieces)) * width
        whole[:, pl.ds(pl.multiple_of(base, width), width)] = piece[...]
    return whole[...], total_ref[...], sums_ref[...], index_ref[:1]


def pair_kernel(
    cases, place_ref, all_ref, far_ref, inverse_hbm, _, x_ref, total_ref, sums_ref, index_ref, inverse, sems,
):
    width = inverse.shape[1]
    slab = place_ref[3]
    copies = fetched(
        [
            (
                inverse_hbm.at[pl.ds(pl.multiple_of((slab ^ j) * width, width), width)],
                inverse.at[pl.ds(j * width, width)],
            )
            for j in range(4)
        ],
        sems,
    )
    flip = slab * width
    gathered_forces(cases, all_ref, 4 * width, flip, sums_ref, total_ref)
    index = near_index(cases, place_ref, all_ref) ^ flip
    index_ref[...] = jnp.broadcast_to(index, index_ref.shape)
    total = total_ref[...]
    last = [
        far_ref[pl.ds(pl.multiple_of((slab % 2 ^ j) * width, width), width)] for j in range(2)
    ]
    third = product(total[:, 2 * width :], *parts(jnp.concatenate(last, axis=0), 2))
    for copy in copies:
        copy.wait()
    high, low = parts(inverse[...], 2)
    x_ref[:, :width] = product(total, high, low)
    x_ref[:, width : 2 * width] = jnp.zeros((ROWS, width), F32)
    across = product(total[:, :width], high[2 * width :], low[2 * width :], True)
    x_ref[:, 2 * width : 3 * width] = across[:, :width] + third
    x_ref[:, 3 * width :] = across[:, width:]


def paired_coarse(cases, width, refs):
    place_ref, x_ref, other_ref, total_ref, sums_ref, index_ref = refs
    other = [other_ref[:, (j ^ 1) * width : (j ^ 1) * width + width] for j in range(4)]
    solution = x_ref[...] + jnp.concatenate(other, axis=1)
    return solution, total_ref[...], sums_ref[...], index_ref[:1]


def column(x, lane):
    return x[:, lane : lane + 1]


def second_kernel(cases, coarse, given, *refs):
    (
        pack_ref, left_ref, right_ref, back_ref, from_left, from_right,
        s_high, s_low, c_high, c_low, corner_ref, own_ref,
        send_ref, out_ref, keep_ref, spread_ref, scalar_ref,
    ) = refs[given : given + 17]
    solution, total, sums, index = coarse(refs[:given] + refs[given + 17 :])
    picked = moved(solution, chosen_columns(index, solution.shape[1]))
    blank = jnp.zeros((SLOT - (right_ref.shape[0] - ROWS), right_ref.shape[1]), F32)
    none = jnp.zeros((SLOT, right_ref.shape[1]), F32)
    own = jnp.concatenate([none, right_ref[ROWS:], blank, -from_right[ROWS:], blank, none], axis=0)
    other = jnp.concatenate([from_left[ROWS:], blank, -back_ref[ROWS:], blank, none, none], axis=0)
    spread_ref[...] = own
    both = product(picked, *parts(jnp.concatenate([own, other], axis=1), 2))
    records = right_ref.shape[1]
    residual, scale, _ = unpacked(pack_ref[...], cases)
    left_residual, left_scale, left_index = unpacked(left_ref[...], cases)
    live = (scale > 0.0).astype(F32)
    left_live = (left_scale > 0.0).astype(F32)
    image = (right_ref[:ROWS] - from_right[:ROWS] + both[:, :records]) * live
    left_image = (from_left[:ROWS] - back_ref[:ROWS] + both[:, records:]) * left_live
    norm = column(sums, SLOT - 2)
    curvature = column(sums, SLOT - 1) + row_sum(total * solution)
    row = lax.broadcasted_iota(jnp.int32, (ROWS, 1), 0)
    alpha = jnp.where(row < cases, norm / curvature, 0.0)
    residual = residual - alpha * image
    left_residual = left_residual - alpha * left_image
    precon = scale * residual
    left_precon = left_scale * left_residual
    own_map = chosen_columns(own_ref[...], c_high.shape[1])
    left_map = chosen_columns(left_index, c_high.shape[1])
    load = moved(precon, own_map, True) - moved(left_precon, left_map, True)
    through = product(load, s_high[...], s_low[...])
    forces(load, through, row_sum(residual * precon), c_high, c_low, corner_ref, cases, send_ref)
    out_ref[...] = moved(through, left_map)
    keep_ref[:ROWS] = moved(through, own_map)
    keep_ref[ROWS:] = image
    lane = lax.broadcasted_iota(jnp.int32, scalar_ref.shape, 1)
    scalar_ref[...] = jnp.where(lane == 0, norm, alpha)


def last_kernel(cases, coarse, given, *refs):
    (
        pack_ref, from_right, keep_ref, spread_ref, scalar_ref, multipliers_ref, residual_ref,
    ) = refs[given : given + 7]
    solution, total, sums, index = coarse(refs[:given] + refs[given + 7 :])
    picked = moved(solution, chosen_columns(index, solution.shape[1]))
    residual, scale, _ = unpacked(pack_ref[...], cases)
    live = (scale > 0.0).astype(F32)
    spread = product(picked, *parts(spread_ref[...], 2))
    image = (keep_ref[:ROWS] - from_right[...] + spread) * live
    along = keep_ref[ROWS:]
    first_norm = column(scalar_ref[...], 0)
    first_alpha = column(scalar_ref[...], 1)
    norm = column(sums, SLOT - 2)
    curvature = column(sums, SLOT - 1) + row_sum(total * solution)
    ratio = norm / first_norm
    alpha = norm / (curvature - ratio * norm / first_alpha)
    direction = scale * residual
    multipliers = first_alpha * direction
    residual = residual - first_alpha * along
    direction = scale * residual + ratio * direction
    along = image + ratio * along
    multipliers = multipliers + alpha * direction
    residual = residual - alpha * along
    for case in range(cases):
        multipliers_ref[case] = multipliers[case : case + 1]
        residual_ref[case] = residual[case : case + 1]


VM = pl.BlockSpec(memory_space=pltpu.VMEM)
SM = pl.BlockSpec(memory_space=pltpu.SMEM)
HB = pl.BlockSpec(memory_space=pltpu.HBM)


def call(kernel, outs, given, specs, scratch=(), moved_bytes=None):
    specs = specs + [VM] * (len(given) - len(specs))
    given = [
        pltpu.with_memory_space_constraint(x, pltpu.HBM) if spec is HB else x
        for x, spec in zip(given, specs)
    ]
    return pl.pallas_call(
        kernel,
        out_shape=[jax.ShapeDtypeStruct(shape, kind) for shape, kind in outs],
        in_specs=specs,
        out_specs=[VM] * len(outs),
        scratch_shapes=list(scratch),
        cost_estimate=moved_bytes
        and pl.CostEstimate(flops=0, bytes_accessed=moved_bytes, transcendentals=0),
        compiler_params=pltpu.CompilerParams(vmem_limit_bytes=VMEM_LIMIT),
    )(*given)


def passed_along(value, axis, steps):
    count = lax.axis_size(axis)
    pairs = [(source, (source + steps) % count) for source in range(count)]
    return lax.ppermute(value, axis, pairs)


def exchanged(value, axis, bit):
    pairs = [(source, source ^ bit) for source in range(lax.axis_size(axis))]
    return lax.ppermute(value, axis, pairs)


def per_device(
    jump_data,
    lumped_scale,
    schur_inverse,
    coarse_coupling,
    corner_inverse,
    own_dof,
    nbr_dof,
    live_count,
    corner_index,
):
    cases, records = jump_data.shape[2:]
    held, iface = coarse_coupling.shape[2:]
    corners, width = corner_inverse.shape
    chain, slabs = lax.axis_size("sub"), lax.axis_size("crs")
    devices = chain * slabs
    here, slab = lax.axis_index("sub"), lax.axis_index("crs")
    place = jnp.stack(
        [
            (here + chain - 1) % chain * slabs + slab,
            here * slabs + slab,
            (here + 1) % chain * slabs + slab,
            slab,
        ]
    ).astype(jnp.int32)

    def buffers(*arrays):
        return [pltpu.VMEM(a.shape, a.dtype) for a in arrays] + [
            pltpu.SemaphoreType.DMA((len(arrays),))
        ]

    jump = jump_data.reshape(cases, 1, records)
    first = (jump, lumped_scale, nbr_dof)
    pack, half = call(
        pack_kernel,
        [((ROWS, records), F32), ((2 * width, width), F32)],
        (live_count, place, *first, corner_inverse),
        [SM, SM] + [HB] * 4,
        [*buffers(*first)[:-1], pltpu.SemaphoreType.DMA((4,))],
    )
    left = passed_along(pack, "sub", 1)
    fetched_here = (schur_inverse, coarse_coupling, own_dof, corner_index)
    s_high, s_low, c_high, c_low, own_coupling, load, index, own = call(
        functools.partial(prepare_kernel, cases),
        [
            ((iface, iface), BF16),
            ((iface, iface), BF16),
            ((SLOT, iface), BF16),
            ((SLOT, iface), BF16),
            ((held, records), F32),
            ((ROWS, iface), F32),
            ((1, LANES), F32),
            ((1, records), jnp.int32),
        ],
        (pack, *fetched_here),
        [VM] + [HB] * 4,
        buffers(*fetched_here),
        32 << 20,
    )
    is_paired = slabs == 4 and width & (width - 1) == 0
    if is_paired:
        far = exchanged(half, "crs", 2)
    send, right, back = call(
        functools.partial(first_kernel, cases),
        [
            ((devices, ROWS, LANES), F32),
            ((ROWS + held, records), F32),
            ((ROWS + held, records), F32),
        ],
        (left, pack, load, own_coupling, index, s_high, s_low, c_high, c_low, own),
        [],
    )

    def gathered(send, beside):
        everyone = lax.all_to_all(send, ("sub", "crs"), 0, 0)
        row = (ROWS, corners)
        outs = [(row, F32), ((ROWS, LANES), F32), ((ROWS, LANES), jnp.int32)]
        if is_paired:
            x, *others = call(
                functools.partial(pair_kernel, cases),
                [(row, F32), *outs],
                (place, everyone, far, corner_inverse, beside),
                [SM, VM, VM, HB, VM],
                [pltpu.VMEM((corners, width), F32), pltpu.SemaphoreType.DMA((4,))],
            )
            return (
                (place, x, exchanged(x, "crs", 1), *others),
                [SM] + [VM] * 5,
                [],
                functools.partial(paired_coarse, cases, width),
            )
        x, *others = call(
            functools.partial(coarse_kernel, cases),
            [((ROWS, width), F32), *outs],
            (place, everyone, corner_inverse),
            [SM, VM, HB],
            buffers(corner_inverse),
        )
        pieces = [x] + [passed_along(x, "crs", -m) for m in range(1, slabs)]
        return (
            (place, *pieces, *others),
            [SM] + [VM] * (len(pieces) + len(others)),
            [pltpu.VMEM(row, F32)],
            functools.partial(shared_coarse, cases, width),
        )

    from_left = passed_along(right, "sub", 1)
    from_right = passed_along(back, "sub", -1)
    given, specs, scratch, coarse = gathered(send, from_right)
    send, out, keep, spread, scalars = call(
        functools.partial(second_kernel, cases, coarse, len(given)),
        [
            ((devices, ROWS, LANES), F32),
            ((ROWS, records), F32),
            ((2 * ROWS, records), F32),
            ((LANES, records), F32),
            ((ROWS, LANES), F32),
        ],
        (
            *given, pack, left, right, back, from_left, from_right,
            s_high, s_low, c_high, c_low, index, own,
        ),
        specs,
        scratch,
    )
    from_right = passed_along(out, "sub", -1)
    given, specs, scratch, coarse = gathered(send, from_right)
    outs = call(
        functools.partial(last_kernel, cases, coarse, len(given)),
        [(jump.shape, F32), (jump.shape, F32)],
        (*given, pack, from_right, keep, spread, scalars),
        specs,
        scratch,
    )
    return tuple(out.reshape(jump_data.shape) for out in outs)


def solution(mesh):
    return jax.shard_map(
        per_device,
        mesh=mesh,
        in_specs=(
            P("sub", "crs", None, None),
            P("sub", "crs", None),
            P("sub", "crs", None, None),
            P("sub", "crs", None, None),
            P(None, "crs"),
            P("sub", "crs", None),
            P("sub", "crs", None),
            P("sub", "crs"),
            P("sub", "crs", None),
        ),
        out_specs=(P("sub", "crs", None, None), P("sub", "crs", None, None)),
        check_vma=False,
    )
```

time: 62.9 us -> 50.7 us (0.81); the launches traced: 61.7 us -> 50.3 us
  local copies, waits for them, and re-layouts: 15.2 us -> 0 us
  Pallas kernels: 8.99 us -> 15.6 us
  starting transfers between devices: 24.1 us -> 21.3 us
  waiting for transfers between devices: 11.2 us -> 12 us
  other arithmetic: 0.73 us -> 0.08 us
    unnamed x53 -> x0, local copies, waits for them, and re-layouts: 13.9 us -> none
    pallas_call x7, Pallas kernels: 8.99 us -> 15.6 us  [call(): pl.pallas_call(kernel, out_shape=[jax.ShapeDtypeStruct(shape, kind) for s...]
    ppermute x10 -> x4, starting transfers between devices: 16.4 us -> 10.7 us  [passed_along(): return lax.ppermute(value, axis, pairs)]
    ppermute x0 -> x3, starting transfers between devices: none -> 3.56 us  [exchanged(): return lax.ppermute(value, axis, pairs)]
    all_to_all x2, waiting for transfers between devices: 7 us -> 4.09 us  [gathered(): everyone = lax.all_to_all(send, ('sub', 'crs'), 0, 0)]
    ppermute x0 -> x3, waiting for transfers between devices: none -> 1.95 us  [exchanged(): return lax.ppermute(value, axis, pairs)]
    ppermute x10 -> x4, waiting for transfers between devices: 4.18 us -> 5.93 us  [passed_along(): return lax.ppermute(value, axis, pairs)]
    pallas_call x2 -> x0, local copies, waits for them, and re-layouts: 1.23 us -> none  [call(): pl.pallas_call(kernel, out_shape=[jax.ShapeDtypeStruct(shape, kind) for s...]
  transfers between devices with their start and end apart: 12 -> 9, of which waited for: 6 -> 7; matrix products, arithmetic and copies ran while one was open for 1% -> 0% of each run, Pallas kernels for 8% -> 13%
where the time goes in v2:
time: 50.7 us; the launch traced here: 50.3 us
  starting transfers between devices  21.3 us (42%)
  Pallas kernels  15.6 us (31%)
  waiting for transfers between devices  12 us (24%)
  between operations  1.36 us (3%)
    pallas_call x7, Pallas kernels, call(): pl.pallas_call(kernel, out_shape=[jax.ShapeDtypeStruct(shape, kind) for s...  15.6 us
    ppermute x4, starting transfers between devices, passed_along(): return lax.ppermute(value, axis, pairs)  10.7 us
    all_to_all x2, starting transfers between devices, gathered(): everyone = lax.all_to_all(send, ('sub', 'crs'), 0, 0)  7 us
    ppermute x4, waiting for transfers between devices, passed_along(): return lax.ppermute(value, axis, pairs)  5.93 us
    all_to_all x2, waiting for transfers between devices, gathered(): everyone = lax.all_to_all(send, ('sub', 'crs'), 0, 0)  4.09 us
    ppermute x3, starting transfers between devices, exchanged(): return lax.ppermute(value, axis, pairs)  3.56 us
    ppermute x3, waiting for transfers between devices, exchanged(): return lax.ppermute(value, axis, pairs)  1.95 us
  transfers between devices with their start and end apart: 9, of which 7 were waited for; matrix products, arithmetic and copies ran while one was open for 0% of the time, Pallas kernels for 13%

profile of v2, /device:TPU:0, one launch (start us, length us, event | category | flops | bytes accessed | tf_op | source)
XLA Modules:
  0.0 50.3 jit_solution(9479188059401695929)
XLA Ops:
  1.3 0.1 pad_add_fusion.place_ref.refs_0_
  1.4 2.5 %shard_map.104 = (f32[8,384]{1,0:T(8,128)S(1)}, f32[512,256]{1,0:T(8,128)}) custom-call(s32[1,1]{1,0:T(1,128)S(6)} %copy.13.live_ref, s32[4]{0:T(128)S(1)} %pad_add_fusion.place_ref.refs_0_, f32[6,1,384]{2,1,0:T(1,128)} %bitcast.11, f32[1,1,384]{2,1,0:T(1,128)} %scale_hbm.1, s32[1,1,384]{2,1,0:T(1,128)} %nbr_hbm.1, f32[1024,256]{1,0:T(8,128)} %inverse_hbm.5), custom_call_target="tpu_custom_call" | custom-call | tf_op jit(solution)/shard_map/pallas_call | solution.py:357
  3.8 3.0 %collective-permute-start.1 = (f32[512,256]{1,0:T(8,128)}, f32[512,256]{1,0:T(8,128)S(1)}, u32[]{:S(2)}, u32[]{:S(2)}) collective-permute-start(f32[512,256]{1,0:T(8,128)} %get-tuple-element.40), channel_id=1, source_target_pairs={{0,2},{1,3},{2,0},{3,1},{4,6},{5,7},{6,4},{7,5},{8,10},{9,11},{10,... | collective-permute-start | bytes 1572872 | tf_op jit(solution)/shard_map/ppermute | solution.py:377
  6.8 1.5 %collective-permute-start = (f32[8,384]{1,0:T(8,128)S(1)}, f32[8,384]{1,0:T(8,128)S(1)}, u32[]{:S(2)}, u32[]{:S(2)}) collective-permute-start(f32[8,384]{1,0:T(8,128)S(1)} %get-tuple-element.30.pack_ref.refs_6_), channel_id=1, source_target_pairs={{0,4},{4,8},{8,12},{12,16},{16,20},{20,24},{24,28},{28,0},{1,5},{5... | collective-permute-start | bytes 36872 | tf_op jit(solution)/shard_map/ppermute | solution.py:372
  8.4 2.1 %shard_map.105 = (bf16[768,768]{1,0:T(8,128)(2,1)S(1)}, bf16[768,768]{1,0:T(8,128)(2,1)S(1)}, bf16[32,768]{1,0:T(8,128)(2,1)S(1)}, bf16[32,768]{1,0:T(8,128)(2,1...) custom-call(f32[8,384]{1,0:T(8,128)S(1)} %get-tuple-element.30.pack_ref.refs_, ...), custom_call_target="tpu_custom_call" | custom-call | bytes 33554432 | tf_op jit(solution)/shard_map/pallas_call | solution.py:357
  10.5 2.7 %collective-permute-done.left_ref.refs_7_ = f32[8,384]{1,0:T(8,128)S(1)} collective-permute-done((f32[8,384]{1,0:T(8,128)S(1)}, f32[8,384]{1,0:T(8,128)S(1)}, u32[]{:S(2)}, u32[]{:S(2)}) %collective-permute-start) | collective-permute-done | bytes 12320 | tf_op jit(solution)/shard_map/ppermute | solution.py:372
  13.2 1.5 %shard_map.106 = (f32[32,8,128]{2,1,0:T(8,128)}, f32[32,384]{1,0:T(8,128)S(1)}, f32[32,384]{1,0:T(8,128)S(1)}) custom-call(f32[8,384]{1,0:T(8,128)S(1)} %collective-permute-done.left_ref.refs_7_, f32[8,384]{1,0:T(8,128)S(1)} %get-tuple-element.30.pack_ref.refs_6_, f32[8,768]{1,0:T(8,128)S(1)} %get-tuple-element.31.load_ref, ...), custom_call_target="tpu_custom_call" | custom-call | tf_op jit(solution)/shard_map/pallas_call | solution.py:357
  14.7 2.6 %all-to-all-start = ((f32[32,8,128]{2,1,0:T(8,128)}), f32[32,8,128]{2,1,0:T(8,128)S(1)}, u32[]{:S(2)}, u32[]{:S(2)}) async-start(f32[32,8,128]{2,1,0:T(8,128)} %get-tuple-element.39), calls=%async_computation | async-start | bytes 262144 | tf_op jit(solution)/shard_map/all_to_all | solution.py:454
  17.3 4.6 %collective-permute-start.2 = (f32[32,384]{1,0:T(8,128)S(1)}, f32[32,384]{1,0:T(8,128)S(1)}, u32[]{:S(2)}, u32[]{:S(2)}) collective-permute-start(f32[32,384]{1,0:T(8,128)S(1)} %get-tuple-element.41.refs_9_), channel_id=1, source_target_pairs={{0,28},{4,0},{8,4},{12,8},{16,12},{20,16},{24,20},{28,24},{1,29},{... | collective-permute-start | bytes 147464 | tf_op jit(solution)/shard_map/ppermute | solution.py:372
  21.9 0.0 collective-permute-start.4
  21.9 1.7 %collective-permute-done.2._.refs_11_ = f32[32,384]{1,0:T(8,128)S(1)} collective-permute-done((f32[32,384]{1,0:T(8,128)S(1)}, f32[32,384]{1,0:T(8,128)S(1)}, u32[]{:S(2)}, u32[]{:S(2)}) %collective-permute-start.2) | collective-permute-done | bytes 49184 | tf_op jit(solution)/shard_map/ppermute | solution.py:372
  23.6 1.9 %all-to-all-done.all_ref = f32[32,8,128]{2,1,0:T(8,128)S(1)} async-done(((f32[32,8,128]{2,1,0:T(8,128)}), f32[32,8,128]{2,1,0:T(8,128)S(1)}, u32[]{:S(2)}, u32[]{:S(2)}) %all-to-all-start) | async-done | bytes 131104 | tf_op jit(solution)/shard_map/all_to_all | solution.py:454
  25.5 0.0 collective-permute-done.1.far_ref
  25.5 2.8 %shard_map.107 = (f32[8,1024]{1,0:T(8,128)S(1)}, f32[8,1024]{1,0:T(8,128)S(1)}, f32[8,128]{1,0:T(8,128)S(1)}, s32[8,128]{1,0:T(8,128)S(1)}) custom-call(s32[4]{0:T(128)S(1)} %pad_add_fusion.place_ref.refs_0_, f32[32,8,128]{2,1,0:T(8,128)S(1)} %all-to-all-done.all_ref, f32[512,256]{1,0:T(8,128)S(1)} %collective-permute-done.1.far_ref, ...), custom_call_target="tpu_custom_call" | custom-call | tf_op jit(solution)/shard_map/pallas_call | solution.py:357
  28.3 0.3 collective-permute-start.3
  28.6 0.0 collective-permute-done.4.refs_10_
  28.7 1.0 %collective-permute-done.3.refs_2_ = f32[8,1024]{1,0:T(8,128)S(1)} collective-permute-done((f32[8,1024]{1,0:T(8,128)S(1)}, f32[8,1024]{1,0:T(8,128)S(1)}, u32[]{:S(2)}, u32[]{:S(2)}) %collective-permute-start.3) | collective-permute-done | bytes 32800 | tf_op jit(solution)/shard_map/ppermute | solution.py:377
  29.6 2.4 %shard_map.108 = (f32[32,8,128]{2,1,0:T(8,128)}, f32[8,384]{1,0:T(8,128)S(1)}, f32[16,384]{1,0:T(8,128)S(1)}, f32[128,384]{1,0:T(8,128)S(1)}, f32[8,128]{1,0:T(8,128)S(1)}) custom-call(s32[4]{0:T(128)S(1)} %pad_add_fusion.place_ref.refs_0_, f32[8,1024]{1,0:T(8,128)S(1)} %get-tuple-element.42.refs_1_, f32[8,1024]{1,0:T(8,128)S(1)} %collective-permute-done.3.refs_2_, ...), custom_call_target="tpu_custom_call" | custom-call | tf_op jit(solution)/shard_map/pallas_call | solution.py:357
  32.0 4.4 %all-to-all-start.1 = ((f32[32,8,128]{2,1,0:T(8,128)}), f32[32,8,128]{2,1,0:T(8,128)S(1)}, u32[]{:S(2)}, u32[]{:S(2)}) async-start(f32[32,8,128]{2,1,0:T(8,128)} %get-tuple-element.47), calls=%async_computation.1 | async-start | bytes 262144 | tf_op jit(solution)/shard_map/all_to_all | solution.py:454
  36.5 4.6 %collective-permute-start.5 = (f32[8,384]{1,0:T(8,128)S(1)}, f32[8,384]{1,0:T(8,128)S(1)}, u32[]{:S(2)}, u32[]{:S(2)}) collective-permute-start(f32[8,384]{1,0:T(8,128)S(1)} %get-tuple-element.48), channel_id=1, source_target_pairs={{0,28},{4,0},{8,4},{12,8},{16,12},{20,16},{24,20},{28,24},{1,29},{... | collective-permute-start | bytes 36872 | tf_op jit(solution)/shard_map/ppermute | solution.py:372
  41.1 1.4 %collective-permute-done.5._.refs_7_ = f32[8,384]{1,0:T(8,128)S(1)} collective-permute-done((f32[8,384]{1,0:T(8,128)S(1)}, f32[8,384]{1,0:T(8,128)S(1)}, u32[]{:S(2)}, u32[]{:S(2)}) %collective-permute-start.5) | collective-permute-done | bytes 12320 | tf_op jit(solution)/shard_map/ppermute | solution.py:372
  42.5 2.2 %all-to-all-done.1.all_ref = f32[32,8,128]{2,1,0:T(8,128)S(1)} async-done(((f32[32,8,128]{2,1,0:T(8,128)}), f32[32,8,128]{2,1,0:T(8,128)S(1)}, u32[]{:S(2)}, u32[]{:S(2)}) %all-to-all-start.1) | async-done | bytes 131104 | tf_op jit(solution)/shard_map/all_to_all | solution.py:454
  44.7 2.8 %shard_map.109 = (f32[8,1024]{1,0:T(8,128)S(1)}, f32[8,1024]{1,0:T(8,128)S(1)}, f32[8,128]{1,0:T(8,128)S(1)}, s32[8,128]{1,0:T(8,128)S(1)}) custom-call(s32[4]{0:T(128)S(1)} %pad_add_fusion.place_ref.refs_0_, f32[32,8,128]{2,1,0:T(8,128)S(1)} %all-to-all-done.1.all_ref, f32[512,256]{1,0:T(8,128)S(1)} %collective-permute-done.1.far_ref, ...), custom_call_target="tpu_custom_call" | custom-call | tf_op jit(solution)/shard_map/pallas_call | solution.py:357
  47.5 0.3 collective-permute-start.6
  47.8 1.0 %collective-permute-done.6.refs_2_ = f32[8,1024]{1,0:T(8,128)S(1)} collective-permute-done((f32[8,1024]{1,0:T(8,128)S(1)}, f32[8,1024]{1,0:T(8,128)S(1)}, u32[]{:S(2)}, u32[]{:S(2)}) %collective-permute-start.6) | collective-permute-done | bytes 32800 | tf_op jit(solution)/shard_map/ppermute | solution.py:377
  48.8 1.5 %shard_map.110 = (f32[6,1,384]{2,1,0:T(1,128)}, f32[6,1,384]{2,1,0:T(1,128)}) custom-call(s32[4]{0:T(128)S(1)} %pad_add_fusion.place_ref.refs_0_, f32[8,1024]{1,0:T(8,128)S(1)} %get-tuple-element.49.refs_1_, f32[8,1024]{1,0:T(8,128)S(1)} %collective-permute-done.6.refs_2_, f32[8,1024]{1,0:T(8,128)S(1)} %get-tuple-element.50.refs_3_, ...), custom_call_target="tpu_custom_call" | custom-call | tf_op jit(solution)/shard_map/pallas_call | solution.py:357
Async XLA Ops:
  3.8 21.7 %collective-permute-start.1 = (f32[512,256]{1,0:T(8,128)}, f32[512,256]{1,0:T(8,128)S(1)}, u32[]{:S(2)}, u32[]{:S(2)}) collective-permute-start(f32[512,256]{1,0:T(8,128)} %get-tuple-element.40), channel_id=1, source_target_pairs={{0,2},{1,3},{2,0},{3,1},{4,6},{5,7},{6,4},{7,5},{8,10},{9,11},{10,... | collective-permute-start | bytes 1572872 | tf_op jit(solution)/shard_map/ppermute | solution.py:377
  6.8 6.4 %collective-permute-start = (f32[8,384]{1,0:T(8,128)S(1)}, f32[8,384]{1,0:T(8,128)S(1)}, u32[]{:S(2)}, u32[]{:S(2)}) collective-permute-start(f32[8,384]{1,0:T(8,128)S(1)} %get-tuple-element.30.pack_ref.refs_6_), channel_id=1, source_target_pairs={{0,4},{4,8},{8,12},{12,16},{16,20},{20,24},{24,28},{28,0},{1,5},{5... | collective-permute-start | bytes 36872 | tf_op jit(solution)/shard_map/ppermute | solution.py:372
  14.7 10.8 %all-to-all-start = ((f32[32,8,128]{2,1,0:T(8,128)}), f32[32,8,128]{2,1,0:T(8,128)S(1)}, u32[]{:S(2)}, u32[]{:S(2)}) async-start(f32[32,8,128]{2,1,0:T(8,128)} %get-tuple-element.39), calls=%async_computation | async-start | bytes 262144 | tf_op jit(solution)/shard_map/all_to_all | solution.py:454
  17.3 6.4 %collective-permute-start.2 = (f32[32,384]{1,0:T(8,128)S(1)}, f32[32,384]{1,0:T(8,128)S(1)}, u32[]{:S(2)}, u32[]{:S(2)}) collective-permute-start(f32[32,384]{1,0:T(8,128)S(1)} %get-tuple-element.41.refs_9_), channel_id=1, source_target_pairs={{0,28},{4,0},{8,4},{12,8},{16,12},{20,16},{24,20},{28,24},{1,29},{... | collective-permute-start | bytes 147464 | tf_op jit(solution)/shard_map/ppermute | solution.py:372
  21.9 6.8 %collective-permute-start.4 = (f32[32,384]{1,0:T(8,128)S(1)}, f32[32,384]{1,0:T(8,128)S(1)}, u32[]{:S(2)}, u32[]{:S(2)}) collective-permute-start(f32[32,384]{1,0:T(8,128)S(1)} %get-tuple-element.46.refs_8_), channel_id=1, source_target_pairs={{0,4},{4,8},{8,12},{12,16},{16,20},{20,24},{24,28},{28,0},{1,5},{5... | collective-permute-start | bytes 147464 | tf_op jit(solution)/shard_map/ppermute | solution.py:372
  28.3 1.3 %collective-permute-start.3 = (f32[8,1024]{1,0:T(8,128)S(1)}, f32[8,1024]{1,0:T(8,128)S(1)}, u32[]{:S(2)}, u32[]{:S(2)}) collective-permute-start(f32[8,1024]{1,0:T(8,128)S(1)} %get-tuple-element.42.refs_1_), channel_id=1, source_target_pairs={{0,1},{1,0},{2,3},{3,2},{4,5},{5,4},{6,7},{7,6},{8,9},{9,8},{10,11... | collective-permute-start | bytes 98312 | tf_op jit(solution)/shard_map/ppermute | solution.py:377
  32.0 12.7 %all-to-all-start.1 = ((f32[32,8,128]{2,1,0:T(8,128)}), f32[32,8,128]{2,1,0:T(8,128)S(1)}, u32[]{:S(2)}, u32[]{:S(2)}) async-start(f32[32,8,128]{2,1,0:T(8,128)} %get-tuple-element.47), calls=%async_computation.1 | async-start | bytes 262144 | tf_op jit(solution)/shard_map/all_to_all | solution.py:454
  36.5 6.0 %collective-permute-start.5 = (f32[8,384]{1,0:T(8,128)S(1)}, f32[8,384]{1,0:T(8,128)S(1)}, u32[]{:S(2)}, u32[]{:S(2)}) collective-permute-start(f32[8,384]{1,0:T(8,128)S(1)} %get-tuple-element.48), channel_id=1, source_target_pairs={{0,28},{4,0},{8,4},{12,8},{16,12},{20,16},{24,20},{28,24},{1,29},{... | collective-permute-start | bytes 36872 | tf_op jit(solution)/shard_map/ppermute | solution.py:372
  47.5 1.3 %collective-permute-start.6 = (f32[8,1024]{1,0:T(8,128)S(1)}, f32[8,1024]{1,0:T(8,128)S(1)}, u32[]{:S(2)}, u32[]{:S(2)}) collective-permute-start(f32[8,1024]{1,0:T(8,128)S(1)} %get-tuple-element.49.refs_1_), channel_id=1, source_target_pairs={{0,1},{1,0},{2,3},{3,2},{4,5},{5,4},{6,7},{7,6},{8,9},{9,8},{10,11... | collective-permute-start | bytes 98312 | tf_op jit(solution)/shard_map/ppermute | solution.py:377

commit v3 on v2

--- a/solution.py
+++ b/solution.py
@@ -71,7 +71,7 @@
 
 
 def pack_kernel(
-    live_ref, place_ref, jump_hbm, scale_hbm, nbr_hbm, inverse_hbm, out_ref, half_ref, jump, scale, nbr, sems,
+    live_ref, jump_hbm, scale_hbm, nbr_hbm, inverse_hbm, out_ref, half_ref, jump, scale, nbr, sems,
 ):
     cases, _, records = jump.shape
     copies = fetched(
@@ -79,7 +79,7 @@
             (jump_hbm, jump),
             (scale_hbm, scale),
             (nbr_hbm, nbr),
-            (half_of(place_ref[3], inverse_hbm), half_ref),
+            (half_of(lax.axis_index("crs"), inverse_hbm), half_ref),
         ],
         sems,
     )
@@ -99,6 +99,20 @@
     return residual, pack[cases : cases + 1], pack[cases + 1 : cases + 2].astype(jnp.int32)
 
 
+def near_devices():
+    chain, slabs = lax.axis_size("sub"), lax.axis_size("crs")
+    here, slab = lax.axis_index("sub"), lax.axis_index("crs")
+    return [lax.rem(here + step, chain) * slabs + slab for step in (chain - 1, 0, 1)]
+
+
+def is_paired(width):
+    return lax.axis_size("crs") == 4 and width & (width - 1) == 0
+
+
+def block_at(slab, j, width):
+    return slab ^ j if is_paired(width) else j
+
+
 def half_of(slab, inverse_hbm):
     rows = 2 * inverse_hbm.shape[1]
     first = jnp.minimum(slab // 2 * rows, inverse_hbm.shape[0] - rows)
@@ -106,15 +120,16 @@
 
 
 def prepare_kernel(
-    cases, pack_ref, schur_hbm, coupling_hbm, own_hbm, corner_hbm,
-    s_high, s_low, c_high, c_low, own_coupling, load_ref, index_ref, own_ref,
-    schur, coupling, own, corner, sems,
+    cases, pack_ref, schur_hbm, coupling_hbm, own_hbm, corner_hbm, inverse_hbm,
+    s_high, s_low, c_high, c_low, own_coupling, load_ref, index_ref, own_ref, inv_high, inv_low,
+    schur, coupling, own, corner, inverse, sems,
 ):
     copies = fetched(
         [
             (own_hbm, own),
             (coupling_hbm, coupling),
             (corner_hbm, corner),
+            (inverse_hbm, inverse),
             (schur_hbm, schur),
         ],
         sems,
@@ -134,6 +149,15 @@
     index = jnp.broadcast_to(corner[0].astype(F32), (ROWS, held))
     index_ref[...] = jnp.where(lane[:1] < held, moved(index, tiles.astype(BF16))[:1], -1.0)
     copies[3].wait()
+    slab = lax.axis_index("crs")
+    blocks = lax.axis_size("crs")
+    width = inverse.shape[1]
+    for j in range(blocks):
+        rows = pl.ds(pl.multiple_of(block_at(slab, j, width) * width, width), width)
+        high, low = parts(inverse[rows], 2)
+        inv_high[j * width : (j + 1) * width] = high
+        inv_low[j * width : (j + 1) * width] = low
+    copies[4].wait()
     s_high[...], s_low[...] = parts(schur[0, 0], 2)
 
 
@@ -204,66 +228,55 @@
             total_ref[...] += total
 
 
-def near_index(cases, place_ref, all_ref):
+def near_index(cases, all_ref):
     lane = lax.broadcasted_iota(jnp.int32, (1, LANES), 1) // SLOT
-    index = all_ref[place_ref[0], cases : cases + 1]
-    for e in (1, 2):
-        index = jnp.where(lane == e, all_ref[place_ref[e], cases : cases + 1], index)
+    left, *others = near_devices()
+    index = all_ref[left, cases : cases + 1]
+    for e, device in enumerate(others, 1):
+        index = jnp.where(lane == e, all_ref[device, cases : cases + 1], index)
     return index.astype(jnp.int32)
 
 
-def coarse_kernel(cases, place_ref, all_ref, inverse_hbm, x_ref, total_ref, sums_ref, index_ref, inverse, sems):
-    (copy,) = fetched([(inverse_hbm, inverse)], sems)
+def coarse_kernel(cases, all_ref, inv_high, inv_low, x_ref, total_ref, sums_ref, index_ref):
     gathered_forces(cases, all_ref, total_ref.shape[1], 0, sums_ref, total_ref)
-    index_ref[...] = jnp.broadcast_to(near_index(cases, place_ref, all_ref), index_ref.shape)
-    copy.wait()
-    x_ref[...] = product(total_ref[...], *parts(inverse[...], 2))
+    index_ref[...] = jnp.broadcast_to(near_index(cases, all_ref), index_ref.shape)
+    x_ref[...] = product(total_ref[...], inv_high[...], inv_low[...])
 
 
 def shared_coarse(cases, width, refs):
-    place_ref, *pieces, total_ref, sums_ref, index_ref, whole = refs
+    *pieces, total_ref, sums_ref, index_ref, whole = refs
     for m, piece in enumerate(pieces):
-        base = lax.rem(place_ref[3] + m, len(pieces)) * width
+        base = lax.rem(lax.axis_index("crs") + m, len(pieces)) * width
         whole[:, pl.ds(pl.multiple_of(base, width), width)] = piece[...]
     return whole[...], total_ref[...], sums_ref[...], index_ref[:1]
 
 
 def pair_kernel(
-    cases, place_ref, all_ref, far_ref, inverse_hbm, _, x_ref, total_ref, sums_ref, index_ref, inverse, sems,
+    cases, all_ref, far_ref, inv_high, inv_low, _, schur_hbm, x_ref, total_ref, sums_ref, index_ref, *later,
 ):
-    width = inverse.shape[1]
-    slab = place_ref[3]
-    copies = fetched(
-        [
-            (
-                inverse_hbm.at[pl.ds(pl.multiple_of((slab ^ j) * width, width), width)],
-                inverse.at[pl.ds(j * width, width)],
-            )
-            for j in range(4)
-        ],
-        sems,
-    )
+    copies = fetched([(schur_hbm, later[0])], later[1]) if later else []
+    width = inv_high.shape[1]
+    slab = lax.axis_index("crs")
     flip = slab * width
     gathered_forces(cases, all_ref, 4 * width, flip, sums_ref, total_ref)
-    index = near_index(cases, place_ref, all_ref) ^ flip
+    index = near_index(cases, all_ref) ^ flip
     index_ref[...] = jnp.broadcast_to(index, index_ref.shape)
     total = total_ref[...]
     last = [
         far_ref[pl.ds(pl.multiple_of((slab % 2 ^ j) * width, width), width)] for j in range(2)
     ]
     third = product(total[:, 2 * width :], *parts(jnp.concatenate(last, axis=0), 2))
+    x_ref[:, :width] = product(total, inv_high[...], inv_low[...])
+    x_ref[:, width : 2 * width] = jnp.zeros((ROWS, width), F32)
+    across = product(total[:, :width], inv_high[2 * width :], inv_low[2 * width :], True)
+    x_ref[:, 2 * width : 3 * width] = across[:, :width] + third
+    x_ref[:, 3 * width :] = across[:, width:]
     for copy in copies:
         copy.wait()
-    high, low = parts(inverse[...], 2)
-    x_ref[:, :width] = product(total, high, low)
-    x_ref[:, width : 2 * width] = jnp.zeros((ROWS, width), F32)
-    across = product(total[:, :width], high[2 * width :], low[2 * width :], True)
-    x_ref[:, 2 * width : 3 * width] = across[:, :width] + third
-    x_ref[:, 3 * width :] = across[:, width:]
 
 
 def paired_coarse(cases, width, refs):
-    place_ref, x_ref, other_ref, total_ref, sums_ref, index_ref = refs
+    x_ref, other_ref, total_ref, sums_ref, index_ref = refs
     other = [other_ref[:, (j ^ 1) * width : (j ^ 1) * width + width] for j in range(4)]
     solution = x_ref[...] + jnp.concatenate(other, axis=1)
     return solution, total_ref[...], sums_ref[...], index_ref[:1]
@@ -276,10 +289,10 @@
 def second_kernel(cases, coarse, given, *refs):
     (
         pack_ref, left_ref, right_ref, back_ref, from_left, from_right,
-        s_high, s_low, c_high, c_low, corner_ref, own_ref,
+        schur_ref, c_high, c_low, corner_ref, own_ref,
         send_ref, out_ref, keep_ref, spread_ref, scalar_ref,
-    ) = refs[given : given + 17]
-    solution, total, sums, index = coarse(refs[:given] + refs[given + 17 :])
+    ) = refs[given : given + 16]
+    solution, total, sums, index = coarse(refs[:given] + refs[given + 16 :])
     picked = moved(solution, chosen_columns(index, solution.shape[1]))
     blank = jnp.zeros((SLOT - (right_ref.shape[0] - ROWS), right_ref.shape[1]), F32)
     none = jnp.zeros((SLOT, right_ref.shape[1]), F32)
@@ -305,7 +318,7 @@
     own_map = chosen_columns(own_ref[...], c_high.shape[1])
     left_map = chosen_columns(left_index, c_high.shape[1])
     load = moved(precon, own_map, True) - moved(left_precon, left_map, True)
-    through = product(load, s_high[...], s_low[...])
+    through = product(load, *parts(schur_ref[0, 0], 2))
     forces(load, through, row_sum(residual * precon), c_high, c_low, corner_ref, cases, send_ref)
     out_ref[...] = moved(through, left_map)
     keep_ref[:ROWS] = moved(through, own_map)
@@ -393,15 +406,6 @@
     corners, width = corner_inverse.shape
     chain, slabs = lax.axis_size("sub"), lax.axis_size("crs")
     devices = chain * slabs
-    here, slab = lax.axis_index("sub"), lax.axis_index("crs")
-    place = jnp.stack(
-        [
-            (here + chain - 1) % chain * slabs + slab,
-            here * slabs + slab,
-            (here + 1) % chain * slabs + slab,
-            slab,
-        ]
-    ).astype(jnp.int32)
 
     def buffers(*arrays):
         return [pltpu.VMEM(a.shape, a.dtype) for a in arrays] + [
@@ -413,13 +417,13 @@
     pack, half = call(
         pack_kernel,
         [((ROWS, records), F32), ((2 * width, width), F32)],
-        (live_count, place, *first, corner_inverse),
-        [SM, SM] + [HB] * 4,
+        (live_count, *first, corner_inverse),
+        [SM] + [HB] * 4,
         [*buffers(*first)[:-1], pltpu.SemaphoreType.DMA((4,))],
     )
     left = passed_along(pack, "sub", 1)
-    fetched_here = (schur_inverse, coarse_coupling, own_dof, corner_index)
-    s_high, s_low, c_high, c_low, own_coupling, load, index, own = call(
+    fetched_here = (schur_inverse, coarse_coupling, own_dof, corner_index, corner_inverse)
+    s_high, s_low, c_high, c_low, own_coupling, load, index, own, inv_high, inv_low = call(
         functools.partial(prepare_kernel, cases),
         [
             ((iface, iface), BF16),
@@ -430,14 +434,15 @@
             ((ROWS, iface), F32),
             ((1, LANES), F32),
             ((1, records), jnp.int32),
+            ((corners, width), BF16),
+            ((corners, width), BF16),
         ],
         (pack, *fetched_here),
-        [VM] + [HB] * 4,
+        [VM] + [HB] * 5,
         buffers(*fetched_here),
         32 << 20,
     )
-    is_paired = slabs == 4 and width & (width - 1) == 0
-    if is_paired:
+    if is_paired(width):
         far = exchanged(half, "crs", 2)
     send, right, back = call(
         functools.partial(first_kernel, cases),
@@ -450,42 +455,43 @@
         [],
     )
 
-    def gathered(send, beside):
+    def gathered(send, beside, *later):
         everyone = lax.all_to_all(send, ("sub", "crs"), 0, 0)
         row = (ROWS, corners)
         outs = [(row, F32), ((ROWS, LANES), F32), ((ROWS, LANES), jnp.int32)]
-        if is_paired:
-            x, *others = call(
+        if is_paired(width):
+            x, total, sums, near, *fetched = call(
                 functools.partial(pair_kernel, cases),
-                [(row, F32), *outs],
-                (place, everyone, far, corner_inverse, beside),
-                [SM, VM, VM, HB, VM],
-                [pltpu.VMEM((corners, width), F32), pltpu.SemaphoreType.DMA((4,))],
+                [(row, F32), *outs, *((v.shape, v.dtype) for v in later)],
+                (everyone, far, inv_high, inv_low, beside, schur_inverse),
+                [VM] * 5 + [HB],
+                [pltpu.SemaphoreType.DMA((1,)) for _ in later],
             )
             return (
-                (place, x, exchanged(x, "crs", 1), *others),
-                [SM] + [VM] * 5,
+                (x, exchanged(x, "crs", 1), total, sums, near),
+                [VM] * 5,
                 [],
                 functools.partial(paired_coarse, cases, width),
+                *fetched,
             )
         x, *others = call(
             functools.partial(coarse_kernel, cases),
             [((ROWS, width), F32), *outs],
-            (place, everyone, corner_inverse),
-            [SM, VM, HB],
-            buffers(corner_inverse),
+            (everyone, inv_high, inv_low),
+            [],
         )
         pieces = [x] + [passed_along(x, "crs", -m) for m in range(1, slabs)]
         return (
-            (place, *pieces, *others),
-            [SM] + [VM] * (len(pieces) + len(others)),
+            (*pieces, *others),
+            [VM] * (len(pieces) + len(others)),
             [pltpu.VMEM(row, F32)],
             functools.partial(shared_coarse, cases, width),
+            *later,
         )
 
     from_left = passed_along(right, "sub", 1)
     from_right = passed_along(back, "sub", -1)
-    given, specs, scratch, coarse = gathered(send, from_right)
+    given, specs, scratch, coarse, schur = gathered(send, from_right, schur_inverse)
     send, out, keep, spread, scalars = call(
         functools.partial(second_kernel, cases, coarse, len(given)),
         [
@@ -497,7 +503,7 @@
         ],
         (
             *given, pack, left, right, back, from_left, from_right,
-            s_high, s_low, c_high, c_low, index, own,
+            schur, c_high, c_low, index, own,
         ),
         specs,
         scratch,

time: 50.7 us -> 45.3 us (0.89)
  Pallas kernels: 15.6 us -> 10.7 us
    pallas_call x7, Pallas kernels: 15.6 us -> 10.7 us  [call(): pl.pallas_call(kernel, out_shape=[jax.ShapeDtypeStruct(shape, kind) for s...]
    ppermute x3, waiting for transfers between devices: 1.95 us -> 1 us  [exchanged(): return lax.ppermute(value, axis, pairs)]
    ppermute x4, waiting for transfers between devices: 5.93 us -> 6.75 us  [passed_along(): return lax.ppermute(value, axis, pairs)]
  transfers between devices with their start and end apart: 9 -> 9, of which waited for: 7 -> 7; matrix products, arithmetic and copies ran while one was open for 0% -> 0% of each run, Pallas kernels for 13% -> 12%
where the time goes in v3:
time: 45.3 us; the launch traced here: 45 us
  starting transfers between devices  21.1 us (47%)
  waiting for transfers between devices  11.8 us (26%)
  Pallas kernels  10.7 us (24%)
  between operations  1.33 us (3%)
    pallas_call x7, Pallas kernels, call(): pl.pallas_call(kernel, out_shape=[jax.ShapeDtypeStruct(shape, kind) for s...  10.7 us
    ppermute x4, starting transfers between devices, passed_along(): return lax.ppermute(value, axis, pairs)  10.7 us
    all_to_all x2, starting transfers between devices, gathered(): everyone = lax.all_to_all(send, ('sub', 'crs'), 0, 0)  6.83 us
    ppermute x4, waiting for transfers between devices, passed_along(): return lax.ppermute(value, axis, pairs)  6.75 us
    all_to_all x2, waiting for transfers between devices, gathered(): everyone = lax.all_to_all(send, ('sub', 'crs'), 0, 0)  4.09 us
    ppermute x3, starting transfers between devices, exchanged(): return lax.ppermute(value, axis, pairs)  3.53 us
    ppermute x3, waiting for transfers between devices, exchanged(): return lax.ppermute(value, axis, pairs)  1 us
  transfers between devices with their start and end apart: 9, of which 7 were waited for; matrix products, arithmetic and copies ran while one was open for 0% of the time, Pallas kernels for 12%

profile of v3, /device:TPU:0, one launch (start us, length us, event | category | flops | bytes accessed | tf_op | source)
XLA Modules:
  0.0 45.0 jit_solution(6697664524869897000)
XLA Ops:
  1.3 1.1 %shard_map.104 = (f32[8,384]{1,0:T(8,128)S(1)}, f32[512,256]{1,0:T(8,128)S(1)}) custom-call(s32[1,1]{1,0:T(1,128)S(6)} %copy.13.live_ref, f32[6,1,384]{2,1,0:T(1,128)} %bitcast.7, f32[1,1,384]{2,1,0:T(1,128)} %scale_hbm.1, s32[1,1,384]{2,1,0:T(1,128)} %nbr_hbm.1, f32[1024,256]{1,0:T(8,128)} %inverse_hbm.3), custom_call_target="tpu_custom_call" | custom-call | tf_op jit(solution)/shard_map/pallas_call | solution.py:370
  2.4 3.0 %collective-permute-start.1 = (f32[512,256]{1,0:T(8,128)S(1)}, f32[512,256]{1,0:T(8,128)S(1)}, u32[]{:S(2)}, u32[]{:S(2)}) collective-permute-start(f32[512,256]{1,0:T(8,128)S(1)} %get-tuple-element.43), channel_id=1, source_target_pairs={{0,2},{1,3},{2,0},{3,1},{4,6},{5,7},{6,4},{7,5},{8,10},{9,11},{10,... | collective-permute-start | bytes 1572872 | tf_op jit(solution)/shard_map/ppermute | solution.py:390
  5.4 1.5 %collective-permute-start = (f32[8,384]{1,0:T(8,128)S(1)}, f32[8,384]{1,0:T(8,128)S(1)}, u32[]{:S(2)}, u32[]{:S(2)}) collective-permute-start(f32[8,384]{1,0:T(8,128)S(1)} %get-tuple-element.33.pack_ref.refs_5_), channel_id=1, source_target_pairs={{0,4},{4,8},{8,12},{12,16},{16,20},{20,24},{24,28},{28,0},{1,5},{5... | collective-permute-start | bytes 36872 | tf_op jit(solution)/shard_map/ppermute | solution.py:385
  6.9 2.4 %shard_map.105 = (bf16[768,768]{1,0:T(8,128)(2,1)S(1)}, bf16[768,768]{1,0:T(8,128)(2,1)S(1)}, bf16[32,768]{1,0:T(8,128)(2,1)S(1)}, bf16[32,768]{1,0:T(8,128)(2,1...) custom-call(f32[8,384]{1,0:T(8,128)S(1)} %get-tuple-element.33.pack_, ...), custom_call_target="tpu_custom_call" | custom-call | bytes 33554432 | tf_op jit(solution)/shard_map/pallas_call | solution.py:370
  9.4 2.4 %collective-permute-done.left_ref.refs_6_ = f32[8,384]{1,0:T(8,128)S(1)} collective-permute-done((f32[8,384]{1,0:T(8,128)S(1)}, f32[8,384]{1,0:T(8,128)S(1)}, u32[]{:S(2)}, u32[]{:S(2)}) %collective-permute-start) | collective-permute-done | bytes 12320 | tf_op jit(solution)/shard_map/ppermute | solution.py:385
  11.8 1.5 %shard_map.106 = (f32[32,8,128]{2,1,0:T(8,128)}, f32[32,384]{1,0:T(8,128)S(1)}, f32[32,384]{1,0:T(8,128)S(1)}) custom-call(f32[8,384]{1,0:T(8,128)S(1)} %collective-permute-done.left_ref.refs_6_, f32[8,384]{1,0:T(8,128)S(1)} %get-tuple-element.33.pack_ref.refs_5_, f32[8,768]{1,0:T(8,128)S(1)} %get-tuple-element.34.load_ref, ...), custom_call_target="tpu_custom_call" | custom-call | tf_op jit(solution)/shard_map/pallas_call | solution.py:370
  13.3 2.6 %all-to-all-start = ((f32[32,8,128]{2,1,0:T(8,128)}), f32[32,8,128]{2,1,0:T(8,128)S(1)}, u32[]{:S(2)}, u32[]{:S(2)}) async-start(f32[32,8,128]{2,1,0:T(8,128)} %get-tuple-element.42), calls=%async_computation | async-start | bytes 262144 | tf_op jit(solution)/shard_map/all_to_all | solution.py:459
  15.9 4.6 %collective-permute-start.2 = (f32[32,384]{1,0:T(8,128)S(1)}, f32[32,384]{1,0:T(8,128)S(1)}, u32[]{:S(2)}, u32[]{:S(2)}) collective-permute-start(f32[32,384]{1,0:T(8,128)S(1)} %get-tuple-element.46.refs_8_), channel_id=1, source_target_pairs={{0,28},{4,0},{8,4},{12,8},{16,12},{20,16},{24,20},{28,24},{1,29},{... | collective-permute-start | bytes 147464 | tf_op jit(solution)/shard_map/ppermute | solution.py:385
  20.5 0.0 collective-permute-start.4
  20.5 1.7 %collective-permute-done.2._.refs_10_ = f32[32,384]{1,0:T(8,128)S(1)} collective-permute-done((f32[32,384]{1,0:T(8,128)S(1)}, f32[32,384]{1,0:T(8,128)S(1)}, u32[]{:S(2)}, u32[]{:S(2)}) %collective-permute-start.2) | collective-permute-done | bytes 49184 | tf_op jit(solution)/shard_map/ppermute | solution.py:385
  22.2 1.9 %all-to-all-done.all_ref = f32[32,8,128]{2,1,0:T(8,128)S(1)} async-done(((f32[32,8,128]{2,1,0:T(8,128)}), f32[32,8,128]{2,1,0:T(8,128)S(1)}, u32[]{:S(2)}, u32[]{:S(2)}) %all-to-all-start) | async-done | bytes 131104 | tf_op jit(solution)/shard_map/all_to_all | solution.py:459
  24.1 0.0 collective-permute-done.1.far_ref
  24.1 1.7 %shard_map.107 = (f32[8,1024]{1,0:T(8,128)S(1)}, f32[8,1024]{1,0:T(8,128)S(1)}, f32[8,128]{1,0:T(8,128)S(1)}, s32[8,128]{1,0:T(8,128)S(1)}, f32[1,1,768,768]{3,2,1,0:T(8,128)S(1)}) custom-call(f32[32,8,128]{2,1,0:T(8,128)S(1)} %all-to-all-done.all_ref, f32[512,256]{1,0:T(8,128)S(1)} %collective-permute-done.1.far_ref, ...), custom_call_target="tpu_custom_call" | custom-call | tf_op jit(solution)/shard_map/pallas_call | solution.py:370
  25.8 0.3 collective-permute-start.3
  26.1 1.2 %collective-permute-done.4.refs_9_ = f32[32,384]{1,0:T(8,128)S(1)} collective-permute-done((f32[32,384]{1,0:T(8,128)S(1)}, f32[32,384]{1,0:T(8,128)S(1)}, u32[]{:S(2)}, u32[]{:S(2)}) %collective-permute-start.4) | collective-permute-done | bytes 49184 | tf_op jit(solution)/shard_map/ppermute | solution.py:385
  27.3 0.0 collective-permute-done.3.refs_1_
  27.3 1.9 %shard_map.108 = (f32[32,8,128]{2,1,0:T(8,128)}, f32[8,384]{1,0:T(8,128)S(1)}, f32[16,384]{1,0:T(8,128)S(1)}, f32[128,384]{1,0:T(8,128)S(1)}, f32[8,128]{1,0:T(8,128)S(1)}) custom-call(f32[8,1024]{1,0:T(8,128)S(1)} %get-tuple-element.47.refs_0_, f32[8,1024]{1,0:T(8,128)S(1)} %collective-permute-done.3.refs_1_, f32[8,1024]{1,0:T(8,128)S(1)} %get-tuple-element.48.refs_2_, ...), custom_call_target="tpu_custom_call" | custom-call | tf_op jit(solution)/shard_map/pallas_call | solution.py:370
  29.2 4.3 %all-to-all-start.1 = ((f32[32,8,128]{2,1,0:T(8,128)}), f32[32,8,128]{2,1,0:T(8,128)S(1)}, u32[]{:S(2)}, u32[]{:S(2)}) async-start(f32[32,8,128]{2,1,0:T(8,128)} %get-tuple-element.53), calls=%async_computation.1 | async-start | bytes 262144 | tf_op jit(solution)/shard_map/all_to_all | solution.py:459
  33.5 4.6 %collective-permute-start.5 = (f32[8,384]{1,0:T(8,128)S(1)}, f32[8,384]{1,0:T(8,128)S(1)}, u32[]{:S(2)}, u32[]{:S(2)}) collective-permute-start(f32[8,384]{1,0:T(8,128)S(1)} %get-tuple-element.54), channel_id=1, source_target_pairs={{0,28},{4,0},{8,4},{12,8},{16,12},{20,16},{24,20},{28,24},{1,29},{... | collective-permute-start | bytes 36872 | tf_op jit(solution)/shard_map/ppermute | solution.py:385
  38.1 1.4 %collective-permute-done.5._.refs_6_ = f32[8,384]{1,0:T(8,128)S(1)} collective-permute-done((f32[8,384]{1,0:T(8,128)S(1)}, f32[8,384]{1,0:T(8,128)S(1)}, u32[]{:S(2)}, u32[]{:S(2)}) %collective-permute-start.5) | collective-permute-done | bytes 12320 | tf_op jit(solution)/shard_map/ppermute | solution.py:385
  39.5 2.2 %all-to-all-done.1.all_ref = f32[32,8,128]{2,1,0:T(8,128)S(1)} async-done(((f32[32,8,128]{2,1,0:T(8,128)}), f32[32,8,128]{2,1,0:T(8,128)S(1)}, u32[]{:S(2)}, u32[]{:S(2)}) %all-to-all-start.1) | async-done | bytes 131104 | tf_op jit(solution)/shard_map/all_to_all | solution.py:459
  41.7 1.1 %shard_map.109 = (f32[8,1024]{1,0:T(8,128)S(1)}, f32[8,1024]{1,0:T(8,128)S(1)}, f32[8,128]{1,0:T(8,128)S(1)}, s32[8,128]{1,0:T(8,128)S(1)}) custom-call(f32[32,8,128]{2,1,0:T(8,128)S(1)} %all-to-all-done.1.all_ref, f32[512,256]{1,0:T(8,128)S(1)} %collective-permute-done.1.far_ref, bf16[1024,256]{1,0:T(8,128)(2,1)S(1)} %get-tuple-element.44.inv_high, ...), custom_call_target="tpu_custom_call" | custom-call | tf_op jit(solution)/shard_map/pallas_call | solution.py:370
  42.8 0.2 collective-permute-start.6
  43.1 1.0 %collective-permute-done.6.refs_1_ = f32[8,1024]{1,0:T(8,128)S(1)} collective-permute-done((f32[8,1024]{1,0:T(8,128)S(1)}, f32[8,1024]{1,0:T(8,128)S(1)}, u32[]{:S(2)}, u32[]{:S(2)}) %collective-permute-start.6) | collective-permute-done | bytes 32800 | tf_op jit(solution)/shard_map/ppermute | solution.py:390
  44.1 0.9 %shard_map.110 = (f32[6,1,384]{2,1,0:T(1,128)}, f32[6,1,384]{2,1,0:T(1,128)}) custom-call(f32[8,1024]{1,0:T(8,128)S(1)} %get-tuple-element.55.refs_0_, f32[8,1024]{1,0:T(8,128)S(1)} %collective-permute-done.6.refs_1_, f32[8,1024]{1,0:T(8,128)S(1)} %get-tuple-element.56.refs_2_, f32[8,128]{1,0:T(8,128)S(1)} %get-tuple-element.57.refs_3_, ...), custom_call_target="tpu_custom_call" | custom-call | tf_op jit(solution)/shard_map/pallas_call | solution.py:370
Async XLA Ops:
  2.4 21.7 %collective-permute-start.1 = (f32[512,256]{1,0:T(8,128)S(1)}, f32[512,256]{1,0:T(8,128)S(1)}, u32[]{:S(2)}, u32[]{:S(2)}) collective-permute-start(f32[512,256]{1,0:T(8,128)S(1)} %get-tuple-element.43), channel_id=1, source_target_pairs={{0,2},{1,3},{2,0},{3,1},{4,6},{5,7},{6,4},{7,5},{8,10},{9,11},{10,... | collective-permute-start | bytes 1572872 | tf_op jit(solution)/shard_map/ppermute | solution.py:390
  5.4 6.4 %collective-permute-start = (f32[8,384]{1,0:T(8,128)S(1)}, f32[8,384]{1,0:T(8,128)S(1)}, u32[]{:S(2)}, u32[]{:S(2)}) collective-permute-start(f32[8,384]{1,0:T(8,128)S(1)} %get-tuple-element.33.pack_ref.refs_5_), channel_id=1, source_target_pairs={{0,4},{4,8},{8,12},{12,16},{16,20},{20,24},{24,28},{28,0},{1,5},{5... | collective-permute-start | bytes 36872 | tf_op jit(solution)/shard_map/ppermute | solution.py:385
  13.3 10.8 %all-to-all-start = ((f32[32,8,128]{2,1,0:T(8,128)}), f32[32,8,128]{2,1,0:T(8,128)S(1)}, u32[]{:S(2)}, u32[]{:S(2)}) async-start(f32[32,8,128]{2,1,0:T(8,128)} %get-tuple-element.42), calls=%async_computation | async-start | bytes 262144 | tf_op jit(solution)/shard_map/all_to_all | solution.py:459
  15.9 6.4 %collective-permute-start.2 = (f32[32,384]{1,0:T(8,128)S(1)}, f32[32,384]{1,0:T(8,128)S(1)}, u32[]{:S(2)}, u32[]{:S(2)}) collective-permute-start(f32[32,384]{1,0:T(8,128)S(1)} %get-tuple-element.46.refs_8_), channel_id=1, source_target_pairs={{0,28},{4,0},{8,4},{12,8},{16,12},{20,16},{24,20},{28,24},{1,29},{... | collective-permute-start | bytes 147464 | tf_op jit(solution)/shard_map/ppermute | solution.py:385
  20.5 6.8 %collective-permute-start.4 = (f32[32,384]{1,0:T(8,128)S(1)}, f32[32,384]{1,0:T(8,128)S(1)}, u32[]{:S(2)}, u32[]{:S(2)}) collective-permute-start(f32[32,384]{1,0:T(8,128)S(1)} %get-tuple-element.51.refs_7_), channel_id=1, source_target_pairs={{0,4},{4,8},{8,12},{12,16},{16,20},{20,24},{24,28},{28,0},{1,5},{5... | collective-permute-start | bytes 147464 | tf_op jit(solution)/shard_map/ppermute | solution.py:385
  25.8 1.5 %collective-permute-start.3 = (f32[8,1024]{1,0:T(8,128)S(1)}, f32[8,1024]{1,0:T(8,128)S(1)}, u32[]{:S(2)}, u32[]{:S(2)}) collective-permute-start(f32[8,1024]{1,0:T(8,128)S(1)} %get-tuple-element.47.refs_0_), channel_id=1, source_target_pairs={{0,1},{1,0},{2,3},{3,2},{4,5},{5,4},{6,7},{7,6},{8,9},{9,8},{10,11... | collective-permute-start | bytes 98312 | tf_op jit(solution)/shard_map/ppermute | solution.py:390
  29.2 12.5 %all-to-all-start.1 = ((f32[32,8,128]{2,1,0:T(8,128)}), f32[32,8,128]{2,1,0:T(8,128)S(1)}, u32[]{:S(2)}, u32[]{:S(2)}) async-start(f32[32,8,128]{2,1,0:T(8,128)} %get-tuple-element.53), calls=%async_computation.1 | async-start | bytes 262144 | tf_op jit(solution)/shard_map/all_to_all | solution.py:459
  33.5 6.0 %collective-permute-start.5 = (f32[8,384]{1,0:T(8,128)S(1)}, f32[8,384]{1,0:T(8,128)S(1)}, u32[]{:S(2)}, u32[]{:S(2)}) collective-permute-start(f32[8,384]{1,0:T(8,128)S(1)} %get-tuple-element.54), channel_id=1, source_target_pairs={{0,28},{4,0},{8,4},{12,8},{16,12},{20,16},{24,20},{28,24},{1,29},{... | collective-permute-start | bytes 36872 | tf_op jit(solution)/shard_map/ppermute | solution.py:385
  42.8 1.2 %collective-permute-start.6 = (f32[8,1024]{1,0:T(8,128)S(1)}, f32[8,1024]{1,0:T(8,128)S(1)}, u32[]{:S(2)}, u32[]{:S(2)}) collective-permute-start(f32[8,1024]{1,0:T(8,128)S(1)} %get-tuple-element.55.refs_0_), channel_id=1, source_target_pairs={{0,1},{1,0},{2,3},{3,2},{4,5},{5,4},{6,7},{7,6},{8,9},{9,8},{10,11... | collective-permute-start | bytes 98312 | tf_op jit(solution)/shard_map/ppermute | solution.py:390

commit v4 on v3

--- a/solution.py
+++ b/solution.py
@@ -13,6 +13,7 @@
 LANES = 128
 SLOT = 32
 GROUP = LANES // SLOT
+FOLD = ROWS // GROUP
 VMEM_LIMIT = 24 << 20
 
 
@@ -111,6 +112,17 @@
 
 def block_at(slab, j, width):
     return slab ^ j if is_paired(width) else j
+
+
+def by_turns(count):
+    return count % 2 == 0
+
+
+def dealt(right, left):
+    if not by_turns(lax.axis_size("sub")):
+        return right, left
+    even = lax.rem(lax.axis_index("sub"), 2) == 0
+    return jnp.where(even, right, left), jnp.where(even, left, right)
 
 
 def half_of(slab, inverse_hbm):
@@ -161,7 +173,7 @@
     s_high[...], s_low[...] = parts(schur[0, 0], 2)
 
 
-def forces(load, through, first, c_high, c_low, index_ref, cases, send_ref):
+def forces(load, through, first, c_high, c_low, index_ref, cases, send_hbm, send, sems):
     high, low = [jnp.concatenate([c[...]] * GROUP, axis=0) for c in (c_high, c_low)]
     force = product(load, high, low, True)
     lane = lax.broadcasted_iota(jnp.int32, force.shape, 1) % SLOT
@@ -169,13 +181,28 @@
     force = jnp.where(lane == SLOT - 2, first, force)
     force = jnp.where(lane == SLOT - 1, row_sum(load * through), force)
     force = jnp.where(row == cases, index_ref[...], force)
-    send_ref[...] = jnp.broadcast_to(force[None], send_ref.shape)
+    block = lax.broadcasted_iota(jnp.int32, force.shape, 1) // SLOT
+    force = jnp.where(row // FOLD == block, force, 0.0)
+    folded = sum(force[b * FOLD : (b + 1) * FOLD] for b in range(GROUP))
+    send[...] = jnp.broadcast_to(folded[None], send.shape)
+    (copy,) = fetched([(send, send_hbm)], sems)
+    return copy
+
+
+def unfolded(four):
+    block = lax.broadcasted_iota(jnp.int32, four.shape, 1) // SLOT
+    place = lax.broadcasted_iota(jnp.int32, four.shape, 0) // FOLD
+    out = four
+    for k in range(1, GROUP):
+        turned = pltpu.roll(pltpu.roll(four, SLOT * k, 1), ROWS - FOLD * k, 0)
+        out = jnp.where((block - place) % GROUP == k, turned, out)
+    return out
 
 
 def first_kernel(
     cases, left_ref, pack_ref, load_ref, own_coupling, index_ref,
     s_high, s_low, c_high, c_low, own_ref,
-    send_ref, right_ref, back_ref,
+    send_hbm, right_ref, back_ref, one_ref, two_ref, send, sems,
 ):
     left_residual, left_scale, left_index = unpacked(left_ref[...], cases)
     chosen = chosen_columns(left_index, load_ref.shape[1])
@@ -183,32 +210,30 @@
     through = product(load, s_high[...], s_low[...])
     residual, scale, _ = unpacked(pack_ref[...], cases)
     norm = row_sum(residual * residual * scale)
-    forces(load, through, norm, c_high, c_low, index_ref, cases, send_ref)
+    copy = forces(load, through, norm, c_high, c_low, index_ref, cases, send_hbm, send, sems)
     right_ref[:ROWS] = moved(through, chosen_columns(own_ref[...], load_ref.shape[1]))
     right_ref[ROWS:] = own_coupling[...]
     back_ref[:ROWS] = moved(through, chosen)
     held = own_coupling.shape[0]
     back_ref[ROWS:] = moved_parts(c_high[...], c_low[...], chosen)[:held]
+    one_ref[...], two_ref[...] = dealt(right_ref[...], back_ref[...])
+    copy.wait()
 
 
 def gathered_forces(cases, all_ref, corners, flip, sums_ref, total_ref):
     devices = all_ref.shape[0]
     chunk = min(devices, LANES // GROUP)
-    lane = lax.broadcasted_iota(jnp.int32, (ROWS, LANES), 1) // SLOT
     row = lax.broadcasted_iota(jnp.int32, (ROWS, 1), 0)
     step = min(corners, 1024)
 
     def add(at):
-        pieces = []
-        sums = jnp.zeros((ROWS, LANES), F32)
-        for group in range(chunk // GROUP):
-            piece = all_ref[at + group * GROUP]
-            sums = sums + piece
-            for e in range(1, GROUP):
-                other = all_ref[at + group * GROUP + e]
-                sums = sums + other
-                piece = jnp.where(lane == e, other, piece)
-            pieces.append(piece)
+        pieces = [
+            unfolded(jnp.concatenate([all_ref[at + group + e] for e in range(GROUP)], axis=0))
+            for group in range(0, chunk, GROUP)
+        ]
+        sums = sum(pieces)
+        for turn in (SLOT, 2 * SLOT):
+            sums = sums + pltpu.roll(sums, turn, 1)
         flat = jnp.concatenate(pieces, axis=1)
         index = flat[cases : cases + 1].astype(jnp.int32) ^ flip
         force = jnp.where(row < cases, flat, 0.0)
@@ -230,10 +255,11 @@
 
 def near_index(cases, all_ref):
     lane = lax.broadcasted_iota(jnp.int32, (1, LANES), 1) // SLOT
-    left, *others = near_devices()
-    index = all_ref[left, cases : cases + 1]
-    for e, device in enumerate(others, 1):
-        index = jnp.where(lane == e, all_ref[device, cases : cases + 1], index)
+    index = jnp.zeros((1, LANES), F32)
+    for e, device in enumerate(near_devices()):
+        rows = jnp.concatenate([all_ref[device]] * GROUP, axis=0)
+        rows = pltpu.roll(rows, SLOT * (e - cases // FOLD) % LANES, 1)
+        index = jnp.where(lane == e, rows[cases % FOLD : cases % FOLD + 1], index)
     return index.astype(jnp.int32)
 
 
@@ -252,25 +278,29 @@
 
 
 def pair_kernel(
-    cases, all_ref, far_ref, inv_high, inv_low, _, schur_hbm, x_ref, total_ref, sums_ref, index_ref, *later,
+    cases, all_ref, far_ref, inv_high, inv_low, schur_hbm, x_ref, total_ref, sums_ref, index_ref, *later,
 ):
     copies = fetched([(schur_hbm, later[0])], later[1]) if later else []
     width = inv_high.shape[1]
     slab = lax.axis_index("crs")
     flip = slab * width
-    gathered_forces(cases, all_ref, 4 * width, flip, sums_ref, total_ref)
-    index = near_index(cases, all_ref) ^ flip
-    index_ref[...] = jnp.broadcast_to(index, index_ref.shape)
-    total = total_ref[...]
-    last = [
-        far_ref[pl.ds(pl.multiple_of((slab % 2 ^ j) * width, width), width)] for j in range(2)
-    ]
-    third = product(total[:, 2 * width :], *parts(jnp.concatenate(last, axis=0), 2))
-    x_ref[:, :width] = product(total, inv_high[...], inv_low[...])
-    x_ref[:, width : 2 * width] = jnp.zeros((ROWS, width), F32)
-    across = product(total[:, :width], inv_high[2 * width :], inv_low[2 * width :], True)
-    x_ref[:, 2 * width : 3 * width] = across[:, :width] + third
-    x_ref[:, 3 * width :] = across[:, width:]
+
+    @pl.when(slab >= 0)
+    def _():
+        gathered_forces(cases, all_ref, 4 * width, flip, sums_ref, total_ref)
+        index = near_index(cases, all_ref) ^ flip
+        index_ref[...] = jnp.broadcast_to(index, index_ref.shape)
+        total = total_ref[...]
+        last = [
+            far_ref[pl.ds(pl.multiple_of((slab % 2 ^ j) * width, width), width)] for j in range(2)
+        ]
+        third = product(total[:, 2 * width :], *parts(jnp.concatenate(last, axis=0), 2))
+        x_ref[:, :width] = product(total, inv_high[...], inv_low[...])
+        x_ref[:, width : 2 * width] = jnp.zeros((ROWS, width), F32)
+        across = product(total[:, :width], inv_high[2 * width :], inv_low[2 * width :], True)
+        x_ref[:, 2 * width : 3 * width] = across[:, :width] + third
+        x_ref[:, 3 * width :] = across[:, width:]
+
     for copy in copies:
         copy.wait()
 
@@ -288,12 +318,13 @@
 
 def second_kernel(cases, coarse, given, *refs):
     (
-        pack_ref, left_ref, right_ref, back_ref, from_left, from_right,
+        pack_ref, left_ref, right_ref, back_ref, one_ref, two_ref,
         schur_ref, c_high, c_low, corner_ref, own_ref,
-        send_ref, out_ref, keep_ref, spread_ref, scalar_ref,
-    ) = refs[given : given + 16]
-    solution, total, sums, index = coarse(refs[:given] + refs[given + 16 :])
+        send_hbm, out_ref, keep_ref, spread_ref, scalar_ref, send, sems,
+    ) = refs[given : given + 18]
+    solution, total, sums, index = coarse(refs[:given] + refs[given + 18 :])
     picked = moved(solution, chosen_columns(index, solution.shape[1]))
+    from_right, from_left = dealt(one_ref[...], two_ref[...])
     blank = jnp.zeros((SLOT - (right_ref.shape[0] - ROWS), right_ref.shape[1]), F32)
     none = jnp.zeros((SLOT, right_ref.shape[1]), F32)
     own = jnp.concatenate([none, right_ref[ROWS:], blank, -from_right[ROWS:], blank, none], axis=0)
@@ -319,12 +350,14 @@
     left_map = chosen_columns(left_index, c_high.shape[1])
     load = moved(precon, own_map, True) - moved(left_precon, left_map, True)
     through = product(load, *parts(schur_ref[0, 0], 2))
-    forces(load, through, row_sum(residual * precon), c_high, c_low, corner_ref, cases, send_ref)
+    norm_here = row_sum(residual * precon)
+    copy = forces(load, through, norm_here, c_high, c_low, corner_ref, cases, send_hbm, send, sems)
     out_ref[...] = moved(through, left_map)
     keep_ref[:ROWS] = moved(through, own_map)
     keep_ref[ROWS:] = image
     lane = lax.broadcasted_iota(jnp.int32, scalar_ref.shape, 1)
     scalar_ref[...] = jnp.where(lane == 0, norm, alpha)
+    copy.wait()
 
 
 def last_kernel(cases, coarse, given, *refs):
@@ -361,7 +394,7 @@
 HB = pl.BlockSpec(memory_space=pltpu.HBM)
 
 
-def call(kernel, outs, given, specs, scratch=(), moved_bytes=None):
+def call(kernel, outs, given, specs, scratch=(), moved_bytes=None, stored=0):
     specs = specs + [VM] * (len(given) - len(specs))
     given = [
         pltpu.with_memory_space_constraint(x, pltpu.HBM) if spec is HB else x
@@ -371,7 +404,7 @@
         kernel,
         out_shape=[jax.ShapeDtypeStruct(shape, kind) for shape, kind in outs],
         in_specs=specs,
-        out_specs=[VM] * len(outs),
+        out_specs=[HB] * stored + [VM] * (len(outs) - stored),
         scratch_shapes=list(scratch),
         cost_estimate=moved_bytes
         and pl.CostEstimate(flops=0, bytes_accessed=moved_bytes, transcendentals=0),
@@ -421,6 +454,8 @@
         [SM] + [HB] * 4,
         [*buffers(*first)[:-1], pltpu.SemaphoreType.DMA((4,))],
     )
+    if is_paired(width):
+        far = exchanged(half, "crs", 2)
     left = passed_along(pack, "sub", 1)
     fetched_here = (schur_inverse, coarse_coupling, own_dof, corner_index, corner_inverse)
     s_high, s_low, c_high, c_low, own_coupling, load, index, own, inv_high, inv_low = call(
@@ -442,17 +477,14 @@
         buffers(*fetched_here),
         32 << 20,
     )
-    if is_paired(width):
-        far = exchanged(half, "crs", 2)
-    send, right, back = call(
+    outgoing = [pltpu.VMEM((devices, FOLD, LANES), F32), pltpu.SemaphoreType.DMA((1,))]
+    send, right, back, one, two = call(
         functools.partial(first_kernel, cases),
-        [
-            ((devices, ROWS, LANES), F32),
-            ((ROWS + held, records), F32),
-            ((ROWS + held, records), F32),
-        ],
+        [((devices, FOLD, LANES), F32)] + [((ROWS + held, records), F32)] * 4,
         (left, pack, load, own_coupling, index, s_high, s_low, c_high, c_low, own),
         [],
+        outgoing,
+        stored=1,
     )
 
     def gathered(send, beside, *later):
@@ -463,10 +495,11 @@
             x, total, sums, near, *fetched = call(
                 functools.partial(pair_kernel, cases),
                 [(row, F32), *outs, *((v.shape, v.dtype) for v in later)],
-                (everyone, far, inv_high, inv_low, beside, schur_inverse),
-                [VM] * 5 + [HB],
+                (everyone, far, inv_high, inv_low, schur_inverse),
+                [VM] * 4 + [HB],
                 [pltpu.SemaphoreType.DMA((1,)) for _ in later],
             )
+            x, _ = lax.optimization_barrier((x, beside))
             return (
                 (x, exchanged(x, "crs", 1), total, sums, near),
                 [VM] * 5,
@@ -489,24 +522,30 @@
             *later,
         )
 
-    from_left = passed_along(right, "sub", 1)
-    from_right = passed_along(back, "sub", -1)
-    given, specs, scratch, coarse, schur = gathered(send, from_right, schur_inverse)
+    if by_turns(chain):
+        rounds = [[(c, (c + 1) % chain) for c in range(start, chain, 2)] for start in (0, 1)]
+        rounds = [pairs + [(b, a) for a, b in pairs] for pairs in rounds]
+        two = lax.ppermute(two, "sub", rounds[1])
+        one = lax.ppermute(one, "sub", rounds[0])
+    else:
+        one, two = passed_along(two, "sub", -1), passed_along(one, "sub", 1)
+    given, specs, scratch, coarse, schur = gathered(send, two, schur_inverse)
     send, out, keep, spread, scalars = call(
         functools.partial(second_kernel, cases, coarse, len(given)),
         [
-            ((devices, ROWS, LANES), F32),
+            ((devices, FOLD, LANES), F32),
             ((ROWS, records), F32),
             ((2 * ROWS, records), F32),
             ((LANES, records), F32),
             ((ROWS, LANES), F32),
         ],
         (
-            *given, pack, left, right, back, from_left, from_right,
+            *given, pack, left, right, back, one, two,
             schur, c_high, c_low, index, own,
         ),
         specs,
-        scratch,
+        outgoing + scratch,
+        stored=1,
     )
     from_right = passed_along(out, "sub", -1)
     given, specs, scratch, coarse = gathered(send, from_right)

time: 45.3 us -> 42.6 us (0.940)
  waiting for transfers between devices: 11.8 us -> 9.97 us
  starting transfers between devices: 21.1 us -> 20.3 us
    ppermute x0 -> x2, starting transfers between devices: none -> 4.62 us  [the longest x1 4.62 us: per_device(): two = lax.ppermute(two, 'sub', rounds[1])]
    ppermute x4 -> x2, starting transfers between devices: 10.7 us -> 6.12 us  [passed_along(): return lax.ppermute(value, axis, pairs)]
    ppermute x4 -> x2, waiting for transfers between devices: 6.75 us -> 2.42 us  [passed_along(): return lax.ppermute(value, axis, pairs)]
    all_to_all x2, waiting for transfers between devices: 4.09 us -> 5.36 us  [gathered(): everyone = lax.all_to_all(send, ('sub', 'crs'), 0, 0)]
    ppermute x3, waiting for transfers between devices: 1 us -> 2.18 us  [exchanged(): return lax.ppermute(value, axis, pairs)]
    all_to_all x2, starting transfers between devices: 6.83 us -> 6.16 us  [gathered(): everyone = lax.all_to_all(send, ('sub', 'crs'), 0, 0)]
  transfers between devices with their start and end apart: 9 -> 9, of which waited for: 7 -> 5; matrix products, arithmetic and copies ran while one was open for 0% -> 0% of each run, Pallas kernels for 12% -> 16%
where the time goes in v4:
time: 42.6 us; the launch traced here: 42.4 us
  starting transfers between devices  20.3 us (48%)
  Pallas kernels  10.8 us (25%)
  waiting for transfers between devices  9.97 us (23%)
  between operations  1.35 us (3%)
    pallas_call x7, Pallas kernels, call(): pl.pallas_call(kernel, out_shape=[jax.ShapeDtypeStruct(shape, kind) for s...  10.8 us
    all_to_all x2, starting transfers between devices, gathered(): everyone = lax.all_to_all(send, ('sub', 'crs'), 0, 0)  6.16 us
    ppermute x2, starting transfers between devices, passed_along(): return lax.ppermute(value, axis, pairs)  6.12 us
    all_to_all x2, waiting for transfers between devices, gathered(): everyone = lax.all_to_all(send, ('sub', 'crs'), 0, 0)  5.36 us
    ppermute x1, starting transfers between devices, per_device(): two = lax.ppermute(two, 'sub', rounds[1])  4.62 us
    ppermute x3, starting transfers between devices, exchanged(): return lax.ppermute(value, axis, pairs)  3.35 us
    ppermute x2, waiting for transfers between devices, passed_along(): return lax.ppermute(value, axis, pairs)  2.42 us
    ppermute x3, waiting for transfers between devices, exchanged(): return lax.ppermute(value, axis, pairs)  2.18 us
  transfers between devices with their start and end apart: 9, of which 5 were waited for; matrix products, arithmetic and copies ran while one was open for 0% of the time, Pallas kernels for 16%

profile of v4, /device:TPU:0, one launch (start us, length us, event | category | flops | bytes accessed | tf_op | source)
XLA Modules:
  0.0 42.4 jit_solution(3096284637351379060)
XLA Ops:
  1.3 1.1 %shard_map.104 = (f32[8,384]{1,0:T(8,128)S(1)}, f32[512,256]{1,0:T(8,128)S(1)}) custom-call(s32[1,1]{1,0:T(1,128)S(6)} %copy.13.live_ref, f32[6,1,384]{2,1,0:T(1,128)} %bitcast.7, f32[1,1,384]{2,1,0:T(1,128)} %scale_hbm.1, s32[1,1,384]{2,1,0:T(1,128)} %nbr_hbm.1, f32[1024,256]{1,0:T(8,128)} %inverse_hbm.3), custom_call_target="tpu_custom_call" | custom-call | tf_op jit(solution)/shard_map/pallas_call | solution.py:403
  2.4 3.0 %collective-permute-start.1 = (f32[512,256]{1,0:T(8,128)S(1)}, f32[512,256]{1,0:T(8,128)S(1)}, u32[]{:S(2)}, u32[]{:S(2)}) collective-permute-start(f32[512,256]{1,0:T(8,128)S(1)} %get-tuple-element.47), channel_id=1, source_target_pairs={{0,2},{1,3},{2,0},{3,1},{4,6},{5,7},{6,4},{7,5},{8,10},{9,11},{10,... | collective-permute-start | bytes 1572872 | tf_op jit(solution)/shard_map/ppermute | solution.py:423
  5.4 1.5 %collective-permute-start = (f32[8,384]{1,0:T(8,128)S(1)}, f32[8,384]{1,0:T(8,128)S(1)}, u32[]{:S(2)}, u32[]{:S(2)}) collective-permute-start(f32[8,384]{1,0:T(8,128)S(1)} %get-tuple-element.37.pack_ref.refs_5_), channel_id=1, source_target_pairs={{0,4},{4,8},{8,12},{12,16},{16,20},{20,24},{24,28},{28,0},{1,5},{5... | collective-permute-start | bytes 36872 | tf_op jit(solution)/shard_map/ppermute | solution.py:418
  6.9 2.4 %shard_map.105 = (bf16[768,768]{1,0:T(8,128)(2,1)S(1)}, bf16[768,768]{1,0:T(8,128)(2,1)S(1)}, bf16[32,768]{1,0:T(8,128)(2,1)S(1)}, bf16[32,768]{1,0:T(8,128)(2,1...) custom-call(f32[8,384]{1,0:T(8,128)S(1)} %get-tuple-element.37.pack_, ...), custom_call_target="tpu_custom_call" | custom-call | bytes 33554432 | tf_op jit(solution)/shard_map/pallas_call | solution.py:403
  9.4 2.4 %collective-permute-done.left_ref.refs_6_ = f32[8,384]{1,0:T(8,128)S(1)} collective-permute-done((f32[8,384]{1,0:T(8,128)S(1)}, f32[8,384]{1,0:T(8,128)S(1)}, u32[]{:S(2)}, u32[]{:S(2)}) %collective-permute-start) | collective-permute-done | bytes 12320 | tf_op jit(solution)/shard_map/ppermute | solution.py:418
  11.8 1.5 %shard_map.106 = (f32[32,2,128]{2,1,0:T(2,128)}, f32[32,384]{1,0:T(8,128)S(1)}, f32[32,384]{1,0:T(8,128)S(1)}, f32[32,384]{1,0:T(8,128)S(1)}, f32[32,384]{1,0:T(8,128)S(1)}) custom-call(f32[8,384]{1,0:T(8,128)S(1)} %collective-permute-done.left_ref.refs_6_, f32[8,384]{1,0:T(8,128)S(1)} %get-tuple-element.37.pack_ref.refs_5_, ...), custom_call_target="tpu_custom_call" | custom-call | tf_op jit(solution)/shard_map/pallas_call | solution.py:403
  13.3 2.6 %all-to-all-start = ((f32[32,2,128]{2,1,0:T(2,128)}), f32[32,2,128]{2,1,0:T(2,128)S(1)}, u32[]{:S(2)}, u32[]{:S(2)}) async-start(f32[32,2,128]{2,1,0:T(2,128)} %get-tuple-element.46), calls=%async_computation | async-start | bytes 65536 | tf_op jit(solution)/shard_map/all_to_all | solution.py:491
  15.9 4.6 %collective-permute-start.2 = (f32[32,384]{1,0:T(8,128)S(1)}, f32[32,384]{1,0:T(8,128)S(1)}, u32[]{:S(2)}, u32[]{:S(2)}) collective-permute-start(f32[32,384]{1,0:T(8,128)S(1)} %get-tuple-element.51), channel_id=1, source_target_pairs={{4,8},{12,16},{20,24},{28,0},{8,4},{16,12},{24,20},{0,28},{5,9},{1... | collective-permute-start | bytes 147464 | tf_op jit(solution)/shard_map/ppermute | solution.py:528
  20.5 0.0 collective-permute-start.4
  20.5 2.7 %all-to-all-done.all_ref = f32[32,2,128]{2,1,0:T(2,128)S(1)} async-done(((f32[32,2,128]{2,1,0:T(2,128)}), f32[32,2,128]{2,1,0:T(2,128)S(1)}, u32[]{:S(2)}, u32[]{:S(2)}) %all-to-all-start) | async-done | bytes 32800 | tf_op jit(solution)/shard_map/all_to_all | solution.py:491
  23.2 0.0 collective-permute-done.1.far_ref
  23.2 1.7 %shard_map.107 = (f32[8,1024]{1,0:T(8,128)S(1)}, f32[8,1024]{1,0:T(8,128)S(1)}, f32[8,128]{1,0:T(8,128)S(1)}, s32[8,128]{1,0:T(8,128)S(1)}, f32[1,1,768,768]{3,2,1,0:T(8,128)S(1)}) custom-call(f32[32,2,128]{2,1,0:T(2,128)S(1)} %all-to-all-done.all_ref, f32[512,256]{1,0:T(8,128)S(1)} %collective-permute-done.1.far_ref, ...), custom_call_target="tpu_custom_call" | custom-call | tf_op jit(solution)/shard_map/pallas_call | solution.py:403
  24.9 0.0 collective-permute-done.2.refs_10_
  24.9 0.2 collective-permute-start.3
  25.1 0.0 collective-permute-done.4.refs_9_
  25.1 1.1 %collective-permute-done.3.refs_1_ = f32[8,1024]{1,0:T(8,128)S(1)} collective-permute-done((f32[8,1024]{1,0:T(8,128)S(1)}, f32[8,1024]{1,0:T(8,128)S(1)}, u32[]{:S(2)}, u32[]{:S(2)}) %collective-permute-start.3) | collective-permute-done | bytes 32800 | tf_op jit(solution)/shard_map/ppermute | solution.py:423
  26.2 1.9 %shard_map.108 = (f32[32,2,128]{2,1,0:T(2,128)}, f32[8,384]{1,0:T(8,128)S(1)}, f32[16,384]{1,0:T(8,128)S(1)}, f32[128,384]{1,0:T(8,128)S(1)}, f32[8,128]{1,0:T(8,128)S(1)}) custom-call(f32[8,1024]{1,0:T(8,128)S(1)} %get-tuple-element.52.refs_0_, f32[8,1024]{1,0:T(8,128)S(1)} %collective-permute-done.3.refs_1_, f32[8,1024]{1,0:T(8,128)S(1)} %get-tuple-element.53.refs_2_, ...), custom_call_target="tpu_custom_call" | custom-call | tf_op jit(solution)/shard_map/pallas_call | solution.py:403
  28.1 3.6 %all-to-all-start.1 = ((f32[32,2,128]{2,1,0:T(2,128)}), f32[32,2,128]{2,1,0:T(2,128)S(1)}, u32[]{:S(2)}, u32[]{:S(2)}) async-start(f32[32,2,128]{2,1,0:T(2,128)} %get-tuple-element.60), calls=%async_computation.1 | async-start | bytes 65536 | tf_op jit(solution)/shard_map/all_to_all | solution.py:491
  31.7 4.6 %collective-permute-start.5 = (f32[8,384]{1,0:T(8,128)S(1)}, f32[8,384]{1,0:T(8,128)S(1)}, u32[]{:S(2)}, u32[]{:S(2)}) collective-permute-start(f32[8,384]{1,0:T(8,128)S(1)} %get-tuple-element.62), channel_id=1, source_target_pairs={{0,28},{4,0},{8,4},{12,8},{16,12},{20,16},{24,20},{28,24},{1,29},{... | collective-permute-start | bytes 36872 | tf_op jit(solution)/shard_map/ppermute | solution.py:418
  36.3 2.6 %all-to-all-done.1.all_ref = f32[32,2,128]{2,1,0:T(2,128)S(1)} async-done(((f32[32,2,128]{2,1,0:T(2,128)}), f32[32,2,128]{2,1,0:T(2,128)S(1)}, u32[]{:S(2)}, u32[]{:S(2)}) %all-to-all-start.1) | async-done | bytes 32800 | tf_op jit(solution)/shard_map/all_to_all | solution.py:491
  38.9 1.2 %shard_map.109 = (f32[8,1024]{1,0:T(8,128)S(1)}, f32[8,1024]{1,0:T(8,128)S(1)}, f32[8,128]{1,0:T(8,128)S(1)}, s32[8,128]{1,0:T(8,128)S(1)}) custom-call(f32[32,2,128]{2,1,0:T(2,128)S(1)} %all-to-all-done.1.all_ref, f32[512,256]{1,0:T(8,128)S(1)} %collective-permute-done.1.far_ref, bf16[1024,256]{1,0:T(8,128)(2,1)S(1)} %get-tuple-element.48.inv_high, ...), custom_call_target="tpu_custom_call" | custom-call | tf_op jit(solution)/shard_map/pallas_call | solution.py:403
  40.2 0.0 collective-permute-done.5.refs_6_
  40.2 0.2 collective-permute-start.6
  40.3 1.1 %collective-permute-done.6.refs_1_ = f32[8,1024]{1,0:T(8,128)S(1)} collective-permute-done((f32[8,1024]{1,0:T(8,128)S(1)}, f32[8,1024]{1,0:T(8,128)S(1)}, u32[]{:S(2)}, u32[]{:S(2)}) %collective-permute-start.6) | collective-permute-done | bytes 32800 | tf_op jit(solution)/shard_map/ppermute | solution.py:423
  41.4 0.9 %shard_map.110 = (f32[6,1,384]{2,1,0:T(1,128)}, f32[6,1,384]{2,1,0:T(1,128)}) custom-call(f32[8,1024]{1,0:T(8,128)S(1)} %get-tuple-element.63.refs_0_, f32[8,1024]{1,0:T(8,128)S(1)} %collective-permute-done.6.refs_1_, f32[8,1024]{1,0:T(8,128)S(1)} %get-tuple-element.64.refs_2_, f32[8,128]{1,0:T(8,128)S(1)} %get-tuple-element.65.refs_3_, ...), custom_call_target="tpu_custom_call" | custom-call | tf_op jit(solution)/shard_map/pallas_call | solution.py:403
Async XLA Ops:
  2.4 20.8 %collective-permute-start.1 = (f32[512,256]{1,0:T(8,128)S(1)}, f32[512,256]{1,0:T(8,128)S(1)}, u32[]{:S(2)}, u32[]{:S(2)}) collective-permute-start(f32[512,256]{1,0:T(8,128)S(1)} %get-tuple-element.47), channel_id=1, source_target_pairs={{0,2},{1,3},{2,0},{3,1},{4,6},{5,7},{6,4},{7,5},{8,10},{9,11},{10,... | collective-permute-start | bytes 1572872 | tf_op jit(solution)/shard_map/ppermute | solution.py:423
  5.4 6.4 %collective-permute-start = (f32[8,384]{1,0:T(8,128)S(1)}, f32[8,384]{1,0:T(8,128)S(1)}, u32[]{:S(2)}, u32[]{:S(2)}) collective-permute-start(f32[8,384]{1,0:T(8,128)S(1)} %get-tuple-element.37.pack_ref.refs_5_), channel_id=1, source_target_pairs={{0,4},{4,8},{8,12},{12,16},{16,20},{20,24},{24,28},{28,0},{1,5},{5... | collective-permute-start | bytes 36872 | tf_op jit(solution)/shard_map/ppermute | solution.py:418
  13.3 9.9 %all-to-all-start = ((f32[32,2,128]{2,1,0:T(2,128)}), f32[32,2,128]{2,1,0:T(2,128)S(1)}, u32[]{:S(2)}, u32[]{:S(2)}) async-start(f32[32,2,128]{2,1,0:T(2,128)} %get-tuple-element.46), calls=%async_computation | async-start | bytes 65536 | tf_op jit(solution)/shard_map/all_to_all | solution.py:491
  15.9 9.0 %collective-permute-start.2 = (f32[32,384]{1,0:T(8,128)S(1)}, f32[32,384]{1,0:T(8,128)S(1)}, u32[]{:S(2)}, u32[]{:S(2)}) collective-permute-start(f32[32,384]{1,0:T(8,128)S(1)} %get-tuple-element.51), channel_id=1, source_target_pairs={{4,8},{12,16},{20,24},{28,0},{8,4},{16,12},{24,20},{0,28},{5,9},{1... | collective-permute-start | bytes 147464 | tf_op jit(solution)/shard_map/ppermute | solution.py:528
  20.5 4.6 %collective-permute-start.4 = (f32[32,384]{1,0:T(8,128)S(1)}, f32[32,384]{1,0:T(8,128)S(1)}, u32[]{:S(2)}, u32[]{:S(2)}) collective-permute-start(f32[32,384]{1,0:T(8,128)S(1)} %get-tuple-element.58), channel_id=1, source_target_pairs={{0,4},{8,12},{16,20},{24,28},{4,0},{12,8},{20,16},{28,24},{1,5},{9... | collective-permute-start | bytes 147464 | tf_op jit(solution)/shard_map/ppermute | solution.py:529
  24.9 1.3 %collective-permute-start.3 = (f32[8,1024]{1,0:T(8,128)S(1)}, f32[8,1024]{1,0:T(8,128)S(1)}, u32[]{:S(2)}, u32[]{:S(2)}) collective-permute-start(f32[8,1024]{1,0:T(8,128)S(1)} %get-tuple-element.52.refs_0_), channel_id=1, source_target_pairs={{0,1},{1,0},{2,3},{3,2},{4,5},{5,4},{6,7},{7,6},{8,9},{9,8},{10,11... | collective-permute-start | bytes 98312 | tf_op jit(solution)/shard_map/ppermute | solution.py:423
  28.1 10.9 %all-to-all-start.1 = ((f32[32,2,128]{2,1,0:T(2,128)}), f32[32,2,128]{2,1,0:T(2,128)S(1)}, u32[]{:S(2)}, u32[]{:S(2)}) async-start(f32[32,2,128]{2,1,0:T(2,128)} %get-tuple-element.60), calls=%async_computation.1 | async-start | bytes 65536 | tf_op jit(solution)/shard_map/all_to_all | solution.py:491
  31.7 8.5 %collective-permute-start.5 = (f32[8,384]{1,0:T(8,128)S(1)}, f32[8,384]{1,0:T(8,128)S(1)}, u32[]{:S(2)}, u32[]{:S(2)}) collective-permute-start(f32[8,384]{1,0:T(8,128)S(1)} %get-tuple-element.62), channel_id=1, source_target_pairs={{0,28},{4,0},{8,4},{12,8},{16,12},{20,16},{24,20},{28,24},{1,29},{... | collective-permute-start | bytes 36872 | tf_op jit(solution)/shard_map/ppermute | solution.py:418
  40.2 1.3 %collective-permute-start.6 = (f32[8,1024]{1,0:T(8,128)S(1)}, f32[8,1024]{1,0:T(8,128)S(1)}, u32[]{:S(2)}, u32[]{:S(2)}) collective-permute-start(f32[8,1024]{1,0:T(8,128)S(1)} %get-tuple-element.63.refs_0_), channel_id=1, source_target_pairs={{0,1},{1,0},{2,3},{3,2},{4,5},{5,4},{6,7},{7,6},{8,9},{9,8},{10,11... | collective-permute-start | bytes 98312 | tf_op jit(solution)/shard_map/ppermute | solution.py:423

commit v5 on v4

--- a/solution.py
+++ b/solution.py
@@ -69,6 +69,10 @@
     for copy in copies:
         copy.start()
     return copies
+
+
+def always(body):
+    pl.when(lax.axis_index("crs") >= 0)(body)
 
 
 def pack_kernel(
@@ -132,16 +136,15 @@
 
 
 def prepare_kernel(
-    cases, pack_ref, schur_hbm, coupling_hbm, own_hbm, corner_hbm, inverse_hbm,
-    s_high, s_low, c_high, c_low, own_coupling, load_ref, index_ref, own_ref, inv_high, inv_low,
-    schur, coupling, own, corner, inverse, sems,
+    cases, pack_ref, schur_hbm, coupling_hbm, own_hbm, corner_hbm,
+    s_high, s_low, c_high, c_low, own_coupling, load_ref, index_ref, own_ref,
+    schur, coupling, own, corner, sems,
 ):
     copies = fetched(
         [
             (own_hbm, own),
             (coupling_hbm, coupling),
             (corner_hbm, corner),
-            (inverse_hbm, inverse),
             (schur_hbm, schur),
         ],
         sems,
@@ -161,16 +164,32 @@
     index = jnp.broadcast_to(corner[0].astype(F32), (ROWS, held))
     index_ref[...] = jnp.where(lane[:1] < held, moved(index, tiles.astype(BF16))[:1], -1.0)
     copies[3].wait()
-    slab = lax.axis_index("crs")
-    blocks = lax.axis_size("crs")
-    width = inverse.shape[1]
+    s_high[...], s_low[...] = parts(schur[0, 0], 2)
+
+
+def inverse_kernel(inverse_hbm, inv_high, inv_low, inverse, sems):
+    blocks, width = lax.axis_size("crs"), inverse.shape[1]
+    pairs = []
     for j in range(blocks):
-        rows = pl.ds(pl.multiple_of(block_at(slab, j, width) * width, width), width)
-        high, low = parts(inverse[rows], 2)
-        inv_high[j * width : (j + 1) * width] = high
-        inv_low[j * width : (j + 1) * width] = low
-    copies[4].wait()
-    s_high[...], s_low[...] = parts(schur[0, 0], 2)
+        rows = pl.ds(pl.multiple_of(block_at(lax.axis_index("crs"), j, width) * width, width), width)
+        pairs.append((inverse_hbm.at[rows], inverse.at[pl.ds(j * width, width)]))
+    for copy in fetched(pairs, sems):
+        copy.wait()
+    inv_high[...], inv_low[...] = parts(inverse[...], 2)
+
+
+def terms_kernel(top_ref, left_index, own_ref, schur_hbm, s_high, s_low, own_map, left_map, rest, sems):
+    rows, iface = top_ref.shape
+    (copy,) = fetched([(schur_hbm.at[0, 0, pl.ds(rows, iface - rows)], rest)], sems)
+
+    @always
+    def _():
+        s_high[:rows], s_low[:rows] = parts(top_ref[...], 2)
+        own_map[...] = chosen_columns(own_ref[...], iface)
+        left_map[...] = chosen_columns(left_index[...], iface)
+
+    copy.wait()
+    s_high[rows:], s_low[rows:] = parts(rest[...], 2)
 
 
 def forces(load, through, first, c_high, c_low, index_ref, cases, send_hbm, send, sems):
@@ -202,21 +221,26 @@
 def first_kernel(
     cases, left_ref, pack_ref, load_ref, own_coupling, index_ref,
     s_high, s_low, c_high, c_low, own_ref,
-    send_hbm, right_ref, back_ref, one_ref, two_ref, send, sems,
+    send_hbm, right_ref, back_ref, one_ref, two_ref, index_out, send, sems,
 ):
     left_residual, left_scale, left_index = unpacked(left_ref[...], cases)
+    index_out[...] = left_index
     chosen = chosen_columns(left_index, load_ref.shape[1])
     load = load_ref[...] - moved(left_residual * left_scale, chosen, True)
     through = product(load, s_high[...], s_low[...])
     residual, scale, _ = unpacked(pack_ref[...], cases)
     norm = row_sum(residual * residual * scale)
     copy = forces(load, through, norm, c_high, c_low, index_ref, cases, send_hbm, send, sems)
-    right_ref[:ROWS] = moved(through, chosen_columns(own_ref[...], load_ref.shape[1]))
-    right_ref[ROWS:] = own_coupling[...]
-    back_ref[:ROWS] = moved(through, chosen)
-    held = own_coupling.shape[0]
-    back_ref[ROWS:] = moved_parts(c_high[...], c_low[...], chosen)[:held]
-    one_ref[...], two_ref[...] = dealt(right_ref[...], back_ref[...])
+
+    @always
+    def _():
+        right_ref[:ROWS] = moved(through, chosen_columns(own_ref[...], load_ref.shape[1]))
+        right_ref[ROWS:] = own_coupling[...]
+        back_ref[:ROWS] = moved(through, chosen)
+        held = own_coupling.shape[0]
+        back_ref[ROWS:] = moved_parts(c_high[...], c_low[...], chosen)[:held]
+        one_ref[...], two_ref[...] = dealt(right_ref[...], back_ref[...])
+
     copy.wait()
 
 
@@ -280,12 +304,12 @@
 def pair_kernel(
     cases, all_ref, far_ref, inv_high, inv_low, schur_hbm, x_ref, total_ref, sums_ref, index_ref, *later,
 ):
-    copies = fetched([(schur_hbm, later[0])], later[1]) if later else []
+    copies = fetched([(schur_hbm.at[0, 0, : later[0].shape[0]], later[0])], later[1]) if later else []
     width = inv_high.shape[1]
     slab = lax.axis_index("crs")
     flip = slab * width
 
-    @pl.when(slab >= 0)
+    @always
     def _():
         gathered_forces(cases, all_ref, 4 * width, flip, sums_ref, total_ref)
         index = near_index(cases, all_ref) ^ flip
@@ -319,10 +343,10 @@
 def second_kernel(cases, coarse, given, *refs):
     (
         pack_ref, left_ref, right_ref, back_ref, one_ref, two_ref,
-        schur_ref, c_high, c_low, corner_ref, own_ref,
+        s_high, s_low, own_map, left_map, c_high, c_low, corner_ref,
         send_hbm, out_ref, keep_ref, spread_ref, scalar_ref, send, sems,
-    ) = refs[given : given + 18]
-    solution, total, sums, index = coarse(refs[:given] + refs[given + 18 :])
+    ) = refs[given : given + 20]
+    solution, total, sums, index = coarse(refs[:given] + refs[given + 20 :])
     picked = moved(solution, chosen_columns(index, solution.shape[1]))
     from_right, from_left = dealt(one_ref[...], two_ref[...])
     blank = jnp.zeros((SLOT - (right_ref.shape[0] - ROWS), right_ref.shape[1]), F32)
@@ -333,7 +357,7 @@
     both = product(picked, *parts(jnp.concatenate([own, other], axis=1), 2))
     records = right_ref.shape[1]
     residual, scale, _ = unpacked(pack_ref[...], cases)
-    left_residual, left_scale, left_index = unpacked(left_ref[...], cases)
+    left_residual, left_scale, _ = unpacked(left_ref[...], cases)
     live = (scale > 0.0).astype(F32)
     left_live = (left_scale > 0.0).astype(F32)
     image = (right_ref[:ROWS] - from_right[:ROWS] + both[:, :records]) * live
@@ -346,17 +370,19 @@
     left_residual = left_residual - alpha * left_image
     precon = scale * residual
     left_precon = left_scale * left_residual
-    own_map = chosen_columns(own_ref[...], c_high.shape[1])
-    left_map = chosen_columns(left_index, c_high.shape[1])
-    load = moved(precon, own_map, True) - moved(left_precon, left_map, True)
-    through = product(load, *parts(schur_ref[0, 0], 2))
+    load = moved(precon, own_map[...], True) - moved(left_precon, left_map[...], True)
+    through = product(load, s_high[...], s_low[...])
     norm_here = row_sum(residual * precon)
     copy = forces(load, through, norm_here, c_high, c_low, corner_ref, cases, send_hbm, send, sems)
-    out_ref[...] = moved(through, left_map)
-    keep_ref[:ROWS] = moved(through, own_map)
-    keep_ref[ROWS:] = image
-    lane = lax.broadcasted_iota(jnp.int32, scalar_ref.shape, 1)
-    scalar_ref[...] = jnp.where(lane == 0, norm, alpha)
+
+    @always
+    def _():
+        out_ref[...] = moved(through, left_map[...])
+        keep_ref[:ROWS] = moved(through, own_map[...])
+        keep_ref[ROWS:] = image
+        lane = lax.broadcasted_iota(jnp.int32, scalar_ref.shape, 1)
+        scalar_ref[...] = jnp.where(lane == 0, norm, alpha)
+
     copy.wait()
 
 
@@ -407,7 +433,7 @@
         out_specs=[HB] * stored + [VM] * (len(outs) - stored),
         scratch_shapes=list(scratch),
         cost_estimate=moved_bytes
-        and pl.CostEstimate(flops=0, bytes_accessed=moved_bytes, transcendentals=0),
+        and pl.CostEstimate(flops=int(4e10) if moved_bytes<0 else 0, bytes_accessed=abs(moved_bytes), transcendentals=0),
         compiler_params=pltpu.CompilerParams(vmem_limit_bytes=VMEM_LIMIT),
     )(*given)
 
@@ -457,8 +483,8 @@
     if is_paired(width):
         far = exchanged(half, "crs", 2)
     left = passed_along(pack, "sub", 1)
-    fetched_here = (schur_inverse, coarse_coupling, own_dof, corner_index, corner_inverse)
-    s_high, s_low, c_high, c_low, own_coupling, load, index, own, inv_high, inv_low = call(
+    fetched_here = (schur_inverse, coarse_coupling, own_dof, corner_index)
+    s_high, s_low, c_high, c_low, own_coupling, load, index, own = call(
         functools.partial(prepare_kernel, cases),
         [
             ((iface, iface), BF16),
@@ -469,37 +495,48 @@
             ((ROWS, iface), F32),
             ((1, LANES), F32),
             ((1, records), jnp.int32),
-            ((corners, width), BF16),
-            ((corners, width), BF16),
         ],
         (pack, *fetched_here),
-        [VM] + [HB] * 5,
+        [VM] + [HB] * 4,
         buffers(*fetched_here),
         32 << 20,
     )
+    inv_high, inv_low = call(
+        inverse_kernel,
+        [((corners, width), BF16)] * 2,
+        (corner_inverse,),
+        [HB],
+        [pltpu.VMEM((corners, width), F32), pltpu.SemaphoreType.DMA((slabs,))],
+    )
     outgoing = [pltpu.VMEM((devices, FOLD, LANES), F32), pltpu.SemaphoreType.DMA((1,))]
-    send, right, back, one, two = call(
+    send, right, back, one, two, left_index = call(
         functools.partial(first_kernel, cases),
-        [((devices, FOLD, LANES), F32)] + [((ROWS + held, records), F32)] * 4,
+        [((devices, FOLD, LANES), F32)]
+        + [((ROWS + held, records), F32)] * 4
+        + [((1, records), jnp.int32)],
         (left, pack, load, own_coupling, index, s_high, s_low, c_high, c_low, own),
         [],
         outgoing,
+        -1,
         stored=1,
     )
 
-    def gathered(send, beside, *later):
+    top = (iface // 16 * 8, iface)
+
+    def gathered(send, beside, ahead):
         everyone = lax.all_to_all(send, ("sub", "crs"), 0, 0)
         row = (ROWS, corners)
         outs = [(row, F32), ((ROWS, LANES), F32), ((ROWS, LANES), jnp.int32)]
         if is_paired(width):
             x, total, sums, near, *fetched = call(
                 functools.partial(pair_kernel, cases),
-                [(row, F32), *outs, *((v.shape, v.dtype) for v in later)],
+                [(row, F32), *outs] + [(top, F32)] * ahead,
                 (everyone, far, inv_high, inv_low, schur_inverse),
                 [VM] * 4 + [HB],
-                [pltpu.SemaphoreType.DMA((1,)) for _ in later],
+                [pltpu.SemaphoreType.DMA((1,))] * ahead,
             )
-            x, _ = lax.optimization_barrier((x, beside))
+            if beside is not None:
+                x, _ = lax.optimization_barrier((x, beside))
             return (
                 (x, exchanged(x, "crs", 1), total, sums, near),
                 [VM] * 5,
@@ -519,7 +556,7 @@
             [VM] * (len(pieces) + len(others)),
             [pltpu.VMEM(row, F32)],
             functools.partial(shared_coarse, cases, width),
-            *later,
+            *[schur_inverse[0, 0, : top[0]]] * ahead,
         )
 
     if by_turns(chain):
@@ -529,7 +566,14 @@
         one = lax.ppermute(one, "sub", rounds[0])
     else:
         one, two = passed_along(two, "sub", -1), passed_along(one, "sub", 1)
-    given, specs, scratch, coarse, schur = gathered(send, two, schur_inverse)
+    given, specs, scratch, coarse, first_rows = gathered(send, None, 1)
+    terms = call(
+        terms_kernel,
+        [((iface, iface), BF16)] * 2 + [((iface, records), BF16)] * 2,
+        (first_rows, left_index, own, schur_inverse),
+        [VM] * 3 + [HB],
+        [pltpu.VMEM((iface - top[0], iface), F32), pltpu.SemaphoreType.DMA((1,))],
+    )
     send, out, keep, spread, scalars = call(
         functools.partial(second_kernel, cases, coarse, len(given)),
         [
@@ -541,14 +585,14 @@
         ],
         (
             *given, pack, left, right, back, one, two,
-            schur, c_high, c_low, index, own,
+            *terms, c_high, c_low, index,
         ),
         specs,
         outgoing + scratch,
         stored=1,
     )
     from_right = passed_along(out, "sub", -1)
-    given, specs, scratch, coarse = gathered(send, from_right)
+    given, specs, scratch, coarse = gathered(send, from_right, 0)
     outs = call(
         functools.partial(last_kernel, cases, coarse, len(given)),
         [(jump.shape, F32), (jump.shape, F32)],

time: 42.6 us -> 41 us (0.962)
  waiting for transfers between devices: 9.97 us -> 5.59 us
  Pallas kernels: 10.8 us -> 12.8 us
  starting transfers between devices: 20.3 us -> 20.9 us
    pallas_call x7 -> x9, Pallas kernels: 10.8 us -> 12.8 us  [call(): pl.pallas_call(kernel, out_shape=[jax.ShapeDtypeStruct(shape, kind) for s...]
    all_to_all x2, waiting for transfers between devices: 5.36 us -> 3.39 us  [gathered(): everyone = lax.all_to_all(send, ('sub', 'crs'), 0, 0)]
    ppermute x1, starting transfers between devices: 0.01 us -> 1.83 us  [per_device(): one = lax.ppermute(one, 'sub', rounds[0])]
    ppermute x3, starting transfers between devices: 3.35 us -> 1.83 us  [exchanged(): return lax.ppermute(value, axis, pairs)]
    ppermute x2, starting transfers between devices: 6.12 us -> 7.62 us  [passed_along(): return lax.ppermute(value, axis, pairs)]
    ppermute x2, waiting for transfers between devices: 2.42 us -> 1.1 us  [passed_along(): return lax.ppermute(value, axis, pairs)]
    ppermute x1, starting transfers between devices: 4.62 us -> 3.31 us  [per_device(): two = lax.ppermute(two, 'sub', rounds[1])]
    ppermute x3, waiting for transfers between devices: 2.18 us -> 1.1 us  [exchanged(): return lax.ppermute(value, axis, pairs)]
  transfers between devices with their start and end apart: 9 -> 9, of which waited for: 5 -> 4; matrix products, arithmetic and copies ran while one was open for 0% -> 0% of each run, Pallas kernels for 16% -> 22%
where the time goes in v5:
time: 41 us; the launch traced here: 40.7 us
  starting transfers between devices  20.9 us (51%)
  Pallas kernels  12.8 us (31%)
  waiting for transfers between devices  5.59 us (14%)
  between operations  1.38 us (3%)
    pallas_call x9, Pallas kernels, call(): pl.pallas_call(kernel, out_shape=[jax.ShapeDtypeStruct(shape, kind) for s...  12.8 us
    ppermute x2, starting transfers between devices, passed_along(): return lax.ppermute(value, axis, pairs)  7.62 us
    all_to_all x2, starting transfers between devices, gathered(): everyone = lax.all_to_all(send, ('sub', 'crs'), 0, 0)  6.34 us
    all_to_all x2, waiting for transfers between devices, gathered(): everyone = lax.all_to_all(send, ('sub', 'crs'), 0, 0)  3.39 us
    ppermute x1, starting transfers between devices, per_device(): two = lax.ppermute(two, 'sub', rounds[1])  3.31 us
    ppermute x3, starting transfers between devices, exchanged(): return lax.ppermute(value, axis, pairs)  1.83 us
    ppermute x1, starting transfers between devices, per_device(): one = lax.ppermute(one, 'sub', rounds[0])  1.83 us
    ppermute x2, waiting for transfers between devices, passed_along(): return lax.ppermute(value, axis, pairs)  1.1 us
  transfers between devices with their start and end apart: 9, of which 4 were waited for; matrix products, arithmetic and copies ran while one was open for 0% of the time, Pallas kernels for 22%

profile of v5, /device:TPU:0, one launch (start us, length us, event | category | flops | bytes accessed | tf_op | source)
XLA Modules:
  0.0 40.7 jit_solution(16020993719034489153)
XLA Ops:
  1.3 1.1 %shard_map.104 = (f32[8,384]{1,0:T(8,128)S(1)}, f32[512,256]{1,0:T(8,128)S(1)}) custom-call(s32[1,1]{1,0:T(1,128)S(6)} %copy.13.live_ref, f32[6,1,384]{2,1,0:T(1,128)} %bitcast.7, f32[1,1,384]{2,1,0:T(1,128)} %scale_hbm.1, s32[1,1,384]{2,1,0:T(1,128)} %nbr_hbm.1, f32[1024,256]{1,0:T(8,128)} %inverse_hbm.3), custom_call_target="tpu_custom_call" | custom-call | tf_op jit(solution)/shard_map/pallas_call | solution.py:429
  2.4 3.0 %collective-permute-start = (f32[8,384]{1,0:T(8,128)S(1)}, f32[8,384]{1,0:T(8,128)S(1)}, u32[]{:S(2)}, u32[]{:S(2)}) collective-permute-start(f32[8,384]{1,0:T(8,128)S(1)} %get-tuple-element.41.pack_ref.refs_5_), channel_id=1, source_target_pairs={{0,4},{4,8},{8,12},{12,16},{16,20},{20,24},{24,28},{28,0},{1,5},{5... | collective-permute-start | bytes 36872 | tf_op jit(solution)/shard_map/ppermute | solution.py:444
  5.4 1.5 %collective-permute-start.1 = (f32[512,256]{1,0:T(8,128)S(1)}, f32[512,256]{1,0:T(8,128)S(1)}, u32[]{:S(2)}, u32[]{:S(2)}) collective-permute-start(f32[512,256]{1,0:T(8,128)S(1)} %get-tuple-element.51), channel_id=1, source_target_pairs={{0,2},{1,3},{2,0},{3,1},{4,6},{5,7},{6,4},{7,5},{8,10},{9,11},{10,... | collective-permute-start | bytes 1572872 | tf_op jit(solution)/shard_map/ppermute | solution.py:449
  6.9 2.1 %shard_map.105 = (bf16[768,768]{1,0:T(8,128)(2,1)S(1)}, bf16[768,768]{1,0:T(8,128)(2,1)S(1)}, bf16[32,768]{1,0:T(8,128)(2,1)S(1)}, bf16[32,768]{1,0:T(8,128)(2,1...) custom-call(f32[8,384]{1,0:T(8,128)S(1)} %get-tuple-element.41.pack_ref.refs_, ...), custom_call_target="tpu_custom_call" | custom-call | bytes 33554432 | tf_op jit(solution)/shard_map/pallas_call | solution.py:429
  9.1 1.1 %collective-permute-done.left_ref.refs_6_ = f32[8,384]{1,0:T(8,128)S(1)} collective-permute-done((f32[8,384]{1,0:T(8,128)S(1)}, f32[8,384]{1,0:T(8,128)S(1)}, u32[]{:S(2)}, u32[]{:S(2)}) %collective-permute-start) | collective-permute-done | bytes 12320 | tf_op jit(solution)/shard_map/ppermute | solution.py:444
  10.2 1.4 %shard_map.106 = (f32[32,2,128]{2,1,0:T(2,128)}, f32[32,384]{1,0:T(8,128)S(1)}, f32[32,384]{1,0:T(8,128)S(1)}, f32[32,384]{1,0:T(8,128)S(1)}, f32[32,384]{1,0:T(8,128)S(1)}, /*index=5*/s32[1,384]{1,0:T(1,128)S(1)}) custom-call(f32[8,384]{1,0:T(8,128)S(1)} %collective-permute-done.left_ref.refs_6_, f32[8,384]{1,0:T(8,128)S(1)} %get-tuple-element.41.pack_ref.refs_5_, ...), custom_call_target="tpu_custom_call" | custom-call | flops 40000000000 | bytes 1 | tf_op jit(solution)/shard_map/pallas_call | solution.py:429
  11.6 3.3 %all-to-all-start = ((f32[32,2,128]{2,1,0:T(2,128)}), f32[32,2,128]{2,1,0:T(2,128)S(1)}, u32[]{:S(2)}, u32[]{:S(2)}) async-start(f32[32,2,128]{2,1,0:T(2,128)} %get-tuple-element.50), calls=%async_computation | async-start | bytes 65536 | tf_op jit(solution)/shard_map/all_to_all | solution.py:527
  14.9 1.8 %collective-permute-start.3 = (f32[32,384]{1,0:T(8,128)S(1)}, f32[32,384]{1,0:T(8,128)S(1)}, u32[]{:S(2)}, u32[]{:S(2)}) collective-permute-start(f32[32,384]{1,0:T(8,128)S(1)} %get-tuple-element.60), channel_id=1, source_target_pairs={{0,4},{8,12},{16,20},{24,28},{4,0},{12,8},{20,16},{28,24},{1,5},{9... | collective-permute-start | bytes 147464 | tf_op jit(solution)/shard_map/ppermute | solution.py:566
  16.8 3.3 %collective-permute-start.4 = (f32[32,384]{1,0:T(8,128)S(1)}, f32[32,384]{1,0:T(8,128)S(1)}, u32[]{:S(2)}, u32[]{:S(2)}) collective-permute-start(f32[32,384]{1,0:T(8,128)S(1)} %get-tuple-element.61), channel_id=1, source_target_pairs={{4,8},{12,16},{20,24},{28,0},{8,4},{16,12},{24,20},{0,28},{5,9},{1... | collective-permute-start | bytes 147464 | tf_op jit(solution)/shard_map/ppermute | solution.py:565
  20.1 1.4 %shard_map.107 = (bf16[1024,256]{1,0:T(8,128)(2,1)S(1)}, bf16[1024,256]{1,0:T(8,128)(2,1)S(1)}) custom-call(f32[1024,256]{1,0:T(8,128)} %inverse_hbm.3), custom_call_target="tpu_custom_call" | custom-call | tf_op jit(solution)/shard_map/pallas_call | solution.py:429
  21.4 0.7 %all-to-all-done.all_ref = f32[32,2,128]{2,1,0:T(2,128)S(1)} async-done(((f32[32,2,128]{2,1,0:T(2,128)}), f32[32,2,128]{2,1,0:T(2,128)S(1)}, u32[]{:S(2)}, u32[]{:S(2)}) %all-to-all-start) | async-done | bytes 32800 | tf_op jit(solution)/shard_map/all_to_all | solution.py:527
  22.2 0.0 collective-permute-done.1.far_ref
  22.2 1.3 %shard_map.108 = (f32[8,1024]{1,0:T(8,128)S(1)}, f32[8,1024]{1,0:T(8,128)S(1)}, f32[8,128]{1,0:T(8,128)S(1)}, s32[8,128]{1,0:T(8,128)S(1)}, f32[384,768]{1,0:T(8,128)S(1)}) custom-call(f32[32,2,128]{2,1,0:T(2,128)S(1)} %all-to-all-done.all_ref, f32[512,256]{1,0:T(8,128)S(1)} %collective-permute-done.1.far_ref, ...), custom_call_target="tpu_custom_call" | custom-call | tf_op jit(solution)/shard_map/pallas_call | solution.py:429
  23.5 0.2 collective-permute-start.2
  23.6 1.4 %shard_map.109 = (bf16[768,768]{1,0:T(8,128)(2,1)S(1)}, bf16[768,768]{1,0:T(8,128)(2,1)S(1)}, bf16[768,384]{1,0:T(8,128)(2,1)S(1)}, bf16[768,384]{1,0:T(8,128)(2,1)S(1)}) custom-call(f32[384,768]{1,0:T(8,128)S(1)} %get-tuple-element.62.top_ref, s32[1,384]{1,0:T(1,128)S(1)} %get-tuple-element.63.left_index, s32[1,384]{1,0:T(1,128)S(1)} %get-tuple-element.49.own_ref, ...), custom_call_target="tpu_custom_call" | custom-call | tf_op jit(solution)/shard_map/pallas_call | solution.py:429
  25.1 0.0 collective-permute-done.3.refs_9_
  25.1 0.0 collective-permute-done.4.refs_10_
  25.1 0.0 collective-permute-done.2.refs_1_
  25.1 1.8 %shard_map.110 = (f32[32,2,128]{2,1,0:T(2,128)}, f32[8,384]{1,0:T(8,128)S(1)}, f32[16,384]{1,0:T(8,128)S(1)}, f32[128,384]{1,0:T(8,128)S(1)}, f32[8,128]{1,0:T(8,128)S(1)}) custom-call(f32[8,1024]{1,0:T(8,128)S(1)} %get-tuple-element.54.refs_0_, f32[8,1024]{1,0:T(8,128)S(1)} %collective-permute-done.2.refs_1_, f32[8,1024]{1,0:T(8,128)S(1)} %get-tuple-element.55.refs_2_, ...), custom_call_target="tpu_custom_call" | custom-call | tf_op jit(solution)/shard_map/pallas_call | solution.py:429
  27.0 3.0 %all-to-all-start.1 = ((f32[32,2,128]{2,1,0:T(2,128)}), f32[32,2,128]{2,1,0:T(2,128)S(1)}, u32[]{:S(2)}, u32[]{:S(2)}) async-start(f32[32,2,128]{2,1,0:T(2,128)} %get-tuple-element.68), calls=%async_computation.1 | async-start | bytes 65536 | tf_op jit(solution)/shard_map/all_to_all | solution.py:527
  30.0 4.6 %collective-permute-start.5 = (f32[8,384]{1,0:T(8,128)S(1)}, f32[8,384]{1,0:T(8,128)S(1)}, u32[]{:S(2)}, u32[]{:S(2)}) collective-permute-start(f32[8,384]{1,0:T(8,128)S(1)} %get-tuple-element.70), channel_id=1, source_target_pairs={{0,28},{4,0},{8,4},{12,8},{16,12},{20,16},{24,20},{28,24},{1,29},{... | collective-permute-start | bytes 36872 | tf_op jit(solution)/shard_map/ppermute | solution.py:444
  34.6 2.6 %all-to-all-done.1.all_ref = f32[32,2,128]{2,1,0:T(2,128)S(1)} async-done(((f32[32,2,128]{2,1,0:T(2,128)}), f32[32,2,128]{2,1,0:T(2,128)S(1)}, u32[]{:S(2)}, u32[]{:S(2)}) %all-to-all-start.1) | async-done | bytes 32800 | tf_op jit(solution)/shard_map/all_to_all | solution.py:527
  37.2 1.2 %shard_map.111 = (f32[8,1024]{1,0:T(8,128)S(1)}, f32[8,1024]{1,0:T(8,128)S(1)}, f32[8,128]{1,0:T(8,128)S(1)}, s32[8,128]{1,0:T(8,128)S(1)}) custom-call(f32[32,2,128]{2,1,0:T(2,128)S(1)} %all-to-all-done.1.all_ref, f32[512,256]{1,0:T(8,128)S(1)} %collective-permute-done.1.far_ref, bf16[1024,256]{1,0:T(8,128)(2,1)S(1)} %get-tuple-element.52.inv_high, ...), custom_call_target="tpu_custom_call" | custom-call | tf_op jit(solution)/shard_map/pallas_call | solution.py:429
  38.5 0.0 collective-permute-done.5.refs_6_
  38.5 0.2 collective-permute-start.6
  38.6 1.1 %collective-permute-done.6.refs_1_ = f32[8,1024]{1,0:T(8,128)S(1)} collective-permute-done((f32[8,1024]{1,0:T(8,128)S(1)}, f32[8,1024]{1,0:T(8,128)S(1)}, u32[]{:S(2)}, u32[]{:S(2)}) %collective-permute-start.6) | collective-permute-done | bytes 32800 | tf_op jit(solution)/shard_map/ppermute | solution.py:449
  39.7 0.9 %shard_map.112 = (f32[6,1,384]{2,1,0:T(1,128)}, f32[6,1,384]{2,1,0:T(1,128)}) custom-call(f32[8,1024]{1,0:T(8,128)S(1)} %get-tuple-element.71.refs_0_, f32[8,1024]{1,0:T(8,128)S(1)} %collective-permute-done.6.refs_1_, f32[8,1024]{1,0:T(8,128)S(1)} %get-tuple-element.72.refs_2_, f32[8,128]{1,0:T(8,128)S(1)} %get-tuple-element.73.refs_3_, ...), custom_call_target="tpu_custom_call" | custom-call | tf_op jit(solution)/shard_map/pallas_call | solution.py:429
Async XLA Ops:
  2.4 7.7 %collective-permute-start = (f32[8,384]{1,0:T(8,128)S(1)}, f32[8,384]{1,0:T(8,128)S(1)}, u32[]{:S(2)}, u32[]{:S(2)}) collective-permute-start(f32[8,384]{1,0:T(8,128)S(1)} %get-tuple-element.41.pack_ref.refs_5_), channel_id=1, source_target_pairs={{0,4},{4,8},{8,12},{12,16},{16,20},{20,24},{24,28},{28,0},{1,5},{5... | collective-permute-start | bytes 36872 | tf_op jit(solution)/shard_map/ppermute | solution.py:444
  5.4 16.7 %collective-permute-start.1 = (f32[512,256]{1,0:T(8,128)S(1)}, f32[512,256]{1,0:T(8,128)S(1)}, u32[]{:S(2)}, u32[]{:S(2)}) collective-permute-start(f32[512,256]{1,0:T(8,128)S(1)} %get-tuple-element.51), channel_id=1, source_target_pairs={{0,2},{1,3},{2,0},{3,1},{4,6},{5,7},{6,4},{7,5},{8,10},{9,11},{10,... | collective-permute-start | bytes 1572872 | tf_op jit(solution)/shard_map/ppermute | solution.py:449
  11.6 10.6 %all-to-all-start = ((f32[32,2,128]{2,1,0:T(2,128)}), f32[32,2,128]{2,1,0:T(2,128)S(1)}, u32[]{:S(2)}, u32[]{:S(2)}) async-start(f32[32,2,128]{2,1,0:T(2,128)} %get-tuple-element.50), calls=%async_computation | async-start | bytes 65536 | tf_op jit(solution)/shard_map/all_to_all | solution.py:527
  14.9 10.2 %collective-permute-start.3 = (f32[32,384]{1,0:T(8,128)S(1)}, f32[32,384]{1,0:T(8,128)S(1)}, u32[]{:S(2)}, u32[]{:S(2)}) collective-permute-start(f32[32,384]{1,0:T(8,128)S(1)} %get-tuple-element.60), channel_id=1, source_target_pairs={{0,4},{8,12},{16,20},{24,28},{4,0},{12,8},{20,16},{28,24},{1,5},{9... | collective-permute-start | bytes 147464 | tf_op jit(solution)/shard_map/ppermute | solution.py:566
  16.8 8.3 %collective-permute-start.4 = (f32[32,384]{1,0:T(8,128)S(1)}, f32[32,384]{1,0:T(8,128)S(1)}, u32[]{:S(2)}, u32[]{:S(2)}) collective-permute-start(f32[32,384]{1,0:T(8,128)S(1)} %get-tuple-element.61), channel_id=1, source_target_pairs={{4,8},{12,16},{20,24},{28,0},{8,4},{16,12},{24,20},{0,28},{5,9},{1... | collective-permute-start | bytes 147464 | tf_op jit(solution)/shard_map/ppermute | solution.py:565
  23.5 1.6 %collective-permute-start.2 = (f32[8,1024]{1,0:T(8,128)S(1)}, f32[8,1024]{1,0:T(8,128)S(1)}, u32[]{:S(2)}, u32[]{:S(2)}) collective-permute-start(f32[8,1024]{1,0:T(8,128)S(1)} %get-tuple-element.54.refs_0_), channel_id=1, source_target_pairs={{0,1},{1,0},{2,3},{3,2},{4,5},{5,4},{6,7},{7,6},{8,9},{9,8},{10,11... | collective-permute-start | bytes 98312 | tf_op jit(solution)/shard_map/ppermute | solution.py:449
  27.0 10.3 %all-to-all-start.1 = ((f32[32,2,128]{2,1,0:T(2,128)}), f32[32,2,128]{2,1,0:T(2,128)S(1)}, u32[]{:S(2)}, u32[]{:S(2)}) async-start(f32[32,2,128]{2,1,0:T(2,128)} %get-tuple-element.68), calls=%async_computation.1 | async-start | bytes 65536 | tf_op jit(solution)/shard_map/all_to_all | solution.py:527
  30.0 8.5 %collective-permute-start.5 = (f32[8,384]{1,0:T(8,128)S(1)}, f32[8,384]{1,0:T(8,128)S(1)}, u32[]{:S(2)}, u32[]{:S(2)}) collective-permute-start(f32[8,384]{1,0:T(8,128)S(1)} %get-tuple-element.70), channel_id=1, source_target_pairs={{0,28},{4,0},{8,4},{12,8},{16,12},{20,16},{24,20},{28,24},{1,29},{... | collective-permute-start | bytes 36872 | tf_op jit(solution)/shard_map/ppermute | solution.py:444
  38.5 1.3 %collective-permute-start.6 = (f32[8,1024]{1,0:T(8,128)S(1)}, f32[8,1024]{1,0:T(8,128)S(1)}, u32[]{:S(2)}, u32[]{:S(2)}) collective-permute-start(f32[8,1024]{1,0:T(8,128)S(1)} %get-tuple-element.71.refs_0_), channel_id=1, source_target_pairs={{0,1},{1,0},{2,3},{3,2},{4,5},{5,4},{6,7},{7,6},{8,9},{9,8},{10,11... | collective-permute-start | bytes 98312 | tf_op jit(solution)/shard_map/ppermute | solution.py:449

commit v6 on v5

--- a/solution.py
+++ b/solution.py
@@ -30,15 +30,31 @@
     return lax.dot_general(a, b, dims, preferred_element_type=F32)
 
 
-def moved(a, chosen, transposed=False):
+def exact(a, chosen, count, transposed=False):
     rows = a.shape[0]
-    all_parts = dot(jnp.concatenate(parts(a, 3), axis=0), chosen, transposed)
-    return all_parts[:rows] + all_parts[rows : 2 * rows] + all_parts[2 * rows :]
-
-
-def moved_parts(high, low, chosen):
-    both = dot(jnp.concatenate([high, low], axis=0), chosen)
-    return both[: high.shape[0]] + both[high.shape[0] :]
+    all_parts = dot(jnp.concatenate(parts(a, count), axis=0), chosen, transposed)
+    return sum(all_parts[i * rows : (i + 1) * rows] for i in range(count))
+
+
+def lows(index):
+    rows = lax.broadcasted_iota(jnp.int32, (LANES, index.shape[1]), 0)
+    return jnp.where(rows == (index & (LANES - 1)), 1.0, 0.0).astype(BF16)
+
+
+def added_up(a, index, size):
+    rows = a.shape[0]
+    high = index >> 7
+    stacked = [jnp.where(high == h, a, 0.0) for h in range(size // LANES)]
+    out = exact(jnp.concatenate(stacked, axis=0), lows(index), 2, True)
+    return jnp.concatenate([out[h * rows : (h + 1) * rows] for h in range(size // LANES)], axis=1)
+
+
+def taken(a, index):
+    rows, size = a.shape
+    high = index >> 7
+    stacked = [a[:, h * LANES : (h + 1) * LANES] for h in range(size // LANES)]
+    out = exact(jnp.concatenate(stacked, axis=0), lows(index), 2)
+    return sum(jnp.where(high == h, out[h * rows : (h + 1) * rows], 0.0) for h in range(size // LANES))
 
 
 def product(a, high, low, transposed=False):
@@ -46,12 +62,6 @@
     top, rest = parts(a, 2)
     both = dot(jnp.concatenate([top, rest], axis=0), high, transposed)
     return both[:rows] + both[rows:] + dot(top, low, transposed)
-
-
-def chosen_columns(index, count):
-    shape = (count, index.shape[1])
-    rows = lax.broadcasted_iota(jnp.int32, shape, 0)
-    return jnp.where(rows == index, 1.0, 0.0).astype(BF16)
 
 
 def row_sum(x):
@@ -129,6 +139,23 @@
     return jnp.where(even, right, left), jnp.where(even, left, right)
 
 
+PIECES = 6
+
+
+def pieces(source, target, count):
+    rows = source.shape[2] // count
+    at = [(0, 0, pl.ds(i * rows, rows)) for i in range(count)]
+    return [(source.at[i], target.at[i]) for i in at]
+
+
+def split_as_it_comes(copies, whole, high, low, first):
+    rows = whole.shape[2] // len(copies)
+    for i in range(first // rows, (first + high.shape[0]) // rows):
+        copies[i].wait()
+        at = slice(i * rows - first, (i + 1) * rows - first)
+        high[at], low[at] = parts(whole[0, 0, i * rows : (i + 1) * rows], 2)
+
+
 def half_of(slab, inverse_hbm):
     rows = 2 * inverse_hbm.shape[1]
     first = jnp.minimum(slab // 2 * rows, inverse_hbm.shape[0] - rows)
@@ -137,7 +164,7 @@
 
 def prepare_kernel(
     cases, pack_ref, schur_hbm, coupling_hbm, own_hbm, corner_hbm,
-    s_high, s_low, c_high, c_low, own_coupling, load_ref, index_ref, own_ref,
+    top_high, top_low, s_high, s_low, c_high, c_low, own_coupling, load_ref, index_ref, own_ref,
     schur, coupling, own, corner, sems,
 ):
     copies = fetched(
@@ -145,7 +172,7 @@
             (own_hbm, own),
             (coupling_hbm, coupling),
             (corner_hbm, corner),
-            (schur_hbm, schur),
+            *pieces(schur_hbm, schur, PIECES),
         ],
         sems,
     )
@@ -154,17 +181,16 @@
     held, iface = coupling.shape[2:]
     block = padded(coupling[0, 0], SLOT)
     c_high[...], c_low[...] = parts(block, 2)
-    chosen = chosen_columns(own[0], iface)
     own_ref[...] = own[0]
-    own_coupling[...] = moved_parts(c_high[...], c_low[...], chosen)[:held]
+    own_coupling[...] = taken(block, own[0])[:held]
     residual, scale, _ = unpacked(pack_ref[...], cases)
-    load_ref[...] = moved(residual * scale, chosen, True)
+    load_ref[...] = added_up(residual * scale, own[0], iface)
     lane = lax.broadcasted_iota(jnp.int32, (held, LANES), 1) % SLOT
     tiles = jnp.where(lane == lax.broadcasted_iota(jnp.int32, (held, LANES), 0), 1.0, 0.0)
     index = jnp.broadcast_to(corner[0].astype(F32), (ROWS, held))
-    index_ref[...] = jnp.where(lane[:1] < held, moved(index, tiles.astype(BF16))[:1], -1.0)
-    copies[3].wait()
-    s_high[...], s_low[...] = parts(schur[0, 0], 2)
+    index_ref[...] = jnp.where(lane[:1] < held, exact(index, tiles.astype(BF16), 2)[:1], -1.0)
+    split_as_it_comes(copies[3:], schur, top_high, top_low, 0)
+    split_as_it_comes(copies[3:], schur, s_high, s_low, top_high.shape[0])
 
 
 def inverse_kernel(inverse_hbm, inv_high, inv_low, inverse, sems):
@@ -178,18 +204,23 @@
     inv_high[...], inv_low[...] = parts(inverse[...], 2)
 
 
-def terms_kernel(top_ref, left_index, own_ref, schur_hbm, s_high, s_low, own_map, left_map, rest, sems):
-    rows, iface = top_ref.shape
-    (copy,) = fetched([(schur_hbm.at[0, 0, pl.ds(rows, iface - rows)], rest)], sems)
+def terms_kernel(rows_ref, schur_hbm, s_high, s_low, rest, sems):
+    rows, left = rows_ref.shape[0], rest.shape[0]
+    size = schur_hbm.shape[2]
+    (copy,) = fetched([(schur_hbm.at[0, 0, pl.ds(size - left, left)], rest)], sems)
 
     @always
     def _():
-        s_high[:rows], s_low[:rows] = parts(top_ref[...], 2)
-        own_map[...] = chosen_columns(own_ref[...], iface)
-        left_map[...] = chosen_columns(left_index[...], iface)
+        s_high[:rows], s_low[:rows] = parts(rows_ref[...], 2)
 
     copy.wait()
     s_high[rows:], s_low[rows:] = parts(rest[...], 2)
+
+
+def schur_product(load, top_high, top_low, s_high, s_low):
+    rows = top_high.shape[0]
+    top = product(load[:, :rows], top_high[...], top_low[...])
+    return top + product(load[:, rows:], s_high[...], s_low[...])
 
 
 def forces(load, through, first, c_high, c_low, index_ref, cases, send_hbm, send, sems):
@@ -220,26 +251,28 @@
 
 def first_kernel(
     cases, left_ref, pack_ref, load_ref, own_coupling, index_ref,
-    s_high, s_low, c_high, c_low, own_ref,
-    send_hbm, right_ref, back_ref, one_ref, two_ref, index_out, send, sems,
+    top_high, top_low, s_high, s_low, c_high, c_low, own_ref,
+    send_hbm, one_ref, two_ref, index_out, send, sems,
 ):
     left_residual, left_scale, left_index = unpacked(left_ref[...], cases)
     index_out[...] = left_index
-    chosen = chosen_columns(left_index, load_ref.shape[1])
-    load = load_ref[...] - moved(left_residual * left_scale, chosen, True)
-    through = product(load, s_high[...], s_low[...])
+    iface = load_ref.shape[1]
+    load = load_ref[...] - added_up(left_residual * left_scale, left_index, iface)
+    through = schur_product(load, top_high, top_low, s_high, s_low)
     residual, scale, _ = unpacked(pack_ref[...], cases)
     norm = row_sum(residual * residual * scale)
     copy = forces(load, through, norm, c_high, c_low, index_ref, cases, send_hbm, send, sems)
 
     @always
     def _():
-        right_ref[:ROWS] = moved(through, chosen_columns(own_ref[...], load_ref.shape[1]))
-        right_ref[ROWS:] = own_coupling[...]
-        back_ref[:ROWS] = moved(through, chosen)
         held = own_coupling.shape[0]
-        back_ref[ROWS:] = moved_parts(c_high[...], c_low[...], chosen)[:held]
-        one_ref[...], two_ref[...] = dealt(right_ref[...], back_ref[...])
+        one_ref[:ROWS], two_ref[:ROWS] = dealt(
+            taken(through, own_ref[...]), taken(through, left_index)
+        )
+        coupling = c_high[...].astype(F32) + c_low[...].astype(F32)
+        one_ref[ROWS:], two_ref[ROWS:] = dealt(
+            own_coupling[...], taken(coupling, left_index)[:held]
+        )
 
     copy.wait()
 
@@ -248,7 +281,6 @@
     devices = all_ref.shape[0]
     chunk = min(devices, LANES // GROUP)
     row = lax.broadcasted_iota(jnp.int32, (ROWS, 1), 0)
-    step = min(corners, 1024)
 
     def add(at):
         pieces = [
@@ -261,11 +293,7 @@
         flat = jnp.concatenate(pieces, axis=1)
         index = flat[cases : cases + 1].astype(jnp.int32) ^ flip
         force = jnp.where(row < cases, flat, 0.0)
-        total = [
-            moved(force, chosen_columns(index - start, step), True)
-            for start in range(0, corners, step)
-        ]
-        return sums, jnp.concatenate(total, axis=1)
+        return sums, added_up(force, index, corners)
 
     sums_ref[...], total_ref[...] = add(0)
     if devices > chunk:
@@ -302,9 +330,12 @@
 
 
 def pair_kernel(
-    cases, all_ref, far_ref, inv_high, inv_low, schur_hbm, x_ref, total_ref, sums_ref, index_ref, *later,
+    cases, first_row, all_ref, far_ref, inv_high, inv_low, schur_hbm, x_ref, total_ref, sums_ref, index_ref, *later,
 ):
-    copies = fetched([(schur_hbm.at[0, 0, : later[0].shape[0]], later[0])], later[1]) if later else []
+    copies = []
+    if later:
+        rows, sems = later
+        copies = fetched([(schur_hbm.at[0, 0, pl.ds(first_row, rows.shape[0])], rows)], sems)
     width = inv_high.shape[1]
     slab = lax.axis_index("crs")
     flip = slab * width
@@ -342,26 +373,27 @@
 
 def second_kernel(cases, coarse, given, *refs):
     (
-        pack_ref, left_ref, right_ref, back_ref, one_ref, two_ref,
-        s_high, s_low, own_map, left_map, c_high, c_low, corner_ref,
+        pack_ref, left_ref, one_sent, two_sent, one_ref, two_ref,
+        top_high, top_low, s_high, s_low, own_ref, left_index, c_high, c_low, corner_ref,
         send_hbm, out_ref, keep_ref, spread_ref, scalar_ref, send, sems,
-    ) = refs[given : given + 20]
-    solution, total, sums, index = coarse(refs[:given] + refs[given + 20 :])
-    picked = moved(solution, chosen_columns(index, solution.shape[1]))
+    ) = refs[given : given + 22]
+    solution, total, sums, index = coarse(refs[:given] + refs[given + 22 :])
+    picked = taken(solution, index)
+    right, back = dealt(one_sent[...], two_sent[...])
     from_right, from_left = dealt(one_ref[...], two_ref[...])
-    blank = jnp.zeros((SLOT - (right_ref.shape[0] - ROWS), right_ref.shape[1]), F32)
-    none = jnp.zeros((SLOT, right_ref.shape[1]), F32)
-    own = jnp.concatenate([none, right_ref[ROWS:], blank, -from_right[ROWS:], blank, none], axis=0)
-    other = jnp.concatenate([from_left[ROWS:], blank, -back_ref[ROWS:], blank, none, none], axis=0)
+    blank = jnp.zeros((SLOT - (right.shape[0] - ROWS), right.shape[1]), F32)
+    none = jnp.zeros((SLOT, right.shape[1]), F32)
+    own = jnp.concatenate([none, right[ROWS:], blank, -from_right[ROWS:], blank, none], axis=0)
+    other = jnp.concatenate([from_left[ROWS:], blank, -back[ROWS:], blank, none, none], axis=0)
     spread_ref[...] = own
     both = product(picked, *parts(jnp.concatenate([own, other], axis=1), 2))
-    records = right_ref.shape[1]
+    records = right.shape[1]
     residual, scale, _ = unpacked(pack_ref[...], cases)
     left_residual, left_scale, _ = unpacked(left_ref[...], cases)
     live = (scale > 0.0).astype(F32)
     left_live = (left_scale > 0.0).astype(F32)
-    image = (right_ref[:ROWS] - from_right[:ROWS] + both[:, :records]) * live
-    left_image = (from_left[:ROWS] - back_ref[:ROWS] + both[:, records:]) * left_live
+    image = (right[:ROWS] - from_right[:ROWS] + both[:, :records]) * live
+    left_image = (from_left[:ROWS] - back[:ROWS] + both[:, records:]) * left_live
     norm = column(sums, SLOT - 2)
     curvature = column(sums, SLOT - 1) + row_sum(total * solution)
     row = lax.broadcasted_iota(jnp.int32, (ROWS, 1), 0)
@@ -370,15 +402,16 @@
     left_residual = left_residual - alpha * left_image
     precon = scale * residual
     left_precon = left_scale * left_residual
-    load = moved(precon, own_map[...], True) - moved(left_precon, left_map[...], True)
-    through = product(load, s_high[...], s_low[...])
+    iface = c_high.shape[1]
+    load = added_up(precon, own_ref[...], iface) - added_up(left_precon, left_index[...], iface)
+    through = schur_product(load, top_high, top_low, s_high, s_low)
     norm_here = row_sum(residual * precon)
     copy = forces(load, through, norm_here, c_high, c_low, corner_ref, cases, send_hbm, send, sems)
 
     @always
     def _():
-        out_ref[...] = moved(through, left_map[...])
-        keep_ref[:ROWS] = moved(through, own_map[...])
+        out_ref[...] = taken(through, left_index[...])
+        keep_ref[:ROWS] = taken(through, own_ref[...])
         keep_ref[ROWS:] = image
         lane = lax.broadcasted_iota(jnp.int32, scalar_ref.shape, 1)
         scalar_ref[...] = jnp.where(lane == 0, norm, alpha)
@@ -391,7 +424,7 @@
         pack_ref, from_right, keep_ref, spread_ref, scalar_ref, multipliers_ref, residual_ref,
     ) = refs[given : given + 7]
     solution, total, sums, index = coarse(refs[:given] + refs[given + 7 :])
-    picked = moved(solution, chosen_columns(index, solution.shape[1]))
+    picked = taken(solution, index)
     residual, scale, _ = unpacked(pack_ref[...], cases)
     live = (scale > 0.0).astype(F32)
     spread = product(picked, *parts(spread_ref[...], 2))
@@ -484,11 +517,14 @@
         far = exchanged(half, "crs", 2)
     left = passed_along(pack, "sub", 1)
     fetched_here = (schur_inverse, coarse_coupling, own_dof, corner_index)
-    s_high, s_low, c_high, c_low, own_coupling, load, index, own = call(
+    top = iface // 3 // LANES * LANES
+    *tops, s_high, s_low, c_high, c_low, own_coupling, load, index, own = call(
         functools.partial(prepare_kernel, cases),
         [
-            ((iface, iface), BF16),
-            ((iface, iface), BF16),
+            ((top, iface), BF16),
+            ((top, iface), BF16),
+            ((iface - top, iface), BF16),
+            ((iface - top, iface), BF16),
             ((SLOT, iface), BF16),
             ((SLOT, iface), BF16),
             ((held, records), F32),
@@ -498,7 +534,7 @@
         ],
         (pack, *fetched_here),
         [VM] + [HB] * 4,
-        buffers(*fetched_here),
+        [*buffers(*fetched_here)[:-1], pltpu.SemaphoreType.DMA((3 + PIECES,))],
         32 << 20,
     )
     inv_high, inv_low = call(
@@ -509,19 +545,19 @@
         [pltpu.VMEM((corners, width), F32), pltpu.SemaphoreType.DMA((slabs,))],
     )
     outgoing = [pltpu.VMEM((devices, FOLD, LANES), F32), pltpu.SemaphoreType.DMA((1,))]
-    send, right, back, one, two, left_index = call(
+    send, one_sent, two_sent, left_index = call(
         functools.partial(first_kernel, cases),
         [((devices, FOLD, LANES), F32)]
-        + [((ROWS + held, records), F32)] * 4
+        + [((ROWS + held, records), F32)] * 2
         + [((1, records), jnp.int32)],
-        (left, pack, load, own_coupling, index, s_high, s_low, c_high, c_low, own),
+        (left, pack, load, own_coupling, index, *tops, s_high, s_low, c_high, c_low, own),
         [],
         outgoing,
         -1,
         stored=1,
     )
 
-    top = (iface // 16 * 8, iface)
+    more = iface // 64 * 16
 
     def gathered(send, beside, ahead):
         everyone = lax.all_to_all(send, ("sub", "crs"), 0, 0)
@@ -529,8 +565,8 @@
         outs = [(row, F32), ((ROWS, LANES), F32), ((ROWS, LANES), jnp.int32)]
         if is_paired(width):
             x, total, sums, near, *fetched = call(
-                functools.partial(pair_kernel, cases),
-                [(row, F32), *outs] + [(top, F32)] * ahead,
+                functools.partial(pair_kernel, cases, top),
+                [(row, F32), *outs] + [((more, iface), F32)] * ahead,
                 (everyone, far, inv_high, inv_low, schur_inverse),
                 [VM] * 4 + [HB],
                 [pltpu.SemaphoreType.DMA((1,))] * ahead,
@@ -556,23 +592,23 @@
             [VM] * (len(pieces) + len(others)),
             [pltpu.VMEM(row, F32)],
             functools.partial(shared_coarse, cases, width),
-            *[schur_inverse[0, 0, : top[0]]] * ahead,
+            *[schur_inverse[0, 0, top : top + more]] * ahead,
         )
 
     if by_turns(chain):
         rounds = [[(c, (c + 1) % chain) for c in range(start, chain, 2)] for start in (0, 1)]
         rounds = [pairs + [(b, a) for a, b in pairs] for pairs in rounds]
-        two = lax.ppermute(two, "sub", rounds[1])
-        one = lax.ppermute(one, "sub", rounds[0])
+        two = lax.ppermute(two_sent, "sub", rounds[1])
+        one = lax.ppermute(one_sent, "sub", rounds[0])
     else:
-        one, two = passed_along(two, "sub", -1), passed_along(one, "sub", 1)
+        one, two = passed_along(two_sent, "sub", -1), passed_along(one_sent, "sub", 1)
     given, specs, scratch, coarse, first_rows = gathered(send, None, 1)
     terms = call(
         terms_kernel,
-        [((iface, iface), BF16)] * 2 + [((iface, records), BF16)] * 2,
-        (first_rows, left_index, own, schur_inverse),
-        [VM] * 3 + [HB],
-        [pltpu.VMEM((iface - top[0], iface), F32), pltpu.SemaphoreType.DMA((1,))],
+        [((iface - top, iface), BF16)] * 2,
+        (first_rows, schur_inverse),
+        [VM, HB],
+        [pltpu.VMEM((iface - top - more, iface), F32), pltpu.SemaphoreType.DMA((1,))],
     )
     send, out, keep, spread, scalars = call(
         functools.partial(second_kernel, cases, coarse, len(given)),
@@ -584,8 +620,8 @@
             ((ROWS, LANES), F32),
         ],
         (
-            *given, pack, left, right, back, one, two,
-            *terms, c_high, c_low, index,
+            *given, pack, left, one_sent, two_sent, one, two,
+            *tops, *terms, own, left_index, c_high, c_low, index,
         ),
         specs,
         outgoing + scratch,

time: 41 us -> 40.3 us (0.983)
  Pallas kernels: 12.8 us -> 11.4 us
    pallas_call x9, Pallas kernels: 12.8 us -> 11.4 us  [call(): pl.pallas_call(kernel, out_shape=[jax.ShapeDtypeStruct(shape, kind) for s...]
  transfers between devices with their start and end apart: 9 -> 9, of which waited for: 4 -> 4; matrix products, arithmetic and copies ran while one was open for 0% -> 0% of each run, Pallas kernels for 22% -> 19%
where the time goes in v6:
time: 40.3 us; the launch traced here: 39.9 us
  starting transfers between devices  21.2 us (53%)
  Pallas kernels  11.4 us (28%)
  waiting for transfers between devices  5.91 us (15%)
  between operations  1.38 us (3%)
    pallas_call x9, Pallas kernels, call(): pl.pallas_call(kernel, out_shape=[jax.ShapeDtypeStruct(shape, kind) for s...  11.4 us
    ppermute x2, starting transfers between devices, passed_along(): return lax.ppermute(value, axis, pairs)  7.62 us
    all_to_all x2, starting transfers between devices, gathered(): everyone = lax.all_to_all(send, ('sub', 'crs'), 0, 0)  6.64 us
    all_to_all x2, waiting for transfers between devices, gathered(): everyone = lax.all_to_all(send, ('sub', 'crs'), 0, 0)  3.39 us
    ppermute x1, starting transfers between devices, per_device(): two = lax.ppermute(two_sent, 'sub', rounds[1])  3.31 us
    ppermute x1, starting transfers between devices, per_device(): one = lax.ppermute(one_sent, 'sub', rounds[0])  1.83 us
    ppermute x3, starting transfers between devices, exchanged(): return lax.ppermute(value, axis, pairs)  1.81 us
    ppermute x2, waiting for transfers between devices, passed_along(): return lax.ppermute(value, axis, pairs)  1.42 us
  transfers between devices with their start and end apart: 9, of which 4 were waited for; matrix products, arithmetic and copies ran while one was open for 0% of the time, Pallas kernels for 19%

profile of v6, /device:TPU:0, one launch (start us, length us, event | category | flops | bytes accessed | tf_op | source)
XLA Modules:
  0.0 39.9 jit_solution(9601001198912337118)
XLA Ops:
  1.3 1.1 %shard_map.104 = (f32[8,384]{1,0:T(8,128)S(1)}, f32[512,256]{1,0:T(8,128)S(1)}) custom-call(s32[1,1]{1,0:T(1,128)S(6)} %copy.13.live_ref, f32[6,1,384]{2,1,0:T(1,128)} %bitcast.7, f32[1,1,384]{2,1,0:T(1,128)} %scale_hbm.1, s32[1,1,384]{2,1,0:T(1,128)} %nbr_hbm.1, f32[1024,256]{1,0:T(8,128)} %inverse_hbm.3), custom_call_target="tpu_custom_call" | custom-call | tf_op jit(solution)/shard_map/pallas_call | solution.py:462
  2.4 3.0 %collective-permute-start = (f32[8,384]{1,0:T(8,128)S(1)}, f32[8,384]{1,0:T(8,128)S(1)}, u32[]{:S(2)}, u32[]{:S(2)}) collective-permute-start(f32[8,384]{1,0:T(8,128)S(1)} %get-tuple-element.39.pack_ref.refs_5_), channel_id=1, source_target_pairs={{0,4},{4,8},{8,12},{12,16},{16,20},{20,24},{24,28},{28,0},{1,5},{5... | collective-permute-start | bytes 36872 | tf_op jit(solution)/shard_map/ppermute | solution.py:477
  5.4 1.5 %collective-permute-start.1 = (f32[512,256]{1,0:T(8,128)S(1)}, f32[512,256]{1,0:T(8,128)S(1)}, u32[]{:S(2)}, u32[]{:S(2)}) collective-permute-start(f32[512,256]{1,0:T(8,128)S(1)} %get-tuple-element.51), channel_id=1, source_target_pairs={{0,2},{1,3},{2,0},{3,1},{4,6},{5,7},{6,4},{7,5},{8,10},{9,11},{10,... | collective-permute-start | bytes 1572872 | tf_op jit(solution)/shard_map/ppermute | solution.py:482
  6.9 1.8 %shard_map.105 = (bf16[256,768]{1,0:T(8,128)(2,1)S(1)}, bf16[256,768]{1,0:T(8,128)(2,1)S(1)}, bf16[512,768]{1,0:T(8,128)(2,1)S(1)}, bf16[512,768]{1,0:T(8,128)(2...) custom-call(f32[8,384]{1,0:T(8,128)S(1)} %get-tuple-element.39.pack_, ...), custom_call_target="tpu_custom_call" | custom-call | bytes 33554432 | tf_op jit(solution)/shard_map/pallas_call | solution.py:462
  8.7 1.4 %collective-permute-done.left_ref.refs_6_ = f32[8,384]{1,0:T(8,128)S(1)} collective-permute-done((f32[8,384]{1,0:T(8,128)S(1)}, f32[8,384]{1,0:T(8,128)S(1)}, u32[]{:S(2)}, u32[]{:S(2)}) %collective-permute-start) | collective-permute-done | bytes 12320 | tf_op jit(solution)/shard_map/ppermute | solution.py:477
  10.2 1.3 %shard_map.106 = (f32[32,2,128]{2,1,0:T(2,128)}, f32[32,384]{1,0:T(8,128)S(1)}, f32[32,384]{1,0:T(8,128)S(1)}, s32[1,384]{1,0:T(1,128)S(1)}) custom-call(f32[8,384]{1,0:T(8,128)S(1)} %collective-permute-done.left_ref.refs_6_, f32[8,384]{1,0:T(8,128)S(1)} %get-tuple-element.39.pack_ref.refs_5_, f32[8,768]{1,0:T(8,128)S(1)} %get-tuple-element.40.load_ref, ...), custom_call_target="tpu_custom_call" | custom-call | flops 40000000000 | bytes 1 | tf_op jit(solution)/shard_map/pallas_call | solution.py:462
  11.5 3.3 %all-to-all-start = ((f32[32,2,128]{2,1,0:T(2,128)}), f32[32,2,128]{2,1,0:T(2,128)S(1)}, u32[]{:S(2)}, u32[]{:S(2)}) async-start(f32[32,2,128]{2,1,0:T(2,128)} %get-tuple-element.50), calls=%async_computation | async-start | bytes 65536 | tf_op jit(solution)/shard_map/all_to_all | solution.py:563
  14.8 1.8 %collective-permute-start.3 = (f32[32,384]{1,0:T(8,128)S(1)}, f32[32,384]{1,0:T(8,128)S(1)}, u32[]{:S(2)}, u32[]{:S(2)}) collective-permute-start(f32[32,384]{1,0:T(8,128)S(1)} %get-tuple-element.58.refs_7_), channel_id=1, source_target_pairs={{0,4},{8,12},{16,20},{24,28},{4,0},{12,8},{20,16},{28,24},{1,5},{9... | collective-permute-start | bytes 147464 | tf_op jit(solution)/shard_map/ppermute | solution.py:602
  16.6 3.3 %collective-permute-start.4 = (f32[32,384]{1,0:T(8,128)S(1)}, f32[32,384]{1,0:T(8,128)S(1)}, u32[]{:S(2)}, u32[]{:S(2)}) collective-permute-start(f32[32,384]{1,0:T(8,128)S(1)} %get-tuple-element.59.refs_8_), channel_id=1, source_target_pairs={{4,8},{12,16},{20,24},{28,0},{8,4},{16,12},{24,20},{0,28},{5,9},{1... | collective-permute-start | bytes 147464 | tf_op jit(solution)/shard_map/ppermute | solution.py:601
  20.0 1.4 %shard_map.107 = (bf16[1024,256]{1,0:T(8,128)(2,1)S(1)}, bf16[1024,256]{1,0:T(8,128)(2,1)S(1)}) custom-call(f32[1024,256]{1,0:T(8,128)} %inverse_hbm.3), custom_call_target="tpu_custom_call" | custom-call | tf_op jit(solution)/shard_map/pallas_call | solution.py:462
  21.3 0.7 %all-to-all-done.all_ref = f32[32,2,128]{2,1,0:T(2,128)S(1)} async-done(((f32[32,2,128]{2,1,0:T(2,128)}), f32[32,2,128]{2,1,0:T(2,128)S(1)}, u32[]{:S(2)}, u32[]{:S(2)}) %all-to-all-start) | async-done | bytes 32800 | tf_op jit(solution)/shard_map/all_to_all | solution.py:563
  22.1 0.0 collective-permute-done.1.far_ref
  22.1 1.1 %shard_map.108 = (f32[8,1024]{1,0:T(8,128)S(1)}, f32[8,1024]{1,0:T(8,128)S(1)}, f32[8,128]{1,0:T(8,128)S(1)}, s32[8,128]{1,0:T(8,128)S(1)}, f32[192,768]{1,0:T(8,128)S(1)}) custom-call(f32[32,2,128]{2,1,0:T(2,128)S(1)} %all-to-all-done.all_ref, f32[512,256]{1,0:T(8,128)S(1)} %collective-permute-done.1.far_ref, ...), custom_call_target="tpu_custom_call" | custom-call | tf_op jit(solution)/shard_map/pallas_call | solution.py:462
  23.1 0.2 collective-permute-start.2
  23.3 1.3 %shard_map.109 = (bf16[512,768]{1,0:T(8,128)(2,1)S(1)}, bf16[512,768]{1,0:T(8,128)(2,1)S(1)}) custom-call(f32[192,768]{1,0:T(8,128)S(1)} %get-tuple-element.60.rows_ref, f32[1,1,768,768]{3,2,1,0:T(8,128)} %schur_hbm.7), custom_call_target="tpu_custom_call" | custom-call | tf_op jit(solution)/shard_map/pallas_call | solution.py:462
  24.7 0.0 collective-permute-done.3.refs_9_
  24.7 0.0 collective-permute-done.4.refs_10_
  24.7 0.0 collective-permute-done.2.refs_1_
  24.7 1.6 %shard_map.110 = (f32[32,2,128]{2,1,0:T(2,128)}, f32[8,384]{1,0:T(8,128)S(1)}, f32[16,384]{1,0:T(8,128)S(1)}, f32[128,384]{1,0:T(8,128)S(1)}, f32[8,128]{1,0:T(8,128)S(1)}) custom-call(f32[8,1024]{1,0:T(8,128)S(1)} %get-tuple-element.54.refs_0_, f32[8,1024]{1,0:T(8,128)S(1)} %collective-permute-done.2.refs_1_, f32[8,1024]{1,0:T(8,128)S(1)} %get-tuple-element.55.refs_2_, ...), custom_call_target="tpu_custom_call" | custom-call | tf_op jit(solution)/shard_map/pallas_call | solution.py:462
  26.3 3.3 %all-to-all-start.1 = ((f32[32,2,128]{2,1,0:T(2,128)}), f32[32,2,128]{2,1,0:T(2,128)S(1)}, u32[]{:S(2)}, u32[]{:S(2)}) async-start(f32[32,2,128]{2,1,0:T(2,128)} %get-tuple-element.64), calls=%async_computation.1 | async-start | bytes 65536 | tf_op jit(solution)/shard_map/all_to_all | solution.py:563
  29.7 4.6 %collective-permute-start.5 = (f32[8,384]{1,0:T(8,128)S(1)}, f32[8,384]{1,0:T(8,128)S(1)}, u32[]{:S(2)}, u32[]{:S(2)}) collective-permute-start(f32[8,384]{1,0:T(8,128)S(1)} %get-tuple-element.66), channel_id=1, source_target_pairs={{0,28},{4,0},{8,4},{12,8},{16,12},{20,16},{24,20},{28,24},{1,29},{... | collective-permute-start | bytes 36872 | tf_op jit(solution)/shard_map/ppermute | solution.py:477
  34.3 2.6 %all-to-all-done.1.all_ref = f32[32,2,128]{2,1,0:T(2,128)S(1)} async-done(((f32[32,2,128]{2,1,0:T(2,128)}), f32[32,2,128]{2,1,0:T(2,128)S(1)}, u32[]{:S(2)}, u32[]{:S(2)}) %all-to-all-start.1) | async-done | bytes 32800 | tf_op jit(solution)/shard_map/all_to_all | solution.py:563
  36.9 0.9 %shard_map.111 = (f32[8,1024]{1,0:T(8,128)S(1)}, f32[8,1024]{1,0:T(8,128)S(1)}, f32[8,128]{1,0:T(8,128)S(1)}, s32[8,128]{1,0:T(8,128)S(1)}) custom-call(f32[32,2,128]{2,1,0:T(2,128)S(1)} %all-to-all-done.1.all_ref, f32[512,256]{1,0:T(8,128)S(1)} %collective-permute-done.1.far_ref, bf16[1024,256]{1,0:T(8,128)(2,1)S(1)} %get-tuple-element.52.inv_high, ...), custom_call_target="tpu_custom_call" | custom-call | tf_op jit(solution)/shard_map/pallas_call | solution.py:462
  37.8 0.0 collective-permute-done.5.refs_6_
  37.8 0.1 collective-permute-start.6
  37.9 1.1 %collective-permute-done.6.refs_1_ = f32[8,1024]{1,0:T(8,128)S(1)} collective-permute-done((f32[8,1024]{1,0:T(8,128)S(1)}, f32[8,1024]{1,0:T(8,128)S(1)}, u32[]{:S(2)}, u32[]{:S(2)}) %collective-permute-start.6) | collective-permute-done | bytes 32800 | tf_op jit(solution)/shard_map/ppermute | solution.py:482
  39.0 0.9 %shard_map.112 = (f32[6,1,384]{2,1,0:T(1,128)}, f32[6,1,384]{2,1,0:T(1,128)}) custom-call(f32[8,1024]{1,0:T(8,128)S(1)} %get-tuple-element.67.refs_0_, f32[8,1024]{1,0:T(8,128)S(1)} %collective-permute-done.6.refs_1_, f32[8,1024]{1,0:T(8,128)S(1)} %get-tuple-element.68.refs_2_, f32[8,128]{1,0:T(8,128)S(1)} %get-tuple-element.69.refs_3_, ...), custom_call_target="tpu_custom_call" | custom-call | tf_op jit(solution)/shard_map/pallas_call | solution.py:462
Async XLA Ops:
  2.4 7.7 %collective-permute-start = (f32[8,384]{1,0:T(8,128)S(1)}, f32[8,384]{1,0:T(8,128)S(1)}, u32[]{:S(2)}, u32[]{:S(2)}) collective-permute-start(f32[8,384]{1,0:T(8,128)S(1)} %get-tuple-element.39.pack_ref.refs_5_), channel_id=1, source_target_pairs={{0,4},{4,8},{8,12},{12,16},{16,20},{20,24},{24,28},{28,0},{1,5},{5... | collective-permute-start | bytes 36872 | tf_op jit(solution)/shard_map/ppermute | solution.py:477
  5.4 16.6 %collective-permute-start.1 = (f32[512,256]{1,0:T(8,128)S(1)}, f32[512,256]{1,0:T(8,128)S(1)}, u32[]{:S(2)}, u32[]{:S(2)}) collective-permute-start(f32[512,256]{1,0:T(8,128)S(1)} %get-tuple-element.51), channel_id=1, source_target_pairs={{0,2},{1,3},{2,0},{3,1},{4,6},{5,7},{6,4},{7,5},{8,10},{9,11},{10,... | collective-permute-start | bytes 1572872 | tf_op jit(solution)/shard_map/ppermute | solution.py:482
  11.5 10.6 %all-to-all-start = ((f32[32,2,128]{2,1,0:T(2,128)}), f32[32,2,128]{2,1,0:T(2,128)S(1)}, u32[]{:S(2)}, u32[]{:S(2)}) async-start(f32[32,2,128]{2,1,0:T(2,128)} %get-tuple-element.50), calls=%async_computation | async-start | bytes 65536 | tf_op jit(solution)/shard_map/all_to_all | solution.py:563
  14.8 9.9 %collective-permute-start.3 = (f32[32,384]{1,0:T(8,128)S(1)}, f32[32,384]{1,0:T(8,128)S(1)}, u32[]{:S(2)}, u32[]{:S(2)}) collective-permute-start(f32[32,384]{1,0:T(8,128)S(1)} %get-tuple-element.58.refs_7_), channel_id=1, source_target_pairs={{0,4},{8,12},{16,20},{24,28},{4,0},{12,8},{20,16},{28,24},{1,5},{9... | collective-permute-start | bytes 147464 | tf_op jit(solution)/shard_map/ppermute | solution.py:602
  16.6 8.0 %collective-permute-start.4 = (f32[32,384]{1,0:T(8,128)S(1)}, f32[32,384]{1,0:T(8,128)S(1)}, u32[]{:S(2)}, u32[]{:S(2)}) collective-permute-start(f32[32,384]{1,0:T(8,128)S(1)} %get-tuple-element.59.refs_8_), channel_id=1, source_target_pairs={{4,8},{12,16},{20,24},{28,0},{8,4},{16,12},{24,20},{0,28},{5,9},{1... | collective-permute-start | bytes 147464 | tf_op jit(solution)/shard_map/ppermute | solution.py:601
  23.1 1.5 %collective-permute-start.2 = (f32[8,1024]{1,0:T(8,128)S(1)}, f32[8,1024]{1,0:T(8,128)S(1)}, u32[]{:S(2)}, u32[]{:S(2)}) collective-permute-start(f32[8,1024]{1,0:T(8,128)S(1)} %get-tuple-element.54.refs_0_), channel_id=1, source_target_pairs={{0,1},{1,0},{2,3},{3,2},{4,5},{5,4},{6,7},{7,6},{8,9},{9,8},{10,11... | collective-permute-start | bytes 98312 | tf_op jit(solution)/shard_map/ppermute | solution.py:482
  26.3 10.6 %all-to-all-start.1 = ((f32[32,2,128]{2,1,0:T(2,128)}), f32[32,2,128]{2,1,0:T(2,128)S(1)}, u32[]{:S(2)}, u32[]{:S(2)}) async-start(f32[32,2,128]{2,1,0:T(2,128)} %get-tuple-element.64), calls=%async_computation.1 | async-start | bytes 65536 | tf_op jit(solution)/shard_map/all_to_all | solution.py:563
  29.7 8.1 %collective-permute-start.5 = (f32[8,384]{1,0:T(8,128)S(1)}, f32[8,384]{1,0:T(8,128)S(1)}, u32[]{:S(2)}, u32[]{:S(2)}) collective-permute-start(f32[8,384]{1,0:T(8,128)S(1)} %get-tuple-element.66), channel_id=1, source_target_pairs={{0,28},{4,0},{8,4},{12,8},{16,12},{20,16},{24,20},{28,24},{1,29},{... | collective-permute-start | bytes 36872 | tf_op jit(solution)/shard_map/ppermute | solution.py:477
  37.8 1.2 %collective-permute-start.6 = (f32[8,1024]{1,0:T(8,128)S(1)}, f32[8,1024]{1,0:T(8,128)S(1)}, u32[]{:S(2)}, u32[]{:S(2)}) collective-permute-start(f32[8,1024]{1,0:T(8,128)S(1)} %get-tuple-element.67.refs_0_), channel_id=1, source_target_pairs={{0,1},{1,0},{2,3},{3,2},{4,5},{5,4},{6,7},{7,6},{8,9},{9,8},{10,11... | collective-permute-start | bytes 98312 | tf_op jit(solution)/shard_map/ppermute | solution.py:482

commit v7 on v6

--- a/solution.py
+++ b/solution.py
@@ -85,21 +85,10 @@
     pl.when(lax.axis_index("crs") >= 0)(body)
 
 
-def pack_kernel(
-    live_ref, jump_hbm, scale_hbm, nbr_hbm, inverse_hbm, out_ref, half_ref, jump, scale, nbr, sems,
-):
+def pack_kernel(live_ref, jump_hbm, scale_hbm, nbr_hbm, out_ref, jump, scale, nbr, sems):
+    for copy in fetched([(jump_hbm, jump), (scale_hbm, scale), (nbr_hbm, nbr)], sems):
+        copy.wait()
     cases, _, records = jump.shape
-    copies = fetched(
-        [
-            (jump_hbm, jump),
-            (scale_hbm, scale),
-            (nbr_hbm, nbr),
-            (half_of(lax.axis_index("crs"), inverse_hbm), half_ref),
-        ],
-        sems,
-    )
-    for copy in copies:
-        copy.wait()
     live = lax.broadcasted_iota(jnp.int32, (1, records), 1) < live_ref[0, 0]
     live = live.astype(F32)
     for case in range(cases):
@@ -162,16 +151,41 @@
     return inverse_hbm.at[pl.ds(pl.multiple_of(first, 8), rows)]
 
 
+def share_of_half(core, half):
+    width = half.shape[1]
+    own, other = [half[pl.ds(pl.multiple_of(c * width, width), width)] for c in (core, 1 - core)]
+    rows = width // 2
+    return jnp.concatenate(
+        [own, jnp.where(core == 0, other[:rows], jnp.transpose(other[:, rows:]))], axis=0
+    )
+
+
+def far_solution(core, total, share):
+    width = share.shape[1]
+    rows = width // 2
+    near, far = total[:, :width], total[:, width:]
+    first = core == 0
+    block = parts(share[:width], 2)
+    across = parts(share[width:], 2)
+    whole = product(jnp.where(first, far[:, :rows], near[:, rows:]), *across)
+    piece = product(jnp.where(first, near, far), *across, True)
+    none = jnp.zeros_like(piece)
+    near = product(near, *block) + jnp.where(first, whole, jnp.concatenate([none, piece], axis=1))
+    far = jnp.where(first, jnp.concatenate([piece, none], axis=1), whole)
+    return jnp.concatenate([near, far], axis=1)
+
+
 def prepare_kernel(
-    cases, pack_ref, schur_hbm, coupling_hbm, own_hbm, corner_hbm,
-    top_high, top_low, s_high, s_low, c_high, c_low, own_coupling, load_ref, index_ref, own_ref,
-    schur, coupling, own, corner, sems,
+    cases, pack_ref, schur_hbm, coupling_hbm, own_hbm, corner_hbm, inverse_hbm,
+    top_high, top_low, s_high, s_low, c_high, c_low, own_coupling, load_ref, index_ref, own_ref, share_ref,
+    schur, coupling, own, corner, half, sems,
 ):
     copies = fetched(
         [
             (own_hbm, own),
             (coupling_hbm, coupling),
             (corner_hbm, corner),
+            (half_of(lax.axis_index("crs"), inverse_hbm), half),
             *pieces(schur_hbm, schur, PIECES),
         ],
         sems,
@@ -189,8 +203,10 @@
     tiles = jnp.where(lane == lax.broadcasted_iota(jnp.int32, (held, LANES), 0), 1.0, 0.0)
     index = jnp.broadcast_to(corner[0].astype(F32), (ROWS, held))
     index_ref[...] = jnp.where(lane[:1] < held, exact(index, tiles.astype(BF16), 2)[:1], -1.0)
-    split_as_it_comes(copies[3:], schur, top_high, top_low, 0)
-    split_as_it_comes(copies[3:], schur, s_high, s_low, top_high.shape[0])
+    copies[3].wait()
+    share_ref[...] = share_of_half(lax.axis_index("crs") % 2, half)
+    split_as_it_comes(copies[4:], schur, top_high, top_low, 0)
+    split_as_it_comes(copies[4:], schur, s_high, s_low, top_high.shape[0])
 
 
 def inverse_kernel(inverse_hbm, inv_high, inv_low, inverse, sems):
@@ -224,8 +240,8 @@
 
 
 def forces(load, through, first, c_high, c_low, index_ref, cases, send_hbm, send, sems):
-    high, low = [jnp.concatenate([c[...]] * GROUP, axis=0) for c in (c_high, c_low)]
-    force = product(load, high, low, True)
+    force = product(load, c_high[...], c_low[...], True)
+    force = jnp.concatenate([force] * GROUP, axis=1)
     lane = lax.broadcasted_iota(jnp.int32, force.shape, 1) % SLOT
     row = lax.broadcasted_iota(jnp.int32, force.shape, 0)
     force = jnp.where(lane == SLOT - 2, first, force)
@@ -346,15 +362,10 @@
         index = near_index(cases, all_ref) ^ flip
         index_ref[...] = jnp.broadcast_to(index, index_ref.shape)
         total = total_ref[...]
-        last = [
-            far_ref[pl.ds(pl.multiple_of((slab % 2 ^ j) * width, width), width)] for j in range(2)
-        ]
-        third = product(total[:, 2 * width :], *parts(jnp.concatenate(last, axis=0), 2))
         x_ref[:, :width] = product(total, inv_high[...], inv_low[...])
         x_ref[:, width : 2 * width] = jnp.zeros((ROWS, width), F32)
         across = product(total[:, :width], inv_high[2 * width :], inv_low[2 * width :], True)
-        x_ref[:, 2 * width : 3 * width] = across[:, :width] + third
-        x_ref[:, 3 * width :] = across[:, width:]
+        x_ref[:, 2 * width :] = across + far_solution(slab % 2, total[:, 2 * width :], far_ref[...])
 
     for copy in copies:
         copy.wait()
@@ -506,19 +517,19 @@
 
     jump = jump_data.reshape(cases, 1, records)
     first = (jump, lumped_scale, nbr_dof)
-    pack, half = call(
+    (pack,) = call(
         pack_kernel,
-        [((ROWS, records), F32), ((2 * width, width), F32)],
-        (live_count, *first, corner_inverse),
-        [SM] + [HB] * 4,
-        [*buffers(*first)[:-1], pltpu.SemaphoreType.DMA((4,))],
-    )
-    if is_paired(width):
-        far = exchanged(half, "crs", 2)
+        [((ROWS, records), F32)],
+        (live_count, *first),
+        [SM] + [HB] * 3,
+        buffers(*first),
+    )
     left = passed_along(pack, "sub", 1)
     fetched_here = (schur_inverse, coarse_coupling, own_dof, corner_index)
+    half = (2 * width, width)
+    share = (width + width // 2, width)
     top = iface // 3 // LANES * LANES
-    *tops, s_high, s_low, c_high, c_low, own_coupling, load, index, own = call(
+    *tops, s_high, s_low, c_high, c_low, own_coupling, load, index, own, share = call(
         functools.partial(prepare_kernel, cases),
         [
             ((top, iface), BF16),
@@ -531,12 +542,19 @@
             ((ROWS, iface), F32),
             ((1, LANES), F32),
             ((1, records), jnp.int32),
+            (share, F32),
         ],
-        (pack, *fetched_here),
-        [VM] + [HB] * 4,
-        [*buffers(*fetched_here)[:-1], pltpu.SemaphoreType.DMA((3 + PIECES,))],
+        (pack, *fetched_here, corner_inverse),
+        [VM] + [HB] * 5,
+        [
+            *buffers(*fetched_here)[:-1],
+            pltpu.VMEM(half, F32),
+            pltpu.SemaphoreType.DMA((4 + PIECES,)),
+        ],
         32 << 20,
     )
+    if is_paired(width):
+        far = exchanged(share, "crs", 2)
     inv_high, inv_low = call(
         inverse_kernel,
         [((corners, width), BF16)] * 2,

time: 40.3 us -> 39.9 us (0.990)
  transfers between devices with their start and end apart: 9 -> 9, of which waited for: 4 -> 4; matrix products, arithmetic and copies ran while one was open for 0% -> 0% of each run, Pallas kernels for 19% -> 20%
where the time goes in v7:
time: 39.9 us; the launch traced here: 39.5 us
  starting transfers between devices  21.3 us (53%)
  Pallas kernels  11.2 us (28%)
  waiting for transfers between devices  5.68 us (14%)
  between operations  1.38 us (3%)
    pallas_call x9, Pallas kernels, call(): pl.pallas_call(kernel, out_shape=[jax.ShapeDtypeStruct(shape, kind) for s...  11.2 us
    ppermute x2, starting transfers between devices, passed_along(): return lax.ppermute(value, axis, pairs)  7.62 us
    all_to_all x2, starting transfers between devices, gathered(): everyone = lax.all_to_all(send, ('sub', 'crs'), 0, 0)  6.65 us
    all_to_all x2, waiting for transfers between devices, gathered(): everyone = lax.all_to_all(send, ('sub', 'crs'), 0, 0)  3.39 us
    ppermute x1, starting transfers between devices, per_device(): two = lax.ppermute(two_sent, 'sub', rounds[1])  3.31 us
    ppermute x3, starting transfers between devices, exchanged(): return lax.ppermute(value, axis, pairs)  1.9 us
    ppermute x1, starting transfers between devices, per_device(): one = lax.ppermute(one_sent, 'sub', rounds[0])  1.83 us
    ppermute x2, waiting for transfers between devices, passed_along(): return lax.ppermute(value, axis, pairs)  1.18 us
  transfers between devices with their start and end apart: 9, of which 4 were waited for; matrix products, arithmetic and copies ran while one was open for 0% of the time, Pallas kernels for 20%

profile of v7, /device:TPU:0, one launch (start us, length us, event | category | flops | bytes accessed | tf_op | source)
XLA Modules:
  0.0 39.5 jit_solution(8577542115153488579)
XLA Ops:
  1.3 0.8 %shard_map.104.pack_ref.refs_5_ = f32[8,384]{1,0:T(8,128)S(1)} custom-call(s32[1,1]{1,0:T(1,128)S(6)} %copy.13.live_ref, f32[6,1,384]{2,1,0:T(1,128)} %bitcast.7, f32[1,1,384]{2,1,0:T(1,128)} %scale_hbm.1, s32[1,1,384]{2,1,0:T(1,128)} %nbr_hbm.1), custom_call_target="tpu_custom_call" | custom-call | tf_op jit(solution)/shard_map/pallas_call | solution.py:473
  2.0 3.0 %collective-permute-start = (f32[8,384]{1,0:T(8,128)S(1)}, f32[8,384]{1,0:T(8,128)S(1)}, u32[]{:S(2)}, u32[]{:S(2)}) collective-permute-start(f32[8,384]{1,0:T(8,128)S(1)} %shard_map.104.pack_ref.refs_5_), channel_id=1, source_target_pairs={{0,4},{4,8},{8,12},{12,16},{16,20},{20,24},{24,28},{28,0},{1,5},{5... | collective-permute-start | bytes 36872 | tf_op jit(solution)/shard_map/ppermute | solution.py:488
  5.1 2.0 %shard_map.105 = (bf16[256,768]{1,0:T(8,128)(2,1)S(1)}, bf16[256,768]{1,0:T(8,128)(2,1)S(1)}, bf16[512,768]{1,0:T(8,128)(2,1)S(1)}, bf16[512,768]{1,0:T(8,128)(2...) custom-call(f32[8,384]{1,0:T(8,128)S(1)} %shard_map.104.pack_ref.ref, ...), custom_call_target="tpu_custom_call" | custom-call | bytes 33554432 | tf_op jit(solution)/shard_map/pallas_call | solution.py:473
  7.0 1.6 %collective-permute-start.1 = (f32[384,256]{1,0:T(8,128)S(1)}, f32[384,256]{1,0:T(8,128)S(1)}, u32[]{:S(2)}, u32[]{:S(2)}) collective-permute-start(f32[384,256]{1,0:T(8,128)S(1)} %get-tuple-element.49), channel_id=1, source_target_pairs={{0,2},{1,3},{2,0},{3,1},{4,6},{5,7},{6,4},{7,5},{8,10},{9,11},{10,... | collective-permute-start | bytes 1179656 | tf_op jit(solution)/shard_map/ppermute | solution.py:493
  8.6 1.2 %collective-permute-done.left_ref.refs_6_ = f32[8,384]{1,0:T(8,128)S(1)} collective-permute-done((f32[8,384]{1,0:T(8,128)S(1)}, f32[8,384]{1,0:T(8,128)S(1)}, u32[]{:S(2)}, u32[]{:S(2)}) %collective-permute-start) | collective-permute-done | bytes 12320 | tf_op jit(solution)/shard_map/ppermute | solution.py:488
  9.8 1.3 %shard_map.106 = (f32[32,2,128]{2,1,0:T(2,128)}, f32[32,384]{1,0:T(8,128)S(1)}, f32[32,384]{1,0:T(8,128)S(1)}, s32[1,384]{1,0:T(1,128)S(1)}) custom-call(f32[8,384]{1,0:T(8,128)S(1)} %collective-permute-done.left_ref.refs_6_, f32[8,384]{1,0:T(8,128)S(1)} %shard_map.104.pack_ref.refs_5_, f32[8,768]{1,0:T(8,128)S(1)} %get-tuple-element.38.load_ref, ...), custom_call_target="tpu_custom_call" | custom-call | flops 40000000000 | bytes 1 | tf_op jit(solution)/shard_map/pallas_call | solution.py:473
  11.1 3.3 %all-to-all-start = ((f32[32,2,128]{2,1,0:T(2,128)}), f32[32,2,128]{2,1,0:T(2,128)S(1)}, u32[]{:S(2)}, u32[]{:S(2)}) async-start(f32[32,2,128]{2,1,0:T(2,128)} %get-tuple-element.48), calls=%async_computation | async-start | bytes 65536 | tf_op jit(solution)/shard_map/all_to_all | solution.py:581
  14.4 1.8 %collective-permute-start.3 = (f32[32,384]{1,0:T(8,128)S(1)}, f32[32,384]{1,0:T(8,128)S(1)}, u32[]{:S(2)}, u32[]{:S(2)}) collective-permute-start(f32[32,384]{1,0:T(8,128)S(1)} %get-tuple-element.56.refs_7_), channel_id=1, source_target_pairs={{0,4},{8,12},{16,20},{24,28},{4,0},{12,8},{20,16},{28,24},{1,5},{9... | collective-permute-start | bytes 147464 | tf_op jit(solution)/shard_map/ppermute | solution.py:620
  16.3 3.3 %collective-permute-start.4 = (f32[32,384]{1,0:T(8,128)S(1)}, f32[32,384]{1,0:T(8,128)S(1)}, u32[]{:S(2)}, u32[]{:S(2)}) collective-permute-start(f32[32,384]{1,0:T(8,128)S(1)} %get-tuple-element.57.refs_8_), channel_id=1, source_target_pairs={{4,8},{12,16},{20,24},{28,0},{8,4},{16,12},{24,20},{0,28},{5,9},{1... | collective-permute-start | bytes 147464 | tf_op jit(solution)/shard_map/ppermute | solution.py:619
  19.6 1.4 %shard_map.107 = (bf16[1024,256]{1,0:T(8,128)(2,1)S(1)}, bf16[1024,256]{1,0:T(8,128)(2,1)S(1)}) custom-call(f32[1024,256]{1,0:T(8,128)} %inverse_hbm.3), custom_call_target="tpu_custom_call" | custom-call | tf_op jit(solution)/shard_map/pallas_call | solution.py:473
  20.9 0.7 %all-to-all-done.all_ref = f32[32,2,128]{2,1,0:T(2,128)S(1)} async-done(((f32[32,2,128]{2,1,0:T(2,128)}), f32[32,2,128]{2,1,0:T(2,128)S(1)}, u32[]{:S(2)}, u32[]{:S(2)}) %all-to-all-start) | async-done | bytes 32800 | tf_op jit(solution)/shard_map/all_to_all | solution.py:581
  21.7 0.0 collective-permute-done.1.far_ref
  21.7 1.1 %shard_map.108 = (f32[8,1024]{1,0:T(8,128)S(1)}, f32[8,1024]{1,0:T(8,128)S(1)}, f32[8,128]{1,0:T(8,128)S(1)}, s32[8,128]{1,0:T(8,128)S(1)}, f32[192,768]{1,0:T(8,128)S(1)}) custom-call(f32[32,2,128]{2,1,0:T(2,128)S(1)} %all-to-all-done.all_ref, f32[384,256]{1,0:T(8,128)S(1)} %collective-permute-done.1.far_ref, ...), custom_call_target="tpu_custom_call" | custom-call | tf_op jit(solution)/shard_map/pallas_call | solution.py:473
  22.8 0.2 collective-permute-start.2
  22.9 1.3 %shard_map.109 = (bf16[512,768]{1,0:T(8,128)(2,1)S(1)}, bf16[512,768]{1,0:T(8,128)(2,1)S(1)}) custom-call(f32[192,768]{1,0:T(8,128)S(1)} %get-tuple-element.58.rows_ref, f32[1,1,768,768]{3,2,1,0:T(8,128)} %schur_hbm.7), custom_call_target="tpu_custom_call" | custom-call | tf_op jit(solution)/shard_map/pallas_call | solution.py:473
  24.3 0.0 collective-permute-done.3.refs_9_
  24.3 0.0 collective-permute-done.4.refs_10_
  24.3 0.0 collective-permute-done.2.refs_1_
  24.3 1.6 %shard_map.110 = (f32[32,2,128]{2,1,0:T(2,128)}, f32[8,384]{1,0:T(8,128)S(1)}, f32[16,384]{1,0:T(8,128)S(1)}, f32[128,384]{1,0:T(8,128)S(1)}, f32[8,128]{1,0:T(8,128)S(1)}) custom-call(f32[8,1024]{1,0:T(8,128)S(1)} %get-tuple-element.52.refs_0_, f32[8,1024]{1,0:T(8,128)S(1)} %collective-permute-done.2.refs_1_, f32[8,1024]{1,0:T(8,128)S(1)} %get-tuple-element.53.refs_2_, ...), custom_call_target="tpu_custom_call" | custom-call | tf_op jit(solution)/shard_map/pallas_call | solution.py:473
  26.0 3.3 %all-to-all-start.1 = ((f32[32,2,128]{2,1,0:T(2,128)}), f32[32,2,128]{2,1,0:T(2,128)S(1)}, u32[]{:S(2)}, u32[]{:S(2)}) async-start(f32[32,2,128]{2,1,0:T(2,128)} %get-tuple-element.62), calls=%async_computation.1 | async-start | bytes 65536 | tf_op jit(solution)/shard_map/all_to_all | solution.py:581
  29.3 4.6 %collective-permute-start.5 = (f32[8,384]{1,0:T(8,128)S(1)}, f32[8,384]{1,0:T(8,128)S(1)}, u32[]{:S(2)}, u32[]{:S(2)}) collective-permute-start(f32[8,384]{1,0:T(8,128)S(1)} %get-tuple-element.64), channel_id=1, source_target_pairs={{0,28},{4,0},{8,4},{12,8},{16,12},{20,16},{24,20},{28,24},{1,29},{... | collective-permute-start | bytes 36872 | tf_op jit(solution)/shard_map/ppermute | solution.py:488
  33.9 2.6 %all-to-all-done.1.all_ref = f32[32,2,128]{2,1,0:T(2,128)S(1)} async-done(((f32[32,2,128]{2,1,0:T(2,128)}), f32[32,2,128]{2,1,0:T(2,128)S(1)}, u32[]{:S(2)}, u32[]{:S(2)}) %all-to-all-start.1) | async-done | bytes 32800 | tf_op jit(solution)/shard_map/all_to_all | solution.py:581
  36.5 0.8 %shard_map.111 = (f32[8,1024]{1,0:T(8,128)S(1)}, f32[8,1024]{1,0:T(8,128)S(1)}, f32[8,128]{1,0:T(8,128)S(1)}, s32[8,128]{1,0:T(8,128)S(1)}) custom-call(f32[32,2,128]{2,1,0:T(2,128)S(1)} %all-to-all-done.1.all_ref, f32[384,256]{1,0:T(8,128)S(1)} %collective-permute-done.1.far_ref, bf16[1024,256]{1,0:T(8,128)(2,1)S(1)} %get-tuple-element.50.inv_high, ...), custom_call_target="tpu_custom_call" | custom-call | tf_op jit(solution)/shard_map/pallas_call | solution.py:473
  37.4 0.0 collective-permute-done.5.refs_6_
  37.4 0.2 collective-permute-start.6
  37.5 1.1 %collective-permute-done.6.refs_1_ = f32[8,1024]{1,0:T(8,128)S(1)} collective-permute-done((f32[8,1024]{1,0:T(8,128)S(1)}, f32[8,1024]{1,0:T(8,128)S(1)}, u32[]{:S(2)}, u32[]{:S(2)}) %collective-permute-start.6) | collective-permute-done | bytes 32800 | tf_op jit(solution)/shard_map/ppermute | solution.py:493
  38.6 0.9 %shard_map.112 = (f32[6,1,384]{2,1,0:T(1,128)}, f32[6,1,384]{2,1,0:T(1,128)}) custom-call(f32[8,1024]{1,0:T(8,128)S(1)} %get-tuple-element.65.refs_0_, f32[8,1024]{1,0:T(8,128)S(1)} %collective-permute-done.6.refs_1_, f32[8,1024]{1,0:T(8,128)S(1)} %get-tuple-element.66.refs_2_, f32[8,128]{1,0:T(8,128)S(1)} %get-tuple-element.67.refs_3_, ...), custom_call_target="tpu_custom_call" | custom-call | tf_op jit(solution)/shard_map/pallas_call | solution.py:473
Async XLA Ops:
  2.0 7.7 %collective-permute-start = (f32[8,384]{1,0:T(8,128)S(1)}, f32[8,384]{1,0:T(8,128)S(1)}, u32[]{:S(2)}, u32[]{:S(2)}) collective-permute-start(f32[8,384]{1,0:T(8,128)S(1)} %shard_map.104.pack_ref.refs_5_), channel_id=1, source_target_pairs={{0,4},{4,8},{8,12},{12,16},{16,20},{20,24},{24,28},{28,0},{1,5},{5... | collective-permute-start | bytes 36872 | tf_op jit(solution)/shard_map/ppermute | solution.py:488
  7.0 14.7 %collective-permute-start.1 = (f32[384,256]{1,0:T(8,128)S(1)}, f32[384,256]{1,0:T(8,128)S(1)}, u32[]{:S(2)}, u32[]{:S(2)}) collective-permute-start(f32[384,256]{1,0:T(8,128)S(1)} %get-tuple-element.49), channel_id=1, source_target_pairs={{0,2},{1,3},{2,0},{3,1},{4,6},{5,7},{6,4},{7,5},{8,10},{9,11},{10,... | collective-permute-start | bytes 1179656 | tf_op jit(solution)/shard_map/ppermute | solution.py:493
  11.1 10.6 %all-to-all-start = ((f32[32,2,128]{2,1,0:T(2,128)}), f32[32,2,128]{2,1,0:T(2,128)S(1)}, u32[]{:S(2)}, u32[]{:S(2)}) async-start(f32[32,2,128]{2,1,0:T(2,128)} %get-tuple-element.48), calls=%async_computation | async-start | bytes 65536 | tf_op jit(solution)/shard_map/all_to_all | solution.py:581
  14.4 9.9 %collective-permute-start.3 = (f32[32,384]{1,0:T(8,128)S(1)}, f32[32,384]{1,0:T(8,128)S(1)}, u32[]{:S(2)}, u32[]{:S(2)}) collective-permute-start(f32[32,384]{1,0:T(8,128)S(1)} %get-tuple-element.56.refs_7_), channel_id=1, source_target_pairs={{0,4},{8,12},{16,20},{24,28},{4,0},{12,8},{20,16},{28,24},{1,5},{9... | collective-permute-start | bytes 147464 | tf_op jit(solution)/shard_map/ppermute | solution.py:620
  16.3 8.0 %collective-permute-start.4 = (f32[32,384]{1,0:T(8,128)S(1)}, f32[32,384]{1,0:T(8,128)S(1)}, u32[]{:S(2)}, u32[]{:S(2)}) collective-permute-start(f32[32,384]{1,0:T(8,128)S(1)} %get-tuple-element.57.refs_8_), channel_id=1, source_target_pairs={{4,8},{12,16},{20,24},{28,0},{8,4},{16,12},{24,20},{0,28},{5,9},{1... | collective-permute-start | bytes 147464 | tf_op jit(solution)/shard_map/ppermute | solution.py:619
  22.8 1.5 %collective-permute-start.2 = (f32[8,1024]{1,0:T(8,128)S(1)}, f32[8,1024]{1,0:T(8,128)S(1)}, u32[]{:S(2)}, u32[]{:S(2)}) collective-permute-start(f32[8,1024]{1,0:T(8,128)S(1)} %get-tuple-element.52.refs_0_), channel_id=1, source_target_pairs={{0,1},{1,0},{2,3},{3,2},{4,5},{5,4},{6,7},{7,6},{8,9},{9,8},{10,11... | collective-permute-start | bytes 98312 | tf_op jit(solution)/shard_map/ppermute | solution.py:493
  26.0 10.6 %all-to-all-start.1 = ((f32[32,2,128]{2,1,0:T(2,128)}), f32[32,2,128]{2,1,0:T(2,128)S(1)}, u32[]{:S(2)}, u32[]{:S(2)}) async-start(f32[32,2,128]{2,1,0:T(2,128)} %get-tuple-element.62), calls=%async_computation.1 | async-start | bytes 65536 | tf_op jit(solution)/shard_map/all_to_all | solution.py:581
  29.3 8.1 %collective-permute-start.5 = (f32[8,384]{1,0:T(8,128)S(1)}, f32[8,384]{1,0:T(8,128)S(1)}, u32[]{:S(2)}, u32[]{:S(2)}) collective-permute-start(f32[8,384]{1,0:T(8,128)S(1)} %get-tuple-element.64), channel_id=1, source_target_pairs={{0,28},{4,0},{8,4},{12,8},{16,12},{20,16},{24,20},{28,24},{1,29},{... | collective-permute-start | bytes 36872 | tf_op jit(solution)/shard_map/ppermute | solution.py:488
  37.4 1.3 %collective-permute-start.6 = (f32[8,1024]{1,0:T(8,128)S(1)}, f32[8,1024]{1,0:T(8,128)S(1)}, u32[]{:S(2)}, u32[]{:S(2)}) collective-permute-start(f32[8,1024]{1,0:T(8,128)S(1)} %get-tuple-element.65.refs_0_), channel_id=1, source_target_pairs={{0,1},{1,0},{2,3},{3,2},{4,5},{5,4},{6,7},{7,6},{8,9},{9,8},{10,11... | collective-permute-start | bytes 98312 | tf_op jit(solution)/shard_map/ppermute | solution.py:493

commit v8 on v7

--- a/solution.py
+++ b/solution.py
@@ -384,7 +384,7 @@
 
 def second_kernel(cases, coarse, given, *refs):
     (
-        pack_ref, left_ref, one_sent, two_sent, one_ref, two_ref,
+        pack_ref, left_ref, one_sent, two_sent, two_ref, one_ref,
         top_high, top_low, s_high, s_low, own_ref, left_index, c_high, c_low, corner_ref,
         send_hbm, out_ref, keep_ref, spread_ref, scalar_ref, send, sems,
     ) = refs[given : given + 22]
@@ -638,7 +638,7 @@
             ((ROWS, LANES), F32),
         ],
         (
-            *given, pack, left, one_sent, two_sent, one, two,
+            *given, pack, left, one_sent, two_sent, two, one,
             *tops, *terms, own, left_index, c_high, c_low, index,
         ),
         specs,

time: 39.9 us -> 39.4 us (0.987)
  starting transfers between devices: 21.3 us -> 20.2 us
  waiting for transfers between devices: 5.68 us -> 6.28 us
    ppermute x1, starting transfers between devices: 1.83 us -> 0.01 us  [per_device(): one = lax.ppermute(one_sent, 'sub', rounds[0])]
    ppermute x1, starting transfers between devices: 3.31 us -> 4.62 us  [per_device(): two = lax.ppermute(two_sent, 'sub', rounds[1])]
    all_to_all x2, starting transfers between devices: 6.65 us -> 6.03 us  [gathered(): everyone = lax.all_to_all(send, ('sub', 'crs'), 0, 0)]
    all_to_all x2, waiting for transfers between devices: 3.39 us -> 3.99 us  [gathered(): everyone = lax.all_to_all(send, ('sub', 'crs'), 0, 0)]
where the time goes in v8:
time: 39.4 us; the launch traced here: 39 us
  starting transfers between devices  20.2 us (51%)
  Pallas kernels  11.2 us (28%)
  waiting for transfers between devices  6.28 us (16%)
  between operations  1.38 us (4%)
    pallas_call x9, Pallas kernels, call(): pl.pallas_call(kernel, out_shape=[jax.ShapeDtypeStruct(shape, kind) for s...  11.2 us
    ppermute x2, starting transfers between devices, passed_along(): return lax.ppermute(value, axis, pairs)  7.62 us
    all_to_all x2, starting transfers between devices, gathered(): everyone = lax.all_to_all(send, ('sub', 'crs'), 0, 0)  6.03 us
    ppermute x1, starting transfers between devices, per_device(): two = lax.ppermute(two_sent, 'sub', rounds[1])  4.62 us
    all_to_all x2, waiting for transfers between devices, gathered(): everyone = lax.all_to_all(send, ('sub', 'crs'), 0, 0)  3.99 us
    ppermute x3, starting transfers between devices, exchanged(): return lax.ppermute(value, axis, pairs)  1.91 us
    ppermute x2, waiting for transfers between devices, passed_along(): return lax.ppermute(value, axis, pairs)  1.18 us
    ppermute x3, waiting for transfers between devices, exchanged(): return lax.ppermute(value, axis, pairs)  1.1 us
  transfers between devices with their start and end apart: 9, of which 4 were waited for; matrix products, arithmetic and copies ran while one was open for 0% of the time, Pallas kernels for 20%

profile of v8, /device:TPU:0, one launch (start us, length us, event | category | flops | bytes accessed | tf_op | source)
XLA Modules:
  0.0 39.0 jit_solution(1579276114998425394)
XLA Ops:
  1.3 0.8 %shard_map.104.pack_ref.refs_5_ = f32[8,384]{1,0:T(8,128)S(1)} custom-call(s32[1,1]{1,0:T(1,128)S(6)} %copy.13.live_ref, f32[6,1,384]{2,1,0:T(1,128)} %bitcast.7, f32[1,1,384]{2,1,0:T(1,128)} %scale_hbm.1, s32[1,1,384]{2,1,0:T(1,128)} %nbr_hbm.1), custom_call_target="tpu_custom_call" | custom-call | tf_op jit(solution)/shard_map/pallas_call | solution.py:473
  2.0 3.0 %collective-permute-start = (f32[8,384]{1,0:T(8,128)S(1)}, f32[8,384]{1,0:T(8,128)S(1)}, u32[]{:S(2)}, u32[]{:S(2)}) collective-permute-start(f32[8,384]{1,0:T(8,128)S(1)} %shard_map.104.pack_ref.refs_5_), channel_id=1, source_target_pairs={{0,4},{4,8},{8,12},{12,16},{16,20},{20,24},{24,28},{28,0},{1,5},{5... | collective-permute-start | bytes 36872 | tf_op jit(solution)/shard_map/ppermute | solution.py:488
  5.1 2.0 %shard_map.105 = (bf16[256,768]{1,0:T(8,128)(2,1)S(1)}, bf16[256,768]{1,0:T(8,128)(2,1)S(1)}, bf16[512,768]{1,0:T(8,128)(2,1)S(1)}, bf16[512,768]{1,0:T(8,128)(2...) custom-call(f32[8,384]{1,0:T(8,128)S(1)} %shard_map.104.pack_ref.ref, ...), custom_call_target="tpu_custom_call" | custom-call | bytes 33554432 | tf_op jit(solution)/shard_map/pallas_call | solution.py:473
  7.0 1.6 %collective-permute-start.1 = (f32[384,256]{1,0:T(8,128)S(1)}, f32[384,256]{1,0:T(8,128)S(1)}, u32[]{:S(2)}, u32[]{:S(2)}) collective-permute-start(f32[384,256]{1,0:T(8,128)S(1)} %get-tuple-element.49), channel_id=1, source_target_pairs={{0,2},{1,3},{2,0},{3,1},{4,6},{5,7},{6,4},{7,5},{8,10},{9,11},{10,... | collective-permute-start | bytes 1179656 | tf_op jit(solution)/shard_map/ppermute | solution.py:493
  8.6 1.2 %collective-permute-done.left_ref.refs_6_ = f32[8,384]{1,0:T(8,128)S(1)} collective-permute-done((f32[8,384]{1,0:T(8,128)S(1)}, f32[8,384]{1,0:T(8,128)S(1)}, u32[]{:S(2)}, u32[]{:S(2)}) %collective-permute-start) | collective-permute-done | bytes 12320 | tf_op jit(solution)/shard_map/ppermute | solution.py:488
  9.8 1.3 %shard_map.106 = (f32[32,2,128]{2,1,0:T(2,128)}, f32[32,384]{1,0:T(8,128)S(1)}, f32[32,384]{1,0:T(8,128)S(1)}, s32[1,384]{1,0:T(1,128)S(1)}) custom-call(f32[8,384]{1,0:T(8,128)S(1)} %collective-permute-done.left_ref.refs_6_, f32[8,384]{1,0:T(8,128)S(1)} %shard_map.104.pack_ref.refs_5_, f32[8,768]{1,0:T(8,128)S(1)} %get-tuple-element.38.load_ref, ...), custom_call_target="tpu_custom_call" | custom-call | flops 40000000000 | bytes 1 | tf_op jit(solution)/shard_map/pallas_call | solution.py:473
  11.1 3.3 %all-to-all-start = ((f32[32,2,128]{2,1,0:T(2,128)}), f32[32,2,128]{2,1,0:T(2,128)S(1)}, u32[]{:S(2)}, u32[]{:S(2)}) async-start(f32[32,2,128]{2,1,0:T(2,128)} %get-tuple-element.48), calls=%async_computation | async-start | bytes 65536 | tf_op jit(solution)/shard_map/all_to_all | solution.py:581
  14.4 4.6 %collective-permute-start.3 = (f32[32,384]{1,0:T(8,128)S(1)}, f32[32,384]{1,0:T(8,128)S(1)}, u32[]{:S(2)}, u32[]{:S(2)}) collective-permute-start(f32[32,384]{1,0:T(8,128)S(1)} %get-tuple-element.57.refs_8_), channel_id=1, source_target_pairs={{4,8},{12,16},{20,24},{28,0},{8,4},{16,12},{24,20},{0,28},{5,9},{1... | collective-permute-start | bytes 147464 | tf_op jit(solution)/shard_map/ppermute | solution.py:619
  19.0 0.0 collective-permute-start.4
  19.0 1.4 %shard_map.107 = (bf16[1024,256]{1,0:T(8,128)(2,1)S(1)}, bf16[1024,256]{1,0:T(8,128)(2,1)S(1)}) custom-call(f32[1024,256]{1,0:T(8,128)} %inverse_hbm.3), custom_call_target="tpu_custom_call" | custom-call | tf_op jit(solution)/shard_map/pallas_call | solution.py:473
  20.4 1.3 %all-to-all-done.all_ref = f32[32,2,128]{2,1,0:T(2,128)S(1)} async-done(((f32[32,2,128]{2,1,0:T(2,128)}), f32[32,2,128]{2,1,0:T(2,128)S(1)}, u32[]{:S(2)}, u32[]{:S(2)}) %all-to-all-start) | async-done | bytes 32800 | tf_op jit(solution)/shard_map/all_to_all | solution.py:581
  21.8 0.0 collective-permute-done.1.far_ref
  21.8 1.1 %shard_map.108 = (f32[8,1024]{1,0:T(8,128)S(1)}, f32[8,1024]{1,0:T(8,128)S(1)}, f32[8,128]{1,0:T(8,128)S(1)}, s32[8,128]{1,0:T(8,128)S(1)}, f32[192,768]{1,0:T(8,128)S(1)}) custom-call(f32[32,2,128]{2,1,0:T(2,128)S(1)} %all-to-all-done.all_ref, f32[384,256]{1,0:T(8,128)S(1)} %collective-permute-done.1.far_ref, ...), custom_call_target="tpu_custom_call" | custom-call | tf_op jit(solution)/shard_map/pallas_call | solution.py:473
  22.8 0.2 collective-permute-start.2
  23.0 1.3 %shard_map.109 = (bf16[512,768]{1,0:T(8,128)(2,1)S(1)}, bf16[512,768]{1,0:T(8,128)(2,1)S(1)}) custom-call(f32[192,768]{1,0:T(8,128)S(1)} %get-tuple-element.58.rows_ref, f32[1,1,768,768]{3,2,1,0:T(8,128)} %schur_hbm.7), custom_call_target="tpu_custom_call" | custom-call | tf_op jit(solution)/shard_map/pallas_call | solution.py:473
  24.4 0.0 collective-permute-done.3.refs_9_
  24.4 0.0 collective-permute-done.4.refs_10_
  24.4 0.0 collective-permute-done.2.refs_1_
  24.4 1.6 %shard_map.110 = (f32[32,2,128]{2,1,0:T(2,128)}, f32[8,384]{1,0:T(8,128)S(1)}, f32[16,384]{1,0:T(8,128)S(1)}, f32[128,384]{1,0:T(8,128)S(1)}, f32[8,128]{1,0:T(8,128)S(1)}) custom-call(f32[8,1024]{1,0:T(8,128)S(1)} %get-tuple-element.52.refs_0_, f32[8,1024]{1,0:T(8,128)S(1)} %collective-permute-done.2.refs_1_, f32[8,1024]{1,0:T(8,128)S(1)} %get-tuple-element.53.refs_2_, ...), custom_call_target="tpu_custom_call" | custom-call | tf_op jit(solution)/shard_map/pallas_call | solution.py:473
  26.0 2.7 %all-to-all-start.1 = ((f32[32,2,128]{2,1,0:T(2,128)}), f32[32,2,128]{2,1,0:T(2,128)S(1)}, u32[]{:S(2)}, u32[]{:S(2)}) async-start(f32[32,2,128]{2,1,0:T(2,128)} %get-tuple-element.62), calls=%async_computation.1 | async-start | bytes 65536 | tf_op jit(solution)/shard_map/all_to_all | solution.py:581
  28.8 4.6 %collective-permute-start.5 = (f32[8,384]{1,0:T(8,128)S(1)}, f32[8,384]{1,0:T(8,128)S(1)}, u32[]{:S(2)}, u32[]{:S(2)}) collective-permute-start(f32[8,384]{1,0:T(8,128)S(1)} %get-tuple-element.64), channel_id=1, source_target_pairs={{0,28},{4,0},{8,4},{12,8},{16,12},{20,16},{24,20},{28,24},{1,29},{... | collective-permute-start | bytes 36872 | tf_op jit(solution)/shard_map/ppermute | solution.py:488
  33.4 2.6 %all-to-all-done.1.all_ref = f32[32,2,128]{2,1,0:T(2,128)S(1)} async-done(((f32[32,2,128]{2,1,0:T(2,128)}), f32[32,2,128]{2,1,0:T(2,128)S(1)}, u32[]{:S(2)}, u32[]{:S(2)}) %all-to-all-start.1) | async-done | bytes 32800 | tf_op jit(solution)/shard_map/all_to_all | solution.py:581
  36.0 0.8 %shard_map.111 = (f32[8,1024]{1,0:T(8,128)S(1)}, f32[8,1024]{1,0:T(8,128)S(1)}, f32[8,128]{1,0:T(8,128)S(1)}, s32[8,128]{1,0:T(8,128)S(1)}) custom-call(f32[32,2,128]{2,1,0:T(2,128)S(1)} %all-to-all-done.1.all_ref, f32[384,256]{1,0:T(8,128)S(1)} %collective-permute-done.1.far_ref, bf16[1024,256]{1,0:T(8,128)(2,1)S(1)} %get-tuple-element.50.inv_high, ...), custom_call_target="tpu_custom_call" | custom-call | tf_op jit(solution)/shard_map/pallas_call | solution.py:473
  36.8 0.0 collective-permute-done.5.refs_6_
  36.8 0.2 collective-permute-start.6
  37.0 1.1 %collective-permute-done.6.refs_1_ = f32[8,1024]{1,0:T(8,128)S(1)} collective-permute-done((f32[8,1024]{1,0:T(8,128)S(1)}, f32[8,1024]{1,0:T(8,128)S(1)}, u32[]{:S(2)}, u32[]{:S(2)}) %collective-permute-start.6) | collective-permute-done | bytes 32800 | tf_op jit(solution)/shard_map/ppermute | solution.py:493
  38.1 0.9 %shard_map.112 = (f32[6,1,384]{2,1,0:T(1,128)}, f32[6,1,384]{2,1,0:T(1,128)}) custom-call(f32[8,1024]{1,0:T(8,128)S(1)} %get-tuple-element.65.refs_0_, f32[8,1024]{1,0:T(8,128)S(1)} %collective-permute-done.6.refs_1_, f32[8,1024]{1,0:T(8,128)S(1)} %get-tuple-element.66.refs_2_, f32[8,128]{1,0:T(8,128)S(1)} %get-tuple-element.67.refs_3_, ...), custom_call_target="tpu_custom_call" | custom-call | tf_op jit(solution)/shard_map/pallas_call | solution.py:473
Async XLA Ops:
  2.0 7.7 %collective-permute-start = (f32[8,384]{1,0:T(8,128)S(1)}, f32[8,384]{1,0:T(8,128)S(1)}, u32[]{:S(2)}, u32[]{:S(2)}) collective-permute-start(f32[8,384]{1,0:T(8,128)S(1)} %shard_map.104.pack_ref.refs_5_), channel_id=1, source_target_pairs={{0,4},{4,8},{8,12},{12,16},{16,20},{20,24},{24,28},{28,0},{1,5},{5... | collective-permute-start | bytes 36872 | tf_op jit(solution)/shard_map/ppermute | solution.py:488
  7.0 14.7 %collective-permute-start.1 = (f32[384,256]{1,0:T(8,128)S(1)}, f32[384,256]{1,0:T(8,128)S(1)}, u32[]{:S(2)}, u32[]{:S(2)}) collective-permute-start(f32[384,256]{1,0:T(8,128)S(1)} %get-tuple-element.49), channel_id=1, source_target_pairs={{0,2},{1,3},{2,0},{3,1},{4,6},{5,7},{6,4},{7,5},{8,10},{9,11},{10,... | collective-permute-start | bytes 1179656 | tf_op jit(solution)/shard_map/ppermute | solution.py:493
  11.1 10.7 %all-to-all-start = ((f32[32,2,128]{2,1,0:T(2,128)}), f32[32,2,128]{2,1,0:T(2,128)S(1)}, u32[]{:S(2)}, u32[]{:S(2)}) async-start(f32[32,2,128]{2,1,0:T(2,128)} %get-tuple-element.48), calls=%async_computation | async-start | bytes 65536 | tf_op jit(solution)/shard_map/all_to_all | solution.py:581
  14.4 9.9 %collective-permute-start.3 = (f32[32,384]{1,0:T(8,128)S(1)}, f32[32,384]{1,0:T(8,128)S(1)}, u32[]{:S(2)}, u32[]{:S(2)}) collective-permute-start(f32[32,384]{1,0:T(8,128)S(1)} %get-tuple-element.57.refs_8_), channel_id=1, source_target_pairs={{4,8},{12,16},{20,24},{28,0},{8,4},{16,12},{24,20},{0,28},{5,9},{1... | collective-permute-start | bytes 147464 | tf_op jit(solution)/shard_map/ppermute | solution.py:619
  19.0 5.3 %collective-permute-start.4 = (f32[32,384]{1,0:T(8,128)S(1)}, f32[32,384]{1,0:T(8,128)S(1)}, u32[]{:S(2)}, u32[]{:S(2)}) collective-permute-start(f32[32,384]{1,0:T(8,128)S(1)} %get-tuple-element.56.refs_7_), channel_id=1, source_target_pairs={{0,4},{8,12},{16,20},{24,28},{4,0},{12,8},{20,16},{28,24},{1,5},{9... | collective-permute-start | bytes 147464 | tf_op jit(solution)/shard_map/ppermute | solution.py:620
  22.8 1.6 %collective-permute-start.2 = (f32[8,1024]{1,0:T(8,128)S(1)}, f32[8,1024]{1,0:T(8,128)S(1)}, u32[]{:S(2)}, u32[]{:S(2)}) collective-permute-start(f32[8,1024]{1,0:T(8,128)S(1)} %get-tuple-element.52.refs_0_), channel_id=1, source_target_pairs={{0,1},{1,0},{2,3},{3,2},{4,5},{5,4},{6,7},{7,6},{8,9},{9,8},{10,11... | collective-permute-start | bytes 98312 | tf_op jit(solution)/shard_map/ppermute | solution.py:493
  26.0 10.0 %all-to-all-start.1 = ((f32[32,2,128]{2,1,0:T(2,128)}), f32[32,2,128]{2,1,0:T(2,128)S(1)}, u32[]{:S(2)}, u32[]{:S(2)}) async-start(f32[32,2,128]{2,1,0:T(2,128)} %get-tuple-element.62), calls=%async_computation.1 | async-start | bytes 65536 | tf_op jit(solution)/shard_map/all_to_all | solution.py:581
  28.8 8.1 %collective-permute-start.5 = (f32[8,384]{1,0:T(8,128)S(1)}, f32[8,384]{1,0:T(8,128)S(1)}, u32[]{:S(2)}, u32[]{:S(2)}) collective-permute-start(f32[8,384]{1,0:T(8,128)S(1)} %get-tuple-element.64), channel_id=1, source_target_pairs={{0,28},{4,0},{8,4},{12,8},{16,12},{20,16},{24,20},{28,24},{1,29},{... | collective-permute-start | bytes 36872 | tf_op jit(solution)/shard_map/ppermute | solution.py:488
  36.8 1.3 %collective-permute-start.6 = (f32[8,1024]{1,0:T(8,128)S(1)}, f32[8,1024]{1,0:T(8,128)S(1)}, u32[]{:S(2)}, u32[]{:S(2)}) collective-permute-start(f32[8,1024]{1,0:T(8,128)S(1)} %get-tuple-element.65.refs_0_), channel_id=1, source_target_pairs={{0,1},{1,0},{2,3},{3,2},{4,5},{5,4},{6,7},{7,6},{8,9},{9,8},{10,11... | collective-permute-start | bytes 98312 | tf_op jit(solution)/shard_map/ppermute | solution.py:493

commit v9 on v8

--- a/solution.py
+++ b/solution.py
@@ -160,13 +160,13 @@
     )
 
 
-def far_solution(core, total, share):
-    width = share.shape[1]
+def far_solution(core, total, *share):
+    width = share[0].shape[1]
     rows = width // 2
     near, far = total[:, :width], total[:, width:]
     first = core == 0
-    block = parts(share[:width], 2)
-    across = parts(share[width:], 2)
+    block = [part[:width] for part in share]
+    across = [part[width:] for part in share]
     whole = product(jnp.where(first, far[:, :rows], near[:, rows:]), *across)
     piece = product(jnp.where(first, near, far), *across, True)
     none = jnp.zeros_like(piece)
@@ -209,13 +209,20 @@
     split_as_it_comes(copies[4:], schur, s_high, s_low, top_high.shape[0])
 
 
-def inverse_kernel(inverse_hbm, inv_high, inv_low, inverse, sems):
+def inverse_kernel(far_ref, inverse_hbm, inv_high, inv_low, far_high, far_low, inverse, sems):
     blocks, width = lax.axis_size("crs"), inverse.shape[1]
     pairs = []
     for j in range(blocks):
         rows = pl.ds(pl.multiple_of(block_at(lax.axis_index("crs"), j, width) * width, width), width)
         pairs.append((inverse_hbm.at[rows], inverse.at[pl.ds(j * width, width)]))
-    for copy in fetched(pairs, sems):
+    copies = fetched(pairs, sems)
+    if far_ref is not None:
+
+        @always
+        def _():
+            far_high[...], far_low[...] = parts(far_ref[...], 2)
+
+    for copy in copies:
         copy.wait()
     inv_high[...], inv_low[...] = parts(inverse[...], 2)
 
@@ -346,7 +353,7 @@
 
 
 def pair_kernel(
-    cases, first_row, all_ref, far_ref, inv_high, inv_low, schur_hbm, x_ref, total_ref, sums_ref, index_ref, *later,
+    cases, first_row, all_ref, far_high, far_low, inv_high, inv_low, schur_hbm, x_ref, total_ref, sums_ref, index_ref, *later,
 ):
     copies = []
     if later:
@@ -365,7 +372,7 @@
         x_ref[:, :width] = product(total, inv_high[...], inv_low[...])
         x_ref[:, width : 2 * width] = jnp.zeros((ROWS, width), F32)
         across = product(total[:, :width], inv_high[2 * width :], inv_low[2 * width :], True)
-        x_ref[:, 2 * width :] = across + far_solution(slab % 2, total[:, 2 * width :], far_ref[...])
+        x_ref[:, 2 * width :] = across + far_solution(slab % 2, total[:, 2 * width :], far_high, far_low)
 
     for copy in copies:
         copy.wait()
@@ -414,7 +421,8 @@
     precon = scale * residual
     left_precon = left_scale * left_residual
     iface = c_high.shape[1]
-    load = added_up(precon, own_ref[...], iface) - added_up(left_precon, left_index[...], iface)
+    both_index = jnp.concatenate([own_ref[...], left_index[...]], axis=1)
+    load = added_up(jnp.concatenate([precon, -left_precon], axis=1), both_index, iface)
     through = schur_product(load, top_high, top_low, s_high, s_low)
     norm_here = row_sum(residual * precon)
     copy = forces(load, through, norm_here, c_high, c_low, corner_ref, cases, send_hbm, send, sems)
@@ -528,7 +536,7 @@
     fetched_here = (schur_inverse, coarse_coupling, own_dof, corner_index)
     half = (2 * width, width)
     share = (width + width // 2, width)
-    top = iface // 3 // LANES * LANES
+    top = iface // 2 // LANES * LANES
     *tops, s_high, s_low, c_high, c_low, own_coupling, load, index, own, share = call(
         functools.partial(prepare_kernel, cases),
         [
@@ -555,13 +563,24 @@
     )
     if is_paired(width):
         far = exchanged(share, "crs", 2)
-    inv_high, inv_low = call(
-        inverse_kernel,
-        [((corners, width), BF16)] * 2,
-        (corner_inverse,),
-        [HB],
-        [pltpu.VMEM((corners, width), F32), pltpu.SemaphoreType.DMA((slabs,))],
-    )
+    inverse_parts = [((corners, width), BF16)] * 2
+    inverse_scratch = [pltpu.VMEM((corners, width), F32), pltpu.SemaphoreType.DMA((slabs,))]
+    if is_paired(width):
+        inv_high, inv_low, far_high, far_low = call(
+            inverse_kernel,
+            inverse_parts + [(far.shape, BF16)] * 2,
+            (far, corner_inverse),
+            [VM, HB],
+            inverse_scratch,
+        )
+    else:
+        inv_high, inv_low = call(
+            lambda source, high, low, *rest: inverse_kernel(None, source, high, low, None, None, *rest),
+            inverse_parts,
+            (corner_inverse,),
+            [HB],
+            inverse_scratch,
+        )
     outgoing = [pltpu.VMEM((devices, FOLD, LANES), F32), pltpu.SemaphoreType.DMA((1,))]
     send, one_sent, two_sent, left_index = call(
         functools.partial(first_kernel, cases),
@@ -575,7 +594,7 @@
         stored=1,
     )
 
-    more = iface // 64 * 16
+    more = iface // 96 * 16
 
     def gathered(send, beside, ahead):
         everyone = lax.all_to_all(send, ("sub", "crs"), 0, 0)
@@ -585,8 +604,8 @@
             x, total, sums, near, *fetched = call(
                 functools.partial(pair_kernel, cases, top),
                 [(row, F32), *outs] + [((more, iface), F32)] * ahead,
-                (everyone, far, inv_high, inv_low, schur_inverse),
-                [VM] * 4 + [HB],
+                (everyone, far_high, far_low, inv_high, inv_low, schur_inverse),
+                [VM] * 5 + [HB],
                 [pltpu.SemaphoreType.DMA((1,))] * ahead,
             )
             if beside is not None:

time: 39.4 us -> 39.5 us (level)
  no operation moved by 1% of the time
where the time goes in v9:
time: 39.5 us; the launch traced here: 39.1 us
  starting transfers between devices  20.3 us (51%)
  Pallas kernels  11.1 us (28%)
  waiting for transfers between devices  6.27 us (16%)
  between operations  1.38 us (3%)
    pallas_call x9, Pallas kernels, call(): pl.pallas_call(kernel, out_shape=[jax.ShapeDtypeStruct(shape, kind) for s...  11.1 us
    ppermute x2, starting transfers between devices, passed_along(): return lax.ppermute(value, axis, pairs)  7.62 us
    all_to_all x2, starting transfers between devices, gathered(): everyone = lax.all_to_all(send, ('sub', 'crs'), 0, 0)  6.17 us
    ppermute x1, starting transfers between devices, per_device(): two = lax.ppermute(two_sent, 'sub', rounds[1])  4.62 us
    all_to_all x2, waiting for transfers between devices, gathered(): everyone = lax.all_to_all(send, ('sub', 'crs'), 0, 0)  3.99 us
    ppermute x3, starting transfers between devices, exchanged(): return lax.ppermute(value, axis, pairs)  1.91 us
    ppermute x2, waiting for transfers between devices, passed_along(): return lax.ppermute(value, axis, pairs)  1.18 us
    ppermute x3, waiting for transfers between devices, exchanged(): return lax.ppermute(value, axis, pairs)  1.1 us
  transfers between devices with their start and end apart: 9, of which 4 were waited for; matrix products, arithmetic and copies ran while one was open for 0% of the time, Pallas kernels for 20%

profile of v9, /device:TPU:0, one launch (start us, length us, event | category | flops | bytes accessed | tf_op | source)
XLA Modules:
  0.0 39.1 jit_solution(10935648264931259586)
XLA Ops:
  1.3 0.8 %shard_map.104.pack_ref.refs_5_ = f32[8,384]{1,0:T(8,128)S(1)} custom-call(s32[1,1]{1,0:T(1,128)S(6)} %copy.13.live_ref, f32[6,1,384]{2,1,0:T(1,128)} %bitcast.7, f32[1,1,384]{2,1,0:T(1,128)} %scale_hbm.1, s32[1,1,384]{2,1,0:T(1,128)} %nbr_hbm.1), custom_call_target="tpu_custom_call" | custom-call | tf_op jit(solution)/shard_map/pallas_call | solution.py:481
  2.0 3.0 %collective-permute-start = (f32[8,384]{1,0:T(8,128)S(1)}, f32[8,384]{1,0:T(8,128)S(1)}, u32[]{:S(2)}, u32[]{:S(2)}) collective-permute-start(f32[8,384]{1,0:T(8,128)S(1)} %shard_map.104.pack_ref.refs_5_), channel_id=1, source_target_pairs={{0,4},{4,8},{8,12},{12,16},{16,20},{20,24},{24,28},{28,0},{1,5},{5... | collective-permute-start | bytes 36872 | tf_op jit(solution)/shard_map/ppermute | solution.py:496
  5.1 2.0 %shard_map.105 = (bf16[384,768]{1,0:T(8,128)(2,1)S(1)}, bf16[384,768]{1,0:T(8,128)(2,1)S(1)}, bf16[384,768]{1,0:T(8,128)(2,1)S(1)}, bf16[384,768]{1,0:T(8,128)(2...) custom-call(f32[8,384]{1,0:T(8,128)S(1)} %shard_map.104.pack_ref.ref, ...), custom_call_target="tpu_custom_call" | custom-call | bytes 33554432 | tf_op jit(solution)/shard_map/pallas_call | solution.py:481
  7.0 1.6 %collective-permute-start.1 = (f32[384,256]{1,0:T(8,128)S(1)}, f32[384,256]{1,0:T(8,128)S(1)}, u32[]{:S(2)}, u32[]{:S(2)}) collective-permute-start(f32[384,256]{1,0:T(8,128)S(1)} %get-tuple-element.51), channel_id=1, source_target_pairs={{0,2},{1,3},{2,0},{3,1},{4,6},{5,7},{6,4},{7,5},{8,10},{9,11},{10,... | collective-permute-start | bytes 1179656 | tf_op jit(solution)/shard_map/ppermute | solution.py:501
  8.6 1.2 %collective-permute-done.left_ref.refs_6_ = f32[8,384]{1,0:T(8,128)S(1)} collective-permute-done((f32[8,384]{1,0:T(8,128)S(1)}, f32[8,384]{1,0:T(8,128)S(1)}, u32[]{:S(2)}, u32[]{:S(2)}) %collective-permute-start) | collective-permute-done | bytes 12320 | tf_op jit(solution)/shard_map/ppermute | solution.py:496
  9.8 1.3 %shard_map.106 = (f32[32,2,128]{2,1,0:T(2,128)}, f32[32,384]{1,0:T(8,128)S(1)}, f32[32,384]{1,0:T(8,128)S(1)}, s32[1,384]{1,0:T(1,128)S(1)}) custom-call(f32[8,384]{1,0:T(8,128)S(1)} %collective-permute-done.left_ref.refs_6_, f32[8,384]{1,0:T(8,128)S(1)} %shard_map.104.pack_ref.refs_5_, f32[8,768]{1,0:T(8,128)S(1)} %get-tuple-element.40.load_ref, ...), custom_call_target="tpu_custom_call" | custom-call | flops 40000000000 | bytes 1 | tf_op jit(solution)/shard_map/pallas_call | solution.py:481
  11.1 3.3 %all-to-all-start = ((f32[32,2,128]{2,1,0:T(2,128)}), f32[32,2,128]{2,1,0:T(2,128)S(1)}, u32[]{:S(2)}, u32[]{:S(2)}) async-start(f32[32,2,128]{2,1,0:T(2,128)} %get-tuple-element.50), calls=%async_computation | async-start | bytes 65536 | tf_op jit(solution)/shard_map/all_to_all | solution.py:600
  14.4 4.6 %collective-permute-start.3 = (f32[32,384]{1,0:T(8,128)S(1)}, f32[32,384]{1,0:T(8,128)S(1)}, u32[]{:S(2)}, u32[]{:S(2)}) collective-permute-start(f32[32,384]{1,0:T(8,128)S(1)} %get-tuple-element.61.refs_8_), channel_id=1, source_target_pairs={{4,8},{12,16},{20,24},{28,0},{8,4},{16,12},{24,20},{0,28},{5,9},{1... | collective-permute-start | bytes 147464 | tf_op jit(solution)/shard_map/ppermute | solution.py:638
  19.0 0.0 collective-permute-start.4
  19.0 0.0 collective-permute-done.1.far_ref
  19.0 1.4 %shard_map.107 = (bf16[1024,256]{1,0:T(8,128)(2,1)S(1)}, bf16[1024,256]{1,0:T(8,128)(2,1)S(1)}, bf16[384,256]{1,0:T(8,128)(2,1)S(1)}, bf16[384,256]{1,0:T(8,128)(2,1)S(1)}) custom-call(f32[384,256]{1,0:T(8,128)S(1)} %collective-permute-done.1.far_ref, f32[1024,256]{1,0:T(8,128)} %inverse_hbm.3), custom_call_target="tpu_custom_call" | custom-call | tf_op jit(solution)/shard_map/pallas_call | solution.py:481
  20.4 1.3 %all-to-all-done.all_ref = f32[32,2,128]{2,1,0:T(2,128)S(1)} async-done(((f32[32,2,128]{2,1,0:T(2,128)}), f32[32,2,128]{2,1,0:T(2,128)S(1)}, u32[]{:S(2)}, u32[]{:S(2)}) %all-to-all-start) | async-done | bytes 32800 | tf_op jit(solution)/shard_map/all_to_all | solution.py:600
  21.8 1.0 %shard_map.108 = (f32[8,1024]{1,0:T(8,128)S(1)}, f32[8,1024]{1,0:T(8,128)S(1)}, f32[8,128]{1,0:T(8,128)S(1)}, s32[8,128]{1,0:T(8,128)S(1)}, f32[128,768]{1,0:T(8,128)S(1)}) custom-call(f32[32,2,128]{2,1,0:T(2,128)S(1)} %all-to-all-done.all_ref, bf16[384,256]{1,0:T(8,128)(2,1)S(1)} %get-tuple-element.52.far_high, ...), custom_call_target="tpu_custom_call" | custom-call | tf_op jit(solution)/shard_map/pallas_call | solution.py:481
  22.8 0.2 collective-permute-start.2
  22.9 1.3 %shard_map.109 = (bf16[384,768]{1,0:T(8,128)(2,1)S(1)}, bf16[384,768]{1,0:T(8,128)(2,1)S(1)}) custom-call(f32[128,768]{1,0:T(8,128)S(1)} %get-tuple-element.62.rows_ref, f32[1,1,768,768]{3,2,1,0:T(8,128)} %schur_hbm.7), custom_call_target="tpu_custom_call" | custom-call | tf_op jit(solution)/shard_map/pallas_call | solution.py:481
  24.2 0.0 collective-permute-done.3.refs_9_
  24.2 0.0 collective-permute-done.4.refs_10_
  24.2 0.0 collective-permute-done.2.refs_1_
  24.3 1.7 %shard_map.110 = (f32[32,2,128]{2,1,0:T(2,128)}, f32[8,384]{1,0:T(8,128)S(1)}, f32[16,384]{1,0:T(8,128)S(1)}, f32[128,384]{1,0:T(8,128)S(1)}, f32[8,128]{1,0:T(8,128)S(1)}) custom-call(f32[8,1024]{1,0:T(8,128)S(1)} %get-tuple-element.56.refs_0_, f32[8,1024]{1,0:T(8,128)S(1)} %collective-permute-done.2.refs_1_, f32[8,1024]{1,0:T(8,128)S(1)} %get-tuple-element.57.refs_2_, ...), custom_call_target="tpu_custom_call" | custom-call | tf_op jit(solution)/shard_map/pallas_call | solution.py:481
  26.0 2.8 %all-to-all-start.1 = ((f32[32,2,128]{2,1,0:T(2,128)}), f32[32,2,128]{2,1,0:T(2,128)S(1)}, u32[]{:S(2)}, u32[]{:S(2)}) async-start(f32[32,2,128]{2,1,0:T(2,128)} %get-tuple-element.66), calls=%async_computation.1 | async-start | bytes 65536 | tf_op jit(solution)/shard_map/all_to_all | solution.py:600
  28.8 4.6 %collective-permute-start.5 = (f32[8,384]{1,0:T(8,128)S(1)}, f32[8,384]{1,0:T(8,128)S(1)}, u32[]{:S(2)}, u32[]{:S(2)}) collective-permute-start(f32[8,384]{1,0:T(8,128)S(1)} %get-tuple-element.68), channel_id=1, source_target_pairs={{0,28},{4,0},{8,4},{12,8},{16,12},{20,16},{24,20},{28,24},{1,29},{... | collective-permute-start | bytes 36872 | tf_op jit(solution)/shard_map/ppermute | solution.py:496
  33.4 2.6 %all-to-all-done.1.all_ref = f32[32,2,128]{2,1,0:T(2,128)S(1)} async-done(((f32[32,2,128]{2,1,0:T(2,128)}), f32[32,2,128]{2,1,0:T(2,128)S(1)}, u32[]{:S(2)}, u32[]{:S(2)}) %all-to-all-start.1) | async-done | bytes 32800 | tf_op jit(solution)/shard_map/all_to_all | solution.py:600
  36.1 0.8 %shard_map.111 = (f32[8,1024]{1,0:T(8,128)S(1)}, f32[8,1024]{1,0:T(8,128)S(1)}, f32[8,128]{1,0:T(8,128)S(1)}, s32[8,128]{1,0:T(8,128)S(1)}) custom-call(f32[32,2,128]{2,1,0:T(2,128)S(1)} %all-to-all-done.1.all_ref, bf16[384,256]{1,0:T(8,128)(2,1)S(1)} %get-tuple-element.52.far_high, bf16[384,256]{1,0:T(8,128)(2,1)S(1)} %get-tuple-element.53.far_low, ...), custom_call_target="tpu_custom_call" | custom-call | tf_op jit(solution)/shard_map/pallas_call | solution.py:481
  36.9 0.0 collective-permute-done.5.refs_6_
  36.9 0.2 collective-permute-start.6
  37.1 1.1 %collective-permute-done.6.refs_1_ = f32[8,1024]{1,0:T(8,128)S(1)} collective-permute-done((f32[8,1024]{1,0:T(8,128)S(1)}, f32[8,1024]{1,0:T(8,128)S(1)}, u32[]{:S(2)}, u32[]{:S(2)}) %collective-permute-start.6) | collective-permute-done | bytes 32800 | tf_op jit(solution)/shard_map/ppermute | solution.py:501
  38.2 0.9 %shard_map.112 = (f32[6,1,384]{2,1,0:T(1,128)}, f32[6,1,384]{2,1,0:T(1,128)}) custom-call(f32[8,1024]{1,0:T(8,128)S(1)} %get-tuple-element.69.refs_0_, f32[8,1024]{1,0:T(8,128)S(1)} %collective-permute-done.6.refs_1_, f32[8,1024]{1,0:T(8,128)S(1)} %get-tuple-element.70.refs_2_, f32[8,128]{1,0:T(8,128)S(1)} %get-tuple-element.71.refs_3_, ...), custom_call_target="tpu_custom_call" | custom-call | tf_op jit(solution)/shard_map/pallas_call | solution.py:481
Async XLA Ops:
  2.0 7.7 %collective-permute-start = (f32[8,384]{1,0:T(8,128)S(1)}, f32[8,384]{1,0:T(8,128)S(1)}, u32[]{:S(2)}, u32[]{:S(2)}) collective-permute-start(f32[8,384]{1,0:T(8,128)S(1)} %shard_map.104.pack_ref.refs_5_), channel_id=1, source_target_pairs={{0,4},{4,8},{8,12},{12,16},{16,20},{20,24},{24,28},{28,0},{1,5},{5... | collective-permute-start | bytes 36872 | tf_op jit(solution)/shard_map/ppermute | solution.py:496
  7.0 12.0 %collective-permute-start.1 = (f32[384,256]{1,0:T(8,128)S(1)}, f32[384,256]{1,0:T(8,128)S(1)}, u32[]{:S(2)}, u32[]{:S(2)}) collective-permute-start(f32[384,256]{1,0:T(8,128)S(1)} %get-tuple-element.51), channel_id=1, source_target_pairs={{0,2},{1,3},{2,0},{3,1},{4,6},{5,7},{6,4},{7,5},{8,10},{9,11},{10,... | collective-permute-start | bytes 1179656 | tf_op jit(solution)/shard_map/ppermute | solution.py:501
  11.1 10.7 %all-to-all-start = ((f32[32,2,128]{2,1,0:T(2,128)}), f32[32,2,128]{2,1,0:T(2,128)S(1)}, u32[]{:S(2)}, u32[]{:S(2)}) async-start(f32[32,2,128]{2,1,0:T(2,128)} %get-tuple-element.50), calls=%async_computation | async-start | bytes 65536 | tf_op jit(solution)/shard_map/all_to_all | solution.py:600
  14.4 9.8 %collective-permute-start.3 = (f32[32,384]{1,0:T(8,128)S(1)}, f32[32,384]{1,0:T(8,128)S(1)}, u32[]{:S(2)}, u32[]{:S(2)}) collective-permute-start(f32[32,384]{1,0:T(8,128)S(1)} %get-tuple-element.61.refs_8_), channel_id=1, source_target_pairs={{4,8},{12,16},{20,24},{28,0},{8,4},{16,12},{24,20},{0,28},{5,9},{1... | collective-permute-start | bytes 147464 | tf_op jit(solution)/shard_map/ppermute | solution.py:638
  19.0 5.2 %collective-permute-start.4 = (f32[32,384]{1,0:T(8,128)S(1)}, f32[32,384]{1,0:T(8,128)S(1)}, u32[]{:S(2)}, u32[]{:S(2)}) collective-permute-start(f32[32,384]{1,0:T(8,128)S(1)} %get-tuple-element.60.refs_7_), channel_id=1, source_target_pairs={{0,4},{8,12},{16,20},{24,28},{4,0},{12,8},{20,16},{28,24},{1,5},{9... | collective-permute-start | bytes 147464 | tf_op jit(solution)/shard_map/ppermute | solution.py:639
  22.8 1.5 %collective-permute-start.2 = (f32[8,1024]{1,0:T(8,128)S(1)}, f32[8,1024]{1,0:T(8,128)S(1)}, u32[]{:S(2)}, u32[]{:S(2)}) collective-permute-start(f32[8,1024]{1,0:T(8,128)S(1)} %get-tuple-element.56.refs_0_), channel_id=1, source_target_pairs={{0,1},{1,0},{2,3},{3,2},{4,5},{5,4},{6,7},{7,6},{8,9},{9,8},{10,11... | collective-permute-start | bytes 98312 | tf_op jit(solution)/shard_map/ppermute | solution.py:501
  26.0 10.1 %all-to-all-start.1 = ((f32[32,2,128]{2,1,0:T(2,128)}), f32[32,2,128]{2,1,0:T(2,128)S(1)}, u32[]{:S(2)}, u32[]{:S(2)}) async-start(f32[32,2,128]{2,1,0:T(2,128)} %get-tuple-element.66), calls=%async_computation.1 | async-start | bytes 65536 | tf_op jit(solution)/shard_map/all_to_all | solution.py:600
  28.8 8.1 %collective-permute-start.5 = (f32[8,384]{1,0:T(8,128)S(1)}, f32[8,384]{1,0:T(8,128)S(1)}, u32[]{:S(2)}, u32[]{:S(2)}) collective-permute-start(f32[8,384]{1,0:T(8,128)S(1)} %get-tuple-element.68), channel_id=1, source_target_pairs={{0,28},{4,0},{8,4},{12,8},{16,12},{20,16},{24,20},{28,24},{1,29},{... | collective-permute-start | bytes 36872 | tf_op jit(solution)/shard_map/ppermute | solution.py:496
  36.9 1.3 %collective-permute-start.6 = (f32[8,1024]{1,0:T(8,128)S(1)}, f32[8,1024]{1,0:T(8,128)S(1)}, u32[]{:S(2)}, u32[]{:S(2)}) collective-permute-start(f32[8,1024]{1,0:T(8,128)S(1)} %get-tuple-element.69.refs_0_), channel_id=1, source_target_pairs={{0,1},{1,0},{2,3},{3,2},{4,5},{5,4},{6,7},{7,6},{8,9},{9,8},{10,11... | collective-permute-start | bytes 98312 | tf_op jit(solution)/shard_map/ppermute | solution.py:501

commit v10 on v9

--- a/solution.py
+++ b/solution.py
@@ -289,9 +289,9 @@
     @always
     def _():
         held = own_coupling.shape[0]
-        one_ref[:ROWS], two_ref[:ROWS] = dealt(
-            taken(through, own_ref[...]), taken(through, left_index)
-        )
+        slots = taken(through, jnp.concatenate([own_ref[...], left_index], axis=1))
+        records = left_index.shape[1]
+        one_ref[:ROWS], two_ref[:ROWS] = dealt(slots[:, :records], slots[:, records:])
         coupling = c_high[...].astype(F32) + c_low[...].astype(F32)
         one_ref[ROWS:], two_ref[ROWS:] = dealt(
             own_coupling[...], taken(coupling, left_index)[:held]

time: 39.5 us -> 39.5 us (level)
  no operation moved by 1% of the time
where the time goes in v10:
time: 39.5 us; the launch traced here: 39.1 us
  starting transfers between devices  20.3 us (51%)
  Pallas kernels  11.1 us (28%)
  waiting for transfers between devices  6.27 us (16%)
  between operations  1.38 us (3%)
    pallas_call x9, Pallas kernels, call(): pl.pallas_call(kernel, out_shape=[jax.ShapeDtypeStruct(shape, kind) for s...  11.1 us
    ppermute x2, starting transfers between devices, passed_along(): return lax.ppermute(value, axis, pairs)  7.62 us
    all_to_all x2, starting transfers between devices, gathered(): everyone = lax.all_to_all(send, ('sub', 'crs'), 0, 0)  6.17 us
    ppermute x1, starting transfers between devices, per_device(): two = lax.ppermute(two_sent, 'sub', rounds[1])  4.62 us
    all_to_all x2, waiting for transfers between devices, gathered(): everyone = lax.all_to_all(send, ('sub', 'crs'), 0, 0)  3.99 us
    ppermute x3, starting transfers between devices, exchanged(): return lax.ppermute(value, axis, pairs)  1.91 us
    ppermute x2, waiting for transfers between devices, passed_along(): return lax.ppermute(value, axis, pairs)  1.18 us
    ppermute x3, waiting for transfers between devices, exchanged(): return lax.ppermute(value, axis, pairs)  1.1 us
  transfers between devices with their start and end apart: 9, of which 4 were waited for; matrix products, arithmetic and copies ran while one was open for 0% of the time, Pallas kernels for 20%

profile of v10, /device:TPU:0, one launch (start us, length us, event | category | flops | bytes accessed | tf_op | source)
XLA Modules:
  0.0 39.1 jit_solution(15587131775524896795)
XLA Ops:
  1.3 0.8 %shard_map.104.pack_ref.refs_5_ = f32[8,384]{1,0:T(8,128)S(1)} custom-call(s32[1,1]{1,0:T(1,128)S(6)} %copy.13.live_ref, f32[6,1,384]{2,1,0:T(1,128)} %bitcast.7, f32[1,1,384]{2,1,0:T(1,128)} %scale_hbm.1, s32[1,1,384]{2,1,0:T(1,128)} %nbr_hbm.1), custom_call_target="tpu_custom_call" | custom-call | tf_op jit(solution)/shard_map/pallas_call | solution.py:481
  2.0 3.0 %collective-permute-start = (f32[8,384]{1,0:T(8,128)S(1)}, f32[8,384]{1,0:T(8,128)S(1)}, u32[]{:S(2)}, u32[]{:S(2)}) collective-permute-start(f32[8,384]{1,0:T(8,128)S(1)} %shard_map.104.pack_ref.refs_5_), channel_id=1, source_target_pairs={{0,4},{4,8},{8,12},{12,16},{16,20},{20,24},{24,28},{28,0},{1,5},{5... | collective-permute-start | bytes 36872 | tf_op jit(solution)/shard_map/ppermute | solution.py:496
  5.1 2.0 %shard_map.105 = (bf16[384,768]{1,0:T(8,128)(2,1)S(1)}, bf16[384,768]{1,0:T(8,128)(2,1)S(1)}, bf16[384,768]{1,0:T(8,128)(2,1)S(1)}, bf16[384,768]{1,0:T(8,128)(2...) custom-call(f32[8,384]{1,0:T(8,128)S(1)} %shard_map.104.pack_ref.ref, ...), custom_call_target="tpu_custom_call" | custom-call | bytes 33554432 | tf_op jit(solution)/shard_map/pallas_call | solution.py:481
  7.0 1.6 %collective-permute-start.1 = (f32[384,256]{1,0:T(8,128)S(1)}, f32[384,256]{1,0:T(8,128)S(1)}, u32[]{:S(2)}, u32[]{:S(2)}) collective-permute-start(f32[384,256]{1,0:T(8,128)S(1)} %get-tuple-element.51), channel_id=1, source_target_pairs={{0,2},{1,3},{2,0},{3,1},{4,6},{5,7},{6,4},{7,5},{8,10},{9,11},{10,... | collective-permute-start | bytes 1179656 | tf_op jit(solution)/shard_map/ppermute | solution.py:501
  8.6 1.2 %collective-permute-done.left_ref.refs_6_ = f32[8,384]{1,0:T(8,128)S(1)} collective-permute-done((f32[8,384]{1,0:T(8,128)S(1)}, f32[8,384]{1,0:T(8,128)S(1)}, u32[]{:S(2)}, u32[]{:S(2)}) %collective-permute-start) | collective-permute-done | bytes 12320 | tf_op jit(solution)/shard_map/ppermute | solution.py:496
  9.8 1.3 %shard_map.106 = (f32[32,2,128]{2,1,0:T(2,128)}, f32[32,384]{1,0:T(8,128)S(1)}, f32[32,384]{1,0:T(8,128)S(1)}, s32[1,384]{1,0:T(1,128)S(1)}) custom-call(f32[8,384]{1,0:T(8,128)S(1)} %collective-permute-done.left_ref.refs_6_, f32[8,384]{1,0:T(8,128)S(1)} %shard_map.104.pack_ref.refs_5_, f32[8,768]{1,0:T(8,128)S(1)} %get-tuple-element.40.load_ref, ...), custom_call_target="tpu_custom_call" | custom-call | flops 40000000000 | bytes 1 | tf_op jit(solution)/shard_map/pallas_call | solution.py:481
  11.1 3.3 %all-to-all-start = ((f32[32,2,128]{2,1,0:T(2,128)}), f32[32,2,128]{2,1,0:T(2,128)S(1)}, u32[]{:S(2)}, u32[]{:S(2)}) async-start(f32[32,2,128]{2,1,0:T(2,128)} %get-tuple-element.50), calls=%async_computation | async-start | bytes 65536 | tf_op jit(solution)/shard_map/all_to_all | solution.py:600
  14.4 4.6 %collective-permute-start.3 = (f32[32,384]{1,0:T(8,128)S(1)}, f32[32,384]{1,0:T(8,128)S(1)}, u32[]{:S(2)}, u32[]{:S(2)}) collective-permute-start(f32[32,384]{1,0:T(8,128)S(1)} %get-tuple-element.61.refs_8_), channel_id=1, source_target_pairs={{4,8},{12,16},{20,24},{28,0},{8,4},{16,12},{24,20},{0,28},{5,9},{1... | collective-permute-start | bytes 147464 | tf_op jit(solution)/shard_map/ppermute | solution.py:638
  19.0 0.0 collective-permute-start.4
  19.0 0.0 collective-permute-done.1.far_ref
  19.0 1.4 %shard_map.107 = (bf16[1024,256]{1,0:T(8,128)(2,1)S(1)}, bf16[1024,256]{1,0:T(8,128)(2,1)S(1)}, bf16[384,256]{1,0:T(8,128)(2,1)S(1)}, bf16[384,256]{1,0:T(8,128)(2,1)S(1)}) custom-call(f32[384,256]{1,0:T(8,128)S(1)} %collective-permute-done.1.far_ref, f32[1024,256]{1,0:T(8,128)} %inverse_hbm.3), custom_call_target="tpu_custom_call" | custom-call | tf_op jit(solution)/shard_map/pallas_call | solution.py:481
  20.4 1.3 %all-to-all-done.all_ref = f32[32,2,128]{2,1,0:T(2,128)S(1)} async-done(((f32[32,2,128]{2,1,0:T(2,128)}), f32[32,2,128]{2,1,0:T(2,128)S(1)}, u32[]{:S(2)}, u32[]{:S(2)}) %all-to-all-start) | async-done | bytes 32800 | tf_op jit(solution)/shard_map/all_to_all | solution.py:600
  21.8 1.0 %shard_map.108 = (f32[8,1024]{1,0:T(8,128)S(1)}, f32[8,1024]{1,0:T(8,128)S(1)}, f32[8,128]{1,0:T(8,128)S(1)}, s32[8,128]{1,0:T(8,128)S(1)}, f32[128,768]{1,0:T(8,128)S(1)}) custom-call(f32[32,2,128]{2,1,0:T(2,128)S(1)} %all-to-all-done.all_ref, bf16[384,256]{1,0:T(8,128)(2,1)S(1)} %get-tuple-element.52.far_high, ...), custom_call_target="tpu_custom_call" | custom-call | tf_op jit(solution)/shard_map/pallas_call | solution.py:481
  22.8 0.2 collective-permute-start.2
  22.9 1.3 %shard_map.109 = (bf16[384,768]{1,0:T(8,128)(2,1)S(1)}, bf16[384,768]{1,0:T(8,128)(2,1)S(1)}) custom-call(f32[128,768]{1,0:T(8,128)S(1)} %get-tuple-element.62.rows_ref, f32[1,1,768,768]{3,2,1,0:T(8,128)} %schur_hbm.7), custom_call_target="tpu_custom_call" | custom-call | tf_op jit(solution)/shard_map/pallas_call | solution.py:481
  24.2 0.0 collective-permute-done.3.refs_9_
  24.2 0.0 collective-permute-done.4.refs_10_
  24.2 0.0 collective-permute-done.2.refs_1_
  24.3 1.7 %shard_map.110 = (f32[32,2,128]{2,1,0:T(2,128)}, f32[8,384]{1,0:T(8,128)S(1)}, f32[16,384]{1,0:T(8,128)S(1)}, f32[128,384]{1,0:T(8,128)S(1)}, f32[8,128]{1,0:T(8,128)S(1)}) custom-call(f32[8,1024]{1,0:T(8,128)S(1)} %get-tuple-element.56.refs_0_, f32[8,1024]{1,0:T(8,128)S(1)} %collective-permute-done.2.refs_1_, f32[8,1024]{1,0:T(8,128)S(1)} %get-tuple-element.57.refs_2_, ...), custom_call_target="tpu_custom_call" | custom-call | tf_op jit(solution)/shard_map/pallas_call | solution.py:481
  26.0 2.8 %all-to-all-start.1 = ((f32[32,2,128]{2,1,0:T(2,128)}), f32[32,2,128]{2,1,0:T(2,128)S(1)}, u32[]{:S(2)}, u32[]{:S(2)}) async-start(f32[32,2,128]{2,1,0:T(2,128)} %get-tuple-element.66), calls=%async_computation.1 | async-start | bytes 65536 | tf_op jit(solution)/shard_map/all_to_all | solution.py:600
  28.8 4.6 %collective-permute-start.5 = (f32[8,384]{1,0:T(8,128)S(1)}, f32[8,384]{1,0:T(8,128)S(1)}, u32[]{:S(2)}, u32[]{:S(2)}) collective-permute-start(f32[8,384]{1,0:T(8,128)S(1)} %get-tuple-element.68), channel_id=1, source_target_pairs={{0,28},{4,0},{8,4},{12,8},{16,12},{20,16},{24,20},{28,24},{1,29},{... | collective-permute-start | bytes 36872 | tf_op jit(solution)/shard_map/ppermute | solution.py:496
  33.4 2.6 %all-to-all-done.1.all_ref = f32[32,2,128]{2,1,0:T(2,128)S(1)} async-done(((f32[32,2,128]{2,1,0:T(2,128)}), f32[32,2,128]{2,1,0:T(2,128)S(1)}, u32[]{:S(2)}, u32[]{:S(2)}) %all-to-all-start.1) | async-done | bytes 32800 | tf_op jit(solution)/shard_map/all_to_all | solution.py:600
  36.1 0.8 %shard_map.111 = (f32[8,1024]{1,0:T(8,128)S(1)}, f32[8,1024]{1,0:T(8,128)S(1)}, f32[8,128]{1,0:T(8,128)S(1)}, s32[8,128]{1,0:T(8,128)S(1)}) custom-call(f32[32,2,128]{2,1,0:T(2,128)S(1)} %all-to-all-done.1.all_ref, bf16[384,256]{1,0:T(8,128)(2,1)S(1)} %get-tuple-element.52.far_high, bf16[384,256]{1,0:T(8,128)(2,1)S(1)} %get-tuple-element.53.far_low, ...), custom_call_target="tpu_custom_call" | custom-call | tf_op jit(solution)/shard_map/pallas_call | solution.py:481
  36.9 0.0 collective-permute-done.5.refs_6_
  36.9 0.2 collective-permute-start.6
  37.1 1.1 %collective-permute-done.6.refs_1_ = f32[8,1024]{1,0:T(8,128)S(1)} collective-permute-done((f32[8,1024]{1,0:T(8,128)S(1)}, f32[8,1024]{1,0:T(8,128)S(1)}, u32[]{:S(2)}, u32[]{:S(2)}) %collective-permute-start.6) | collective-permute-done | bytes 32800 | tf_op jit(solution)/shard_map/ppermute | solution.py:501
  38.2 0.9 %shard_map.112 = (f32[6,1,384]{2,1,0:T(1,128)}, f32[6,1,384]{2,1,0:T(1,128)}) custom-call(f32[8,1024]{1,0:T(8,128)S(1)} %get-tuple-element.69.refs_0_, f32[8,1024]{1,0:T(8,128)S(1)} %collective-permute-done.6.refs_1_, f32[8,1024]{1,0:T(8,128)S(1)} %get-tuple-element.70.refs_2_, f32[8,128]{1,0:T(8,128)S(1)} %get-tuple-element.71.refs_3_, ...), custom_call_target="tpu_custom_call" | custom-call | tf_op jit(solution)/shard_map/pallas_call | solution.py:481
Async XLA Ops:
  2.0 7.7 %collective-permute-start = (f32[8,384]{1,0:T(8,128)S(1)}, f32[8,384]{1,0:T(8,128)S(1)}, u32[]{:S(2)}, u32[]{:S(2)}) collective-permute-start(f32[8,384]{1,0:T(8,128)S(1)} %shard_map.104.pack_ref.refs_5_), channel_id=1, source_target_pairs={{0,4},{4,8},{8,12},{12,16},{16,20},{20,24},{24,28},{28,0},{1,5},{5... | collective-permute-start | bytes 36872 | tf_op jit(solution)/shard_map/ppermute | solution.py:496
  7.0 12.0 %collective-permute-start.1 = (f32[384,256]{1,0:T(8,128)S(1)}, f32[384,256]{1,0:T(8,128)S(1)}, u32[]{:S(2)}, u32[]{:S(2)}) collective-permute-start(f32[384,256]{1,0:T(8,128)S(1)} %get-tuple-element.51), channel_id=1, source_target_pairs={{0,2},{1,3},{2,0},{3,1},{4,6},{5,7},{6,4},{7,5},{8,10},{9,11},{10,... | collective-permute-start | bytes 1179656 | tf_op jit(solution)/shard_map/ppermute | solution.py:501
  11.1 10.7 %all-to-all-start = ((f32[32,2,128]{2,1,0:T(2,128)}), f32[32,2,128]{2,1,0:T(2,128)S(1)}, u32[]{:S(2)}, u32[]{:S(2)}) async-start(f32[32,2,128]{2,1,0:T(2,128)} %get-tuple-element.50), calls=%async_computation | async-start | bytes 65536 | tf_op jit(solution)/shard_map/all_to_all | solution.py:600
  14.4 9.8 %collective-permute-start.3 = (f32[32,384]{1,0:T(8,128)S(1)}, f32[32,384]{1,0:T(8,128)S(1)}, u32[]{:S(2)}, u32[]{:S(2)}) collective-permute-start(f32[32,384]{1,0:T(8,128)S(1)} %get-tuple-element.61.refs_8_), channel_id=1, source_target_pairs={{4,8},{12,16},{20,24},{28,0},{8,4},{16,12},{24,20},{0,28},{5,9},{1... | collective-permute-start | bytes 147464 | tf_op jit(solution)/shard_map/ppermute | solution.py:638
  19.0 5.2 %collective-permute-start.4 = (f32[32,384]{1,0:T(8,128)S(1)}, f32[32,384]{1,0:T(8,128)S(1)}, u32[]{:S(2)}, u32[]{:S(2)}) collective-permute-start(f32[32,384]{1,0:T(8,128)S(1)} %get-tuple-element.60.refs_7_), channel_id=1, source_target_pairs={{0,4},{8,12},{16,20},{24,28},{4,0},{12,8},{20,16},{28,24},{1,5},{9... | collective-permute-start | bytes 147464 | tf_op jit(solution)/shard_map/ppermute | solution.py:639
  22.8 1.5 %collective-permute-start.2 = (f32[8,1024]{1,0:T(8,128)S(1)}, f32[8,1024]{1,0:T(8,128)S(1)}, u32[]{:S(2)}, u32[]{:S(2)}) collective-permute-start(f32[8,1024]{1,0:T(8,128)S(1)} %get-tuple-element.56.refs_0_), channel_id=1, source_target_pairs={{0,1},{1,0},{2,3},{3,2},{4,5},{5,4},{6,7},{7,6},{8,9},{9,8},{10,11... | collective-permute-start | bytes 98312 | tf_op jit(solution)/shard_map/ppermute | solution.py:501
  26.0 10.1 %all-to-all-start.1 = ((f32[32,2,128]{2,1,0:T(2,128)}), f32[32,2,128]{2,1,0:T(2,128)S(1)}, u32[]{:S(2)}, u32[]{:S(2)}) async-start(f32[32,2,128]{2,1,0:T(2,128)} %get-tuple-element.66), calls=%async_computation.1 | async-start | bytes 65536 | tf_op jit(solution)/shard_map/all_to_all | solution.py:600
  28.8 8.1 %collective-permute-start.5 = (f32[8,384]{1,0:T(8,128)S(1)}, f32[8,384]{1,0:T(8,128)S(1)}, u32[]{:S(2)}, u32[]{:S(2)}) collective-permute-start(f32[8,384]{1,0:T(8,128)S(1)} %get-tuple-element.68), channel_id=1, source_target_pairs={{0,28},{4,0},{8,4},{12,8},{16,12},{20,16},{24,20},{28,24},{1,29},{... | collective-permute-start | bytes 36872 | tf_op jit(solution)/shard_map/ppermute | solution.py:496
  36.9 1.3 %collective-permute-start.6 = (f32[8,1024]{1,0:T(8,128)S(1)}, f32[8,1024]{1,0:T(8,128)S(1)}, u32[]{:S(2)}, u32[]{:S(2)}) collective-permute-start(f32[8,1024]{1,0:T(8,128)S(1)} %get-tuple-element.69.refs_0_), channel_id=1, source_target_pairs={{0,1},{1,0},{2,3},{3,2},{4,5},{5,4},{6,7},{7,6},{8,9},{9,8},{10,11... | collective-permute-start | bytes 98312 | tf_op jit(solution)/shard_map/ppermute | solution.py:501
